TPU v7x, 128 devices: a whole 4x4x4 slice. The times are simulated.
128 devices in a mesh: tm: 4 (over x), state: 32 (over z, y, core).
Axes of the slice: x: 4, y: 4, z: 4, core: 2. Of those that a mesh axis runs over, the one named last changes fastest.
Arguments:
- transitions: bfloat16 [8, 1024, 1024], P('tm', 'state'), may hold values from -0.15 to 1.15
- gain: bfloat16 [1024, 128], P('state'), may hold values from -0.25 to 0.25
- obs_op: bfloat16 [128, 1024], P(None, 'state'), may hold values from -0.1875 to 0.1875
- observations: float32 [8, 128], P('tm'), may hold values from -6 to 6
- start: float32 [1024], P('state'), may hold values from -6 to 6
Outputs:
- means: float32 [8, 1024], P('tm', 'state')
- block_ends: float32 [4, 1024], P('tm', 'state')
All inputs are finite; a program needn't handle non-finite values.
Results may differ from a plain program's by a relative error of at most 0.0047.
Values may be sent and summed in bfloat16 or wider, within the bound.
No kernel may reach another device: no remote copies, remote signals or barrier semaphores. Data moves between devices by JAX's collectives and lax.ppermute only.
A program may use at most 64 MiB of HBM per device.

v0:
```python
import jax
import jax.numpy as jnp
from jax import lax
from jax.sharding import PartitionSpec as P


def from_behind(block, axis, distance):
    devices = range(lax.axis_size(axis))
    route = [(i - distance, i) for i in devices if i - distance in devices]
    return lax.ppermute(block, axis, route)


def accumulate(left, total, piece):
    columns = left.astype(jnp.float32)
    return total + jnp.dot(columns, piece, precision=lax.Precision.HIGHEST)


def apply_mat(matrix, vector):
    return jnp.dot(matrix.astype(jnp.float32), vector, precision=lax.Precision.HIGHEST)


def observed(partial_sums):
    return lax.psum(partial_sums, "state")


def correct(steps_in, gain, projected):
    corrected = jnp.einsum("ro,kon->krn", gain, projected, preferred_element_type=jnp.float32)
    return (steps_in.astype(jnp.float32) - corrected).astype(jnp.bfloat16)


def project(obs_op, steps_in):
    partial_sums = jnp.einsum("or,krn->kon", obs_op, steps_in, preferred_element_type=jnp.float32)
    return observed(partial_sums).astype(jnp.bfloat16)


def shards(transitions, gain, obs_op, observations, start):
    count = lax.axis_size("tm")
    here = lax.axis_index("tm")
    steps = transitions.shape[0]
    rows = transitions.shape[1]
    width = transitions.shape[2]
    high = lax.Precision.HIGHEST
    sources = jnp.einsum("ro,ko->kr", gain.astype(jnp.float32), observations, precision=high)
    models = correct(transitions, gain, project(obs_op, transitions))
    block_end = None
    zeros_mat = jnp.zeros((rows, width), jnp.float32)
    block_mat = models[0].astype(jnp.float32)
    block_vec = sources[0]
    inner = 1
    vec_full = lax.all_gather(block_vec, "state", axis=0, tiled=True)
    new_mat = accumulate(
        models[inner],
        zeros_mat,
        lax.all_gather(block_mat.astype(jnp.bfloat16), "state", axis=0, tiled=True).astype(
            jnp.float32
        ),
    )
    block_vec = apply_mat(models[inner], vec_full) + sources[inner]
    block_mat = new_mat
    span = 1
    while span < count:
        received_vec = from_behind(block_vec, "tm", span)
        received_full = lax.all_gather(received_vec, "state", axis=0, tiled=True)
        earlier_rows = from_behind(block_mat, "tm", span)
        new_mat = accumulate(
            block_mat, zeros_mat, lax.all_gather(earlier_rows, "state", axis=0, tiled=True)
        )
        new_vec = apply_mat(block_mat, received_full) + block_vec
        active = here >= span
        block_mat = jnp.where(active, new_mat, block_mat)
        block_vec = jnp.where(active, new_vec, block_vec)
        span = span * 2
    start_full = lax.all_gather(start, "state", axis=0, tiled=True)
    block_end = apply_mat(block_mat, start_full) + block_vec
    previous = from_behind(block_end, "tm", 1)
    current = jnp.where(here == 0, start, previous)
    results = []
    for inner in range(steps):
        current_full = lax.all_gather(current, "state", axis=0, tiled=True)
        current = apply_mat(models[inner], current_full) + sources[inner]
        results.append(current)
    return (jnp.stack(results, axis=0), block_end[None, :])


def solution(mesh):
    in_specs = (
        P("tm", "state", None),
        P("state", None),
        P(None, "state"),
        P("tm", None),
        P("state"),
    )
    out_specs = (P("tm", "state"), P("tm", "state"))
    return jax.shard_map(shards, mesh=mesh, in_specs=in_specs, out_specs=out_specs, check_vma=False)
```

profile of v0, /device:TPU:6, one launch (start us, length us, event | category | flops | bytes accessed | tf_op | source)
XLA Modules:
  0.0 550.2 jit_solution(9781777386397210487)
XLA Ops:
  7.2 0.0 copy-start
  7.2 0.0 all-gather.10.cloned.1.call-start
  7.2 0.6 copy-done
  7.9 1.2 convolution_bitcast_fusion
  9.1 1.2 dynamic-slice
  11.0 0.8 fusion.19
  11.8 0.1 bitcast_dynamic-update-slice_fusion
  11.9 141.5 %all-reduce.9 = (bf16[2,128,1024]{2,1,0:T(8,128)(2,1)S(1)}, f32[1024]{0:T(1024)S(1)}) all-reduce(f32[2,128,1024]{2,1,0:T(8,128)S(1)} %convolution_bitcast_fusion, f32[1024]{0:T(1024)S(1)} %bitcast_dynamic-update-slice_fusion), channel_id=1, replica_groups=mesh['tm'=4,'state'=32] {'state'}, use_global_device_ids=true, to_apply=%region_0.0 | all-reduce | flops 263168 | bytes 1581056 | tf_op jit(solution)/shard_map/psum | solution.py:23
  153.4 0.0 copy-start.4
  153.4 1.1 fusion.3
  154.6 0.6 slice.21
  155.2 0.0 all-gather.10.cloned.1.call-update
  155.2 0.0 all-gather.6.cloned.1.call-start
  155.3 40.3 %all-gather.10.cloned.1.call-done = bf16[1,1024,1024]{2,1,0:T(8,128)(2,1)} async-done(((bf16[1,32,1024]{2,1,0:T(8,128)(2,1)}), bf16[1,1024,1024]{2,1,0:T(8,128)(2,1)}) %all-gather.10.cloned.1.call-update) | async-done | bytes 2097168 | tf_op jit(solution)/shard_map/all_gather | solution.py:54
  195.6 2.1 fusion
  197.7 1.3 collective-permute-start
  199.0 6.3 %collective-permute-done = f32[32,1024]{1,0:T(8,128)S(1)} collective-permute-done((f32[32,1024]{1,0:T(8,128)S(1)}, f32[32,1024]{1,0:T(8,128)S(1)}, u32[]{:S(2)}, u32[]{:S(2)}) %collective-permute-start) | collective-permute-done | bytes 131104 | tf_op jit(solution)/shard_map/ppermute | solution.py:10
  205.2 0.0 copy-start.2
  205.2 0.6 copy-done.2
  205.9 0.0 all-gather.6.cloned.1.call-update
  205.9 0.0 all-gather.8.cloned.1.call-start
  205.9 45.8 %all-gather.6.cloned.1.call-done = f32[1024,1024]{1,0:T(8,128)} async-done(((f32[32,1024]{1,0:T(8,128)}), f32[1024,1024]{1,0:T(8,128)}) %all-gather.6.cloned.1.call-update) | async-done | bytes 4194320 | tf_op jit(solution)/shard_map/all_gather | solution.py:66
  251.7 4.7 convolution_select_fusion.1
  256.4 1.3 collective-permute-start.1
  257.7 7.8 %collective-permute-done.1 = f32[32,1024]{1,0:T(8,128)S(1)} collective-permute-done((f32[32,1024]{1,0:T(8,128)S(1)}, f32[32,1024]{1,0:T(8,128)S(1)}, u32[]{:S(2)}, u32[]{:S(2)}) %collective-permute-start.1) | collective-permute-done | bytes 131104 | tf_op jit(solution)/shard_map/ppermute | solution.py:10
  265.4 0.0 copy-start.1
  265.5 0.6 copy-done.1
  266.1 0.0 all-gather.8.cloned.1.call-update
  266.1 0.1 fusion.12
  266.3 1.3 collective-permute-start.2
  267.6 4.1 collective-permute-done.2
  271.7 0.2 dynamic-update-slice.2
  271.9 63.5 %all-reduce.2 = f32[1024]{0:T(1024)S(1)} all-reduce(f32[1024]{0:T(1024)S(1)} %dynamic-update-slice.2), channel_id=1, replica_groups=mesh['tm'=4,'state'=32] {'state'}, use_global_device_ids=true, to_apply=%add.2 | all-reduce | flops 1024 | bytes 8192
  335.4 0.2 fusion.11
  335.6 1.3 collective-permute-start.3
  337.0 0.0 copy-done.4
  337.0 0.2 dynamic-update-slice
  337.2 5.4 collective-permute-done.3
  342.6 0.2 dynamic-update-slice.3
  342.8 63.7 %all-reduce.6 = (f32[1024]{0:T(1024)S(1)}, f32[1024]{0:T(1024)S(1)}) all-reduce(f32[1024]{0:T(1024)S(1)} %dynamic-update-slice, f32[1024]{0:T(1024)S(1)} %dynamic-update-slice.3), channel_id=1, replica_groups=mesh['tm'=4,'state'=32] {'state'}, use_global_device_ids=true, to_apply=%add | all-reduce | flops 2048 | bytes 16384
  406.4 0.0 all-gather.8.cloned.1.call-done
  406.5 4.7 convolution_select_fusion
  411.2 0.2 convolution_bitcast_fusion.7
  411.3 0.2 fusion.9
  411.6 0.0 copy-start.3
  411.6 1.3 collective-permute-start.4
  412.9 4.1 collective-permute-done.4
  417.0 0.1 fusion.17
  417.1 62.7 %all-reduce.4 = f32[1024]{0:T(1024)S(1)} all-reduce(f32[1024]{0:T(1024)S(1)} %fusion.17), channel_id=1, replica_groups=mesh['tm'=4,'state'=32] {'state'}, use_global_device_ids=true, to_apply=%add.4 | all-reduce | flops 1024 | bytes 8192
  479.8 0.1 fusion.6
  480.0 0.2 dynamic-update-slice.5
  480.2 62.7 %all-reduce.5 = f32[1024]{0:T(1024)S(1)} all-reduce(f32[1024]{0:T(1024)S(1)} %dynamic-update-slice.5), channel_id=1, replica_groups=mesh['tm'=4,'state'=32] {'state'}, use_global_device_ids=true, to_apply=%add.5 | all-reduce | flops 1024 | bytes 8192
  542.9 0.1 fusion.5
  543.0 0.6 pad_maximum_fusion
  543.6 0.0 copy-done.3
  (6 shorter events, 0.0 us)
Async XLA Ops:
  7.2 0.7 copy-start
  7.2 188.4 %all-gather.10.cloned.1.call-start = ((), (), s32[]{:S(2)}) async-start(), calls=%async_computation.2 | async-start | bytes 2162688 | tf_op jit(solution)/shard_map/all_gather | solution.py:54
  153.4 183.5 %copy-start.4 = (f32[32]{0:T(128)S(1)}, f32[32]{0:T(128)}, u32[]{:S(2)}) copy-start(f32[32]{0:T(128)} %param.9) | copy-start | bytes 388
  155.2 96.5 %all-gather.6.cloned.1.call-start = ((), (), s32[]{:S(2)}) async-start(), calls=%async_computation | async-start | bytes 4325376 | tf_op jit(solution)/shard_map/all_gather | solution.py:66
  197.7 7.6 %collective-permute-start = (f32[32,1024]{1,0:T(8,128)S(1)}, f32[32,1024]{1,0:T(8,128)S(1)}, u32[]{:S(2)}, u32[]{:S(2)}) collective-permute-start(f32[32,1024]{1,0:T(8,128)S(1)} %fusion), channel_id=1, source_target_pairs={{0,32},{32,64},{64,96},{1,33},{33,65},{65,97},{2,34},{34,66},{66,9... | collective-permute-start | bytes 393224 | tf_op jit(solution)/shard_map/ppermute | solution.py:10
  205.2 0.6 copy-start.2
  205.9 200.6 %all-gather.8.cloned.1.call-start = ((), (), s32[]{:S(2)}) async-start(), calls=%async_computation.1 | async-start | bytes 4325376 | tf_op jit(solution)/shard_map/all_gather | solution.py:66
  256.4 9.1 %collective-permute-start.1 = (f32[32,1024]{1,0:T(8,128)S(1)}, f32[32,1024]{1,0:T(8,128)S(1)}, u32[]{:S(2)}, u32[]{:S(2)}) collective-permute-start(f32[32,1024]{1,0:T(8,128)S(1)} %convolution_select_fusion.1), channel_id=1, source_target_pairs={{0,64},{32,96},{1,65},{33,97},{2,66},{34,98},{3,67},{35,99},{4,68}... | collective-permute-start | bytes 393224 | tf_op jit(solution)/shard_map/ppermute | solution.py:10
  265.4 0.6 copy-start.1
  266.3 5.5 collective-permute-start.2
  335.6 7.0 %collective-permute-start.3 = (f32[32]{0:T(128)S(1)}, f32[32]{0:T(128)S(1)}, u32[]{:S(2)}, u32[]{:S(2)}) collective-permute-start(f32[32]{0:T(128)S(1)} %fusion.11), channel_id=1, source_target_pairs={{0,64},{32,96},{1,65},{33,97},{2,66},{34,98},{3,67},{35,99},{4,68}... | collective-permute-start | bytes 392 | tf_op jit(solution)/shard_map/ppermute | solution.py:10
  411.6 132.0 %copy-start.3 = (f32[32]{0:T(128)}, f32[32]{0:T(128)S(1)}, u32[]{:S(2)}) copy-start(f32[32]{0:T(128)S(1)} %fusion.9) | copy-start | bytes 388
  411.6 5.4 collective-permute-start.4
Sparse Core Ops, SparseCore 0:
  155.4 40.1 all-gather.9
  206.0 45.6 all-gather.5
  266.2 45.6 all-gather.7
where the time goes:
time: 551 us; the launch traced here: 550 us
  blocking collectives  394 us (72%)
  waiting for transfers between devices  114 us (21%)
  matrix products  15.7 us (3%)
  between operations  14.6 us (3%)
  starting transfers between devices  6.61 us (1%)
    unnamed x4, blocking collectives  253 us
    psum x1, blocking collectives, observed(): return lax.psum(partial_sums, 'state')  141 us
    all_gather x2, waiting for transfers between devices, shards(): lax.all_gather(earlier_rows, 'state', axis=0, tiled=True)  45.8 us
    all_gather x1, waiting for transfers between devices, shards(): lax.all_gather(block_mat.astype(jnp.bfloat16), 'state', axis=0, tiled=True)  40.3 us
    ppermute x5, waiting for transfers between devices, from_behind(): return lax.ppermute(block, axis, route)  27.6 us
    dot_general x3, matrix products, accumulate(): return total + jnp.dot(columns, piece, precision=lax.Precision.HIGHEST)  11.4 us
  transfers between devices with their start and end apart: 8, of which 7 were waited for; matrix products, arithmetic and copies ran while one was open for 0% of the time, Pallas kernels for 0%

commit v1 on v0

v1 whole, which is shorter than its diff:
```python
import jax
import jax.numpy as jnp
from jax import lax
from jax.experimental import pallas as pl
from jax.experimental.pallas import tpu as pltpu
from jax.sharding import PartitionSpec as P

F32 = jnp.float32
BF16 = jnp.bfloat16
RING = 4
BLOCKS = 4
MATMUL = (((1,), (0,)), ((), ()))
BY_ROWS = (((1,), (1,)), ((), ()))
BY_COLUMNS = (((0,), (0,)), ((), ()))


def dot(left, right, dims):
    return lax.dot_general(left, right, dims, preferred_element_type=F32)


def split(x):
    high = x.astype(BF16)
    rest = x - high.astype(F32)
    mid = rest.astype(BF16)
    low = (rest - mid.astype(F32)).astype(BF16)
    return high, mid, low


def stacked(x, rows):
    pieces = jnp.concatenate([piece.astype(F32) for piece in split(x)], axis=0)
    pad = jnp.zeros((rows - pieces.shape[0], x.shape[1]), F32)
    return jnp.concatenate([pieces, pad], axis=0).astype(BF16)


def step(model, x, source):
    parts = dot(stacked(x, 16), model, BY_ROWS)
    return parts[0:1] + parts[1:2] + parts[2:3] + source


def pack_kernel(trans_ref, gain_ref, obs_ref, start_ref, out_ref):
    rows, width = trans_ref.shape[1], trans_ref.shape[2]
    out_ref[:, 0:width] = trans_ref[0]
    out_ref[:, width : 2 * width] = trans_ref[1]
    out_ref[:, 2 * width : 2 * width + 128] = gain_ref[...]
    eye = (
        lax.broadcasted_iota(jnp.int32, (rows, rows), 0)
        == lax.broadcasted_iota(jnp.int32, (rows, rows), 1)
    ).astype(F32).astype(BF16)
    below = jnp.concatenate([obs_ref[...], stacked(start_ref[...], 128)], axis=0)
    out_ref[:, 2 * width + 128 :] = dot(eye, below, BY_ROWS).astype(BF16)


def pack(transitions, gain, obs_op, start):
    rows, width = transitions.shape[1], transitions.shape[2]
    return pl.pallas_call(
        pack_kernel,
        out_shape=jax.ShapeDtypeStruct((rows, 2 * width + 384), BF16),
        compiler_params=pltpu.CompilerParams(vmem_limit_bytes=4 << 20),
        name="pack",
    )(transitions, gain, obs_op, start[None, :])


def own_lanes(x, shift, rows):
    return pltpu.roll(x, shift, 1)[:, 0:rows]


def emit(shift, rows, u, v, end_ref, means_ref, last_ref):
    end_ref[...] = v
    mine = own_lanes(jnp.concatenate([u, v] + [u] * 6, axis=0), shift, rows)
    means_ref[...] = mine[0:2]
    last_ref[...] = mine[1:2]


def build_kernel(
    where_ref, obs_ref, *refs
):
    parts = refs[0:8]
    m0_ref, m1_ref, src_ref, end_ref, means_ref, last_ref = refs[8:14]
    gains, starts, seen = refs[14:17]
    width = m0_ref.shape[1]
    rows = means_ref.shape[1]
    g = 2 * width
    total = None
    for part in parts:
        term = dot(part[:, g + 128 : g + 256], part[:, 0:g], BY_COLUMNS)
        total = term if total is None else total + term
    seen[...] = total.astype(BF16)
    for index, part in enumerate(parts):
        gain = part[:, g : g + 128]
        for k, out in enumerate((m0_ref, m1_ref)):
            fix = dot(gain, seen[:, k * width : (k + 1) * width], MATMUL)
            model = (part[:, k * width : (k + 1) * width].astype(F32) - fix).astype(BF16)
            for j in range(RING):
                at = pl.multiple_of(where_ref[index * RING + j], rows)
                out[pl.ds(at, rows), :] = model[j * rows : (j + 1) * rows]
        for j in range(RING):
            at = pl.multiple_of(where_ref[index * RING + j], rows)
            gains[pl.ds(at, rows), :] = gain[j * rows : (j + 1) * rows]
            starts[pl.ds(at, rows), :] = part[j * rows : (j + 1) * rows, g + 256 : g + 384]
    first = dot(stacked(obs_ref[0:1, :], 16), gains[...], BY_ROWS)
    second = dot(stacked(obs_ref[1:2, :], 16), gains[...], BY_ROWS)
    s0 = first[0:1] + first[1:2] + first[2:3]
    s1 = second[0:1] + second[1:2] + second[2:3]
    src_ref[0:1, :] = s0
    src_ref[1:2, :] = s1
    pick = (
        lax.broadcasted_iota(jnp.int32, (16, 128), 0)
        == lax.broadcasted_iota(jnp.int32, (16, 128), 1)
    ).astype(F32).astype(BF16)
    begun = dot(pick, starts[...], BY_ROWS)
    x = begun[0:1] + begun[1:2] + begun[2:3]
    u = step(m0_ref[...], x, s0)
    v = step(m1_ref[...], u, s1)
    emit(where_ref[32], rows, u, v, end_ref, means_ref, last_ref)


def chain_shapes(rows, width):
    return (
        jax.ShapeDtypeStruct((1, width), F32),
        jax.ShapeDtypeStruct((2, rows), F32),
        jax.ShapeDtypeStruct((1, rows), F32),
    )


def build(where, observations, parts, rows, width):
    smem = pl.BlockSpec(memory_space=pltpu.SMEM)
    vmem = pl.BlockSpec(memory_space=pltpu.VMEM)
    return pl.pallas_call(
        build_kernel,
        in_specs=[smem] + [vmem] * 9,
        out_shape=(
            jax.ShapeDtypeStruct((width, width), BF16),
            jax.ShapeDtypeStruct((width, width), BF16),
            jax.ShapeDtypeStruct((2, width), F32),
        )
        + chain_shapes(rows, width),
        scratch_shapes=[
            pltpu.VMEM((width, 128), BF16),
            pltpu.VMEM((width, 128), BF16),
            pltpu.VMEM((128, 2 * width), BF16),
        ],
        compiler_params=pltpu.CompilerParams(vmem_limit_bytes=24 << 20),
        name="build",
    )(where, observations, *parts)


def advance_kernel(
    at_ref, m0_ref, m1_ref, src_ref, x_ref, end0, means0, last0, end_ref, means_ref, last_ref
):
    rows = means_ref.shape[1]

    @pl.when(at_ref[1] == 1)
    def _():
        u = step(m0_ref[...], x_ref[...], src_ref[0:1, :])
        v = step(m1_ref[...], u, src_ref[1:2, :])
        emit(at_ref[0], rows, u, v, end_ref, means_ref, last_ref)

    @pl.when(at_ref[1] == 0)
    def _():
        end_ref[...] = end0[...]
        means_ref[...] = means0[...]
        last_ref[...] = last0[...]


def advance(at, m0, m1, sources, x, before):
    smem = pl.BlockSpec(memory_space=pltpu.SMEM)
    vmem = pl.BlockSpec(memory_space=pltpu.VMEM)
    return pl.pallas_call(
        advance_kernel,
        in_specs=[smem] + [vmem] * 7,
        out_shape=chain_shapes(before[1].shape[1], m0.shape[1]),
        compiler_params=pltpu.CompilerParams(vmem_limit_bytes=8 << 20),
        name="advance",
    )(at, m0, m1, sources, x, *before)


def place(index):
    return index // (2 * RING), (index // 2) % RING, index % 2


def index_of(z, y, core):
    return ((z % RING) * RING + y % RING) * 2 + core


def along(first, distance):
    route = []
    for index in range(2 * RING * RING):
        z, y, core = place(index)
        if (core == 0) == first:
            route.append((index, index_of(z, y + distance, core)))
        else:
            route.append((index, index_of(z + distance, y, core)))
    return route


SWAP = [(index, index ^ 1) for index in range(2 * RING * RING)]


def shards(transitions, gain, obs_op, observations, start):
    here = lax.axis_index("tm")
    me = lax.axis_index("state")
    rows, width = transitions.shape[1], transitions.shape[2]
    z, y, core = place(me)

    offsets = []
    for side in (core, 1 - core):
        for far in range(RING):
            for near in range(RING):
                zz = jnp.where(side == 0, z - far, z - near)
                yy = jnp.where(side == 0, y - near, y - far)
                offsets.append(rows * index_of(zz, yy, side))
    shift = (width - rows * me) % width
    where = jnp.stack(offsets + [shift]).astype(jnp.int32)

    mine = pack(transitions, gain, obs_op, start)
    near = [mine] + [lax.ppermute(mine, "state", along(True, d)) for d in range(1, RING)]
    line = jnp.concatenate(near, axis=0)
    own = [line] + [lax.ppermute(line, "state", along(False, d)) for d in range(1, RING)]
    others = [lax.ppermute(part, "state", SWAP) for part in own]

    m0, m1, sources, *state = build(where, observations, own + others, rows, width)
    for block in range(1, BLOCKS):
        x = lax.ppermute(state[0], "tm", [(block - 1, block)])
        at = jnp.stack([shift, (here == block).astype(jnp.int32)]).astype(jnp.int32)
        state = advance(at, m0, m1, sources, x, state)
    return state[1], state[2]


def solution(mesh):
    in_specs = (
        P("tm", "state", None),
        P("state", None),
        P(None, "state"),
        P("tm", None),
        P("state"),
    )
    out_specs = (P("tm", "state"), P("tm", "state"))
    return jax.shard_map(shards, mesh=mesh, in_specs=in_specs, out_specs=out_specs, check_vma=False)
```

time: 551 us -> 69.4 us (0.13)
  blocking collectives: 394 us -> 0 us
  waiting for transfers between devices: 114 us -> 30.5 us
  matrix products: 15.7 us -> 0 us
  between operations: 14.6 us -> 1.69 us
  starting transfers between devices: 6.61 us -> 15.7 us
  Pallas kernels: 0 us -> 9.06 us
  local copies, waits for them, and re-layouts: 4.77 us -> 11.8 us
    unnamed x4 -> x0, blocking collectives: 253 us -> none
    psum x1 -> x0, blocking collectives: 141 us -> none  [observed(): return lax.psum(partial_sums, 'state')]
    all_gather x3 -> x0, waiting for transfers between devices: 86.1 us -> none  [the longest x2 45.8 us: shards(): lax.all_gather(earlier_rows, 'state', axis=0, tiled=True)]
    dot_general x12 -> x0, matrix products: 15.7 us -> none  [the longest x3 11.4 us: accumulate(): return total + jnp.dot(columns, piece, precision=lax.Precision.HIGHEST)]
    ppermute x5 -> x13, starting transfers between devices: 6.49 us -> 15.7 us  [the longest x3 6.58 us: shards(): lax.ppermute(line, 'state', along(False, d))]
    pallas_call x0 -> x5, Pallas kernels: none -> 9.06 us  [the longest x1 5.39 us: build(): pl.pallas_call(build_kernel, in_specs=[smem] + [vmem] * 9, out_shape=(jax...]
    unnamed x22 -> x29, local copies, waits for them, and re-layouts: 4.14 us -> 11.7 us
    ppermute x5 -> x13, waiting for transfers between devices: 27.6 us -> 30.5 us  [the longest x3 13.9 us: shards(): lax.ppermute(line, 'state', along(False, d))]
  transfers between devices with their start and end apart: 8 -> 13, of which waited for: 7 -> 7; matrix products, arithmetic and copies ran while one was open for 0% -> 1% of each run, Pallas kernels for 0% -> 0%
where the time goes in v1:
time: 69.4 us; the launch traced here: 68.9 us
  waiting for transfers between devices  30.5 us (44%)
  starting transfers between devices  15.7 us (23%)
  local copies, waits for them, and re-layouts  11.8 us (17%)
  Pallas kernels  9.06 us (13%)
  between operations  1.69 us (2%)
    ppermute x3, waiting for transfers between devices, shards(): lax.ppermute(line, 'state', along(False, d))  13.9 us
    ppermute x3, waiting for transfers between devices, shards(): x = lax.ppermute(state[0], 'tm', [(block - 1, block)])  12.1 us
    unnamed x29, local copies, waits for them, and re-layouts  11.7 us
    ppermute x3, starting transfers between devices, shards(): lax.ppermute(line, 'state', along(False, d))  6.58 us
    ppermute x3, starting transfers between devices, shards(): lax.ppermute(mine, 'state', along(True, d))  5.84 us
    pallas_call x1, Pallas kernels, build(): pl.pallas_call(build_kernel, in_specs=[smem] + [vmem] * 9, out_shape=(jax...  5.39 us
    ppermute x3, waiting for transfers between devices, shards(): lax.ppermute(mine, 'state', along(True, d))  3.88 us
    pallas_call x3, Pallas kernels, advance(): pl.pallas_call(advance_kernel, in_specs=[smem] + [vmem] * 7, out_shape=ch...  3.53 us
  transfers between devices with their start and end apart: 13, of which 7 were waited for; matrix products, arithmetic and copies ran while one was open for 1% of the time, Pallas kernels for 0%

profile of v1, /device:TPU:6, one launch (start us, length us, event | category | flops | bytes accessed | tf_op | source)
XLA Modules:
  0.0 68.9 jit_solution(11462202493525644097)
XLA Ops:
  0.6 0.8 %copy.7.obs_ref = bf16[128,32]{1,0:T(8,128)(2,1)S(1)} copy(bf16[128,32]{0,1:T(8,128)(2,1)} %param.7) | data formatting | bytes 16384 | tf_op args[2]
  1.4 0.0 copy-start.10
  1.4 0.9 %copy-done.10 = bf16[2,32,1024]{2,1,0:T(8,128)(2,1)S(1)} copy-done((bf16[2,32,1024]{2,1,0:T(8,128)(2,1)S(1)}, bf16[2,32,1024]{2,1,0:T(8,128)(2,1)}, u32[]{:S(2)}) %copy-start.10) | copy-done | bytes 131096
  2.4 0.0 copy-start.11
  2.4 0.7 %copy-done.11 = bf16[32,128]{1,0:T(8,128)(2,1)S(1)} copy-done((bf16[32,128]{1,0:T(8,128)(2,1)S(1)}, bf16[32,128]{1,0:T(8,128)(2,1)}, u32[]{:S(2)}) %copy-start.11) | copy-done | bytes 8216
  3.0 0.0 copy-start.13
  3.1 0.7 copy-done.13
  3.7 0.1 pack.1
  3.8 0.0 copy-start.12
  3.8 1.6 %collective-permute-start = (bf16[32,2432]{1,0:T(8,128)(2,1)S(1)}, bf16[32,2432]{1,0:T(8,128)(2,1)S(1)}, u32[]{:S(2)}, u32[]{:S(2)}) collective-permute-start(bf16[32,2432]{1,0:T(8,128)(2,1)S(1)} %pack.1), channel_id=1, source_target_pairs={{0,2},{1,9},{2,4},{3,11},{4,6},{5,13},{6,0},{7,15},{8,10},{9,17},{... | collective-permute-start | bytes 466952 | tf_op jit(solution)/shard_map/ppermute | solution.py:216
  5.4 2.9 %collective-permute-start.1 = (bf16[32,2432]{1,0:T(8,128)(2,1)S(1)}, bf16[32,2432]{1,0:T(8,128)(2,1)S(1)}, u32[]{:S(2)}, u32[]{:S(2)}) collective-permute-start(bf16[32,2432]{1,0:T(8,128)(2,1)S(1)} %pack.1), channel_id=1, source_target_pairs={{0,4},{1,17},{2,6},{3,19},{4,0},{5,21},{6,2},{7,23},{8,12},{9,25},... | collective-permute-start | bytes 466952 | tf_op jit(solution)/shard_map/ppermute | solution.py:216
  8.3 1.3 %collective-permute-start.2 = (bf16[32,2432]{1,0:T(8,128)(2,1)S(1)}, bf16[32,2432]{1,0:T(8,128)(2,1)S(1)}, u32[]{:S(2)}, u32[]{:S(2)}) collective-permute-start(bf16[32,2432]{1,0:T(8,128)(2,1)S(1)} %pack.1), channel_id=1, source_target_pairs={{0,6},{1,25},{2,0},{3,27},{4,2},{5,29},{6,4},{7,31},{8,14},{9,1},{... | collective-permute-start | bytes 466952 | tf_op jit(solution)/shard_map/ppermute | solution.py:216
  9.7 0.6 collective-permute-done
  10.3 2.9 %collective-permute-done.1 = bf16[32,2432]{1,0:T(8,128)(2,1)S(1)} collective-permute-done((bf16[32,2432]{1,0:T(8,128)(2,1)S(1)}, bf16[32,2432]{1,0:T(8,128)(2,1)S(1)}, u32[]{:S(2)}, u32[]{:S(2)}) %collective-permute-start.1) | collective-permute-done | bytes 155680 | tf_op jit(solution)/shard_map/ppermute | solution.py:216
  13.2 0.4 collective-permute-done.2
  13.6 2.0 %collective-permute-start.3 = (bf16[128,2432]{1,0:T(8,128)(2,1)S(1)}, bf16[128,2432]{1,0:T(8,128)(2,1)S(1)}, u32[]{:S(2)}, u32[]{:S(2)}) collective-permute-start(bf16[128,2432]{1,0:T(8,128)(2,1)S(1)} %pad_maximum_fusion.refs_0_), channel_id=1, source_target_pairs={{0,8},{1,3},{2,10},{3,5},{4,12},{5,7},{6,14},{7,1},{8,16},{9,11},{... | collective-permute-start | bytes 1867784 | tf_op jit(solution)/shard_map/ppermute | solution.py:218
  15.6 3.6 %collective-permute-start.4 = (bf16[128,2432]{1,0:T(8,128)(2,1)S(1)}, bf16[128,2432]{1,0:T(8,128)(2,1)S(1)}, u32[]{:S(2)}, u32[]{:S(2)}) collective-permute-start(bf16[128,2432]{1,0:T(8,128)(2,1)S(1)} %pad_maximum_fusion.refs_0_), channel_id=1, source_target_pairs={{0,16},{1,5},{2,18},{3,7},{4,20},{5,1},{6,22},{7,3},{8,24},{9,13},... | collective-permute-start | bytes 1867784 | tf_op jit(solution)/shard_map/ppermute | solution.py:218
  19.2 1.0 %collective-permute-start.5 = (bf16[128,2432]{1,0:T(8,128)(2,1)S(1)}, bf16[128,2432]{1,0:T(8,128)(2,1)S(1)}, u32[]{:S(2)}, u32[]{:S(2)}) collective-permute-start(bf16[128,2432]{1,0:T(8,128)(2,1)S(1)} %pad_maximum_fusion.refs_0_), channel_id=1, source_target_pairs={{0,24},{1,7},{2,26},{3,1},{4,28},{5,3},{6,30},{7,5},{8,0},{9,15},{... | collective-permute-start | bytes 1867784 | tf_op jit(solution)/shard_map/ppermute | solution.py:218
  20.2 0.0 collective-permute-start.6
  20.2 5.7 %collective-permute-done.3.refs_1_ = bf16[128,2432]{1,0:T(8,128)(2,1)S(1)} collective-permute-done((bf16[128,2432]{1,0:T(8,128)(2,1)S(1)}, bf16[128,2432]{1,0:T(8,128)(2,1)S(1)}, u32[]{:S(2)}, u32[]{:S(2)}) %collective-permute-start.3) | collective-permute-done | bytes 622624 | tf_op jit(solution)/shard_map/ppermute | solution.py:218
  25.9 0.0 collective-permute-start.7
  25.9 8.1 %collective-permute-done.4.refs_2_ = bf16[128,2432]{1,0:T(8,128)(2,1)S(1)} collective-permute-done((bf16[128,2432]{1,0:T(8,128)(2,1)S(1)}, bf16[128,2432]{1,0:T(8,128)(2,1)S(1)}, u32[]{:S(2)}, u32[]{:S(2)}) %collective-permute-start.4) | collective-permute-done | bytes 622624 | tf_op jit(solution)/shard_map/ppermute | solution.py:218
  34.1 0.0 copy-start.4
  34.1 0.0 collective-permute-start.8
  34.1 0.0 collective-permute-done.5.refs_3_
  34.1 0.0 copy-start.6
  34.1 0.5 collective-permute-start.9
  35.5 0.1 stack.168.where_ref
  35.6 0.0 collective-permute-done.6.refs_4_
  35.7 0.0 copy-start.8
  35.7 0.8 %copy-done.8 = bf16[128,2432]{1,0:T(8,128)(2,1)} copy-done((bf16[128,2432]{1,0:T(8,128)(2,1)}, bf16[128,2432]{1,0:T(8,128)(2,1)S(1)}, u32[]{:S(2)}) %copy-start.8) | copy-done | bytes 622616
  36.5 0.0 collective-permute-done.7.refs_5_
  36.5 0.0 collective-permute-done.8.refs_6_
  36.5 0.0 copy-done.4
  36.5 0.0 copy-done.6
  36.5 0.6 collective-permute-done.9.refs_7_
  37.1 0.0 copy-done.12
  37.1 0.0 copy-start.5
  37.1 1.1 %copy-done.5 = bf16[128,2432]{1,0:T(8,128)(2,1)S(1)} copy-done((bf16[128,2432]{1,0:T(8,128)(2,1)S(1)}, bf16[128,2432]{1,0:T(8,128)(2,1)}, u32[]{:S(2)}) %copy-start.5) | copy-done | bytes 622616
  38.2 0.0 copy-start.7
  38.2 1.1 %copy-done.7 = bf16[128,2432]{1,0:T(8,128)(2,1)S(1)} copy-done((bf16[128,2432]{1,0:T(8,128)(2,1)S(1)}, bf16[128,2432]{1,0:T(8,128)(2,1)}, u32[]{:S(2)}) %copy-start.7) | copy-done | bytes 622616
  39.3 0.0 copy-start.9
  39.3 1.1 %copy-done.9 = bf16[128,2432]{1,0:T(8,128)(2,1)S(1)} copy-done((bf16[128,2432]{1,0:T(8,128)(2,1)S(1)}, bf16[128,2432]{1,0:T(8,128)(2,1)}, u32[]{:S(2)}) %copy-start.9) | copy-done | bytes 622616
  40.4 5.4 %build.1 = (bf16[1024,1024]{1,0:T(8,128)(2,1)S(1)}, bf16[1024,1024]{1,0:T(8,128)(2,1)S(1)}, f32[2,1024]{1,0:T(2,128)S(1)}, f32[1,1024]{1,0:T(1,128)S(1)}, f32[2,32]{1,0:T(2,128)S(1)}, /*index=5*/f32[1,32]{1,0:T(1,128)S(1)}) custom-call(s32[33]{0:T(128)S(1)} %stack.168.where_ref, f32[2,128]{1,0:T(2,128)S(1)} %copy-done.12, ...), custom_call_target="tpu_custom_call" | custom-call | tf_op jit(solution)/shard_map/build/pallas_call | solution.py:128
  45.8 0.0 copy-start
  45.8 1.3 %copy-done = bf16[1024,1024]{1,0:T(8,128)(2,1)} copy-done((bf16[1024,1024]{1,0:T(8,128)(2,1)}, bf16[1024,1024]{1,0:T(8,128)(2,1)S(1)}, u32[]{:S(2)}) %copy-start) | copy-done | bytes 2097176
  47.1 0.6 collective-permute-start.10
  47.8 0.1 pad_add_fusion.2.at_ref
  47.9 0.0 collective-permute-done.10.x_ref
  47.9 0.0 copy-start.1
  47.9 1.6 %copy-done.1 = bf16[1024,1024]{1,0:T(8,128)(2,1)S(1)} copy-done((bf16[1024,1024]{1,0:T(8,128)(2,1)S(1)}, bf16[1024,1024]{1,0:T(8,128)(2,1)}, u32[]{:S(2)}) %copy-start.1) | copy-done | bytes 2097176
  49.5 0.6 advance.3
  50.0 0.7 collective-permute-start.11
  50.7 0.1 pad_add_fusion.1.at_ref
  50.8 0.0 collective-permute-done.11.x_ref
  50.8 0.0 copy-start.2
  50.8 1.6 %copy-done.2 = bf16[1024,1024]{1,0:T(8,128)(2,1)S(1)} copy-done((bf16[1024,1024]{1,0:T(8,128)(2,1)S(1)}, bf16[1024,1024]{1,0:T(8,128)(2,1)}, u32[]{:S(2)}) %copy-start.2) | copy-done | bytes 2097176
  52.4 0.0 copy-start.3
  52.4 0.6 advance.4
  52.9 1.4 %collective-permute-start.12 = (f32[1,1024]{1,0:T(1,128)S(1)}, f32[1,1024]{1,0:T(1,128)S(1)}, u32[]{:S(2)}, u32[]{:S(2)}) collective-permute-start(f32[1,1024]{1,0:T(1,128)S(1)} %get-tuple-element.25.end0), channel_id=1, source_target_pairs={{64,96},{65,97},{66,98},{67,99},{68,100},{69,101},{70,102},{71,103... | collective-permute-start | bytes 12296 | tf_op jit(solution)/shard_map/ppermute | solution.py:223
  54.4 0.1 pad_add_fusion.at_ref
  54.4 12.1 %collective-permute-done.12.x_ref = f32[1,1024]{1,0:T(1,128)S(1)} collective-permute-done((f32[1,1024]{1,0:T(1,128)S(1)}, f32[1,1024]{1,0:T(1,128)S(1)}, u32[]{:S(2)}, u32[]{:S(2)}) %collective-permute-start.12) | collective-permute-done | bytes 4128 | tf_op jit(solution)/shard_map/ppermute | solution.py:223
  66.5 0.0 copy-done.3
  66.5 2.4 %advance.5 = (f32[1,1024]{1,0:T(1,128)}, f32[2,32]{1,0:T(2,128)}, f32[1,32]{1,0:T(1,128)}) custom-call(s32[2]{0:T(128)S(1)} %pad_add_fusion.at_ref, bf16[1024,1024]{1,0:T(8,128)(2,1)S(1)} %get-tuple-element.16.m0_ref, bf16[1024,1024]{1,0:T(8,128)(2,1)S(1)} %copy-done.3, f32[2,1024]{1,0:T(2,128)S(1)} %get-tuple-element.18.src_ref, ...), custom_call_target="tpu_custom_call" | custom-call | tf_op jit(solution)/shard_map/advance/pallas_call | solution.py:168
  (1 shorter events, 0.0 us)
Async XLA Ops:
  1.4 0.9 %copy-start.10 = (bf16[2,32,1024]{2,1,0:T(8,128)(2,1)S(1)}, bf16[2,32,1024]{2,1,0:T(8,128)(2,1)}, u32[]{:S(2)}) copy-start(bf16[2,32,1024]{2,1,0:T(8,128)(2,1)} %trans_ref.1) | copy-start | bytes 393220
  2.4 0.7 %copy-start.11 = (bf16[32,128]{1,0:T(8,128)(2,1)S(1)}, bf16[32,128]{1,0:T(8,128)(2,1)}, u32[]{:S(2)}) copy-start(bf16[32,128]{1,0:T(8,128)(2,1)} %gain_ref.1) | copy-start | bytes 24580
  3.0 0.7 copy-start.13
  3.8 33.3 %copy-start.12 = (f32[2,128]{1,0:T(2,128)S(1)}, f32[2,128]{1,0:T(2,128)}, u32[]{:S(2)}) copy-start(f32[2,128]{1,0:T(2,128)} %obs_ref.2) | copy-start | bytes 3076
  3.8 6.5 %collective-permute-start = (bf16[32,2432]{1,0:T(8,128)(2,1)S(1)}, bf16[32,2432]{1,0:T(8,128)(2,1)S(1)}, u32[]{:S(2)}, u32[]{:S(2)}) collective-permute-start(bf16[32,2432]{1,0:T(8,128)(2,1)S(1)} %pack.1), channel_id=1, source_target_pairs={{0,2},{1,9},{2,4},{3,11},{4,6},{5,13},{6,0},{7,15},{8,10},{9,17},{... | collective-permute-start | bytes 466952 | tf_op jit(solution)/shard_map/ppermute | solution.py:216
  5.4 7.8 %collective-permute-start.1 = (bf16[32,2432]{1,0:T(8,128)(2,1)S(1)}, bf16[32,2432]{1,0:T(8,128)(2,1)S(1)}, u32[]{:S(2)}, u32[]{:S(2)}) collective-permute-start(bf16[32,2432]{1,0:T(8,128)(2,1)S(1)} %pack.1), channel_id=1, source_target_pairs={{0,4},{1,17},{2,6},{3,19},{4,0},{5,21},{6,2},{7,23},{8,12},{9,25},... | collective-permute-start | bytes 466952 | tf_op jit(solution)/shard_map/ppermute | solution.py:216
  8.3 5.2 %collective-permute-start.2 = (bf16[32,2432]{1,0:T(8,128)(2,1)S(1)}, bf16[32,2432]{1,0:T(8,128)(2,1)S(1)}, u32[]{:S(2)}, u32[]{:S(2)}) collective-permute-start(bf16[32,2432]{1,0:T(8,128)(2,1)S(1)} %pack.1), channel_id=1, source_target_pairs={{0,6},{1,25},{2,0},{3,27},{4,2},{5,29},{6,4},{7,31},{8,14},{9,1},{... | collective-permute-start | bytes 466952 | tf_op jit(solution)/shard_map/ppermute | solution.py:216
  13.6 12.3 %collective-permute-start.3 = (bf16[128,2432]{1,0:T(8,128)(2,1)S(1)}, bf16[128,2432]{1,0:T(8,128)(2,1)S(1)}, u32[]{:S(2)}, u32[]{:S(2)}) collective-permute-start(bf16[128,2432]{1,0:T(8,128)(2,1)S(1)} %pad_maximum_fusion.refs_0_), channel_id=1, source_target_pairs={{0,8},{1,3},{2,10},{3,5},{4,12},{5,7},{6,14},{7,1},{8,16},{9,11},{... | collective-permute-start | bytes 1867784 | tf_op jit(solution)/shard_map/ppermute | solution.py:218
  15.6 18.5 %collective-permute-start.4 = (bf16[128,2432]{1,0:T(8,128)(2,1)S(1)}, bf16[128,2432]{1,0:T(8,128)(2,1)S(1)}, u32[]{:S(2)}, u32[]{:S(2)}) collective-permute-start(bf16[128,2432]{1,0:T(8,128)(2,1)S(1)} %pad_maximum_fusion.refs_0_), channel_id=1, source_target_pairs={{0,16},{1,5},{2,18},{3,7},{4,20},{5,1},{6,22},{7,3},{8,24},{9,13},... | collective-permute-start | bytes 1867784 | tf_op jit(solution)/shard_map/ppermute | solution.py:218
  19.2 14.9 %collective-permute-start.5 = (bf16[128,2432]{1,0:T(8,128)(2,1)S(1)}, bf16[128,2432]{1,0:T(8,128)(2,1)S(1)}, u32[]{:S(2)}, u32[]{:S(2)}) collective-permute-start(bf16[128,2432]{1,0:T(8,128)(2,1)S(1)} %pad_maximum_fusion.refs_0_), channel_id=1, source_target_pairs={{0,24},{1,7},{2,26},{3,1},{4,28},{5,3},{6,30},{7,5},{8,0},{9,15},{... | collective-permute-start | bytes 1867784 | tf_op jit(solution)/shard_map/ppermute | solution.py:218
  20.2 15.4 %collective-permute-start.6 = (bf16[128,2432]{1,0:T(8,128)(2,1)S(1)}, bf16[128,2432]{1,0:T(8,128)(2,1)S(1)}, u32[]{:S(2)}, u32[]{:S(2)}) collective-permute-start(bf16[128,2432]{1,0:T(8,128)(2,1)S(1)} %pad_maximum_fusion.refs_0_), channel_id=1, source_target_pairs={{0,1},{1,0},{2,3},{3,2},{4,5},{5,4},{6,7},{7,6},{8,9},{9,8},{10,11... | collective-permute-start | bytes 1867784 | tf_op jit(solution)/shard_map/ppermute | solution.py:219
  25.9 10.5 %collective-permute-start.7 = (bf16[128,2432]{1,0:T(8,128)(2,1)S(1)}, bf16[128,2432]{1,0:T(8,128)(2,1)}, u32[]{:S(2)}, u32[]{:S(2)}) collective-permute-start(bf16[128,2432]{1,0:T(8,128)(2,1)S(1)} %collective-permute-done.3.refs_1_), channel_id=1, source_target_pairs={{0,1},{1,0},{2,3},{3,2},{4,5},{5,4},{6,7},{7,6},{8,9},{9,8},{10,11... | collective-permute-start | bytes 1867784 | tf_op jit(solution)/shard_map/ppermute | solution.py:219
  34.1 2.4 %copy-start.4 = (bf16[128,2432]{1,0:T(8,128)(2,1)}, bf16[128,2432]{1,0:T(8,128)(2,1)S(1)}, u32[]{:S(2)}) copy-start(bf16[128,2432]{1,0:T(8,128)(2,1)S(1)} %collective-permute-done.4.refs_2_) | copy-start | bytes 1867780
  34.1 2.4 %collective-permute-start.8 = (bf16[128,2432]{1,0:T(8,128)(2,1)S(1)}, bf16[128,2432]{1,0:T(8,128)(2,1)}, u32[]{:S(2)}, u32[]{:S(2)}) collective-permute-start(bf16[128,2432]{1,0:T(8,128)(2,1)S(1)} %collective-permute-done.4.refs_2_), channel_id=1, source_target_pairs={{0,1},{1,0},{2,3},{3,2},{4,5},{5,4},{6,7},{7,6},{8,9},{9,8},{10,11... | collective-permute-start | bytes 1867784 | tf_op jit(solution)/shard_map/ppermute | solution.py:219
  34.1 2.4 %copy-start.6 = (bf16[128,2432]{1,0:T(8,128)(2,1)}, bf16[128,2432]{1,0:T(8,128)(2,1)S(1)}, u32[]{:S(2)}) copy-start(bf16[128,2432]{1,0:T(8,128)(2,1)S(1)} %collective-permute-done.5.refs_3_) | copy-start | bytes 1867780
  34.1 3.1 %collective-permute-start.9 = (bf16[128,2432]{1,0:T(8,128)(2,1)S(1)}, bf16[128,2432]{1,0:T(8,128)(2,1)}, u32[]{:S(2)}, u32[]{:S(2)}) collective-permute-start(bf16[128,2432]{1,0:T(8,128)(2,1)S(1)} %collective-permute-done.5.refs_3_), channel_id=1, source_target_pairs={{0,1},{1,0},{2,3},{3,2},{4,5},{5,4},{6,7},{7,6},{8,9},{9,8},{10,11... | collective-permute-start | bytes 1867784 | tf_op jit(solution)/shard_map/ppermute | solution.py:219
  35.7 0.8 %copy-start.8 = (bf16[128,2432]{1,0:T(8,128)(2,1)}, bf16[128,2432]{1,0:T(8,128)(2,1)S(1)}, u32[]{:S(2)}) copy-start(bf16[128,2432]{1,0:T(8,128)(2,1)S(1)} %collective-permute-done.6.refs_4_) | copy-start | bytes 1867780
  37.1 1.1 %copy-start.5 = (bf16[128,2432]{1,0:T(8,128)(2,1)S(1)}, bf16[128,2432]{1,0:T(8,128)(2,1)}, u32[]{:S(2)}) copy-start(bf16[128,2432]{1,0:T(8,128)(2,1)} %copy-done.4) | copy-start | bytes 1867780
  38.2 1.1 %copy-start.7 = (bf16[128,2432]{1,0:T(8,128)(2,1)S(1)}, bf16[128,2432]{1,0:T(8,128)(2,1)}, u32[]{:S(2)}) copy-start(bf16[128,2432]{1,0:T(8,128)(2,1)} %copy-done.6) | copy-start | bytes 1867780
  39.3 1.1 %copy-start.9 = (bf16[128,2432]{1,0:T(8,128)(2,1)S(1)}, bf16[128,2432]{1,0:T(8,128)(2,1)}, u32[]{:S(2)}) copy-start(bf16[128,2432]{1,0:T(8,128)(2,1)} %copy-done.8) | copy-start | bytes 1867780
  45.8 1.4 %copy-start = (bf16[1024,1024]{1,0:T(8,128)(2,1)}, bf16[1024,1024]{1,0:T(8,128)(2,1)S(1)}, u32[]{:S(2)}) copy-start(bf16[1024,1024]{1,0:T(8,128)(2,1)S(1)} %get-tuple-element.17.m1_ref) | copy-start | bytes 6291460
  47.1 0.7 %collective-permute-start.10 = (f32[1,1024]{1,0:T(1,128)S(1)}, f32[1,1024]{1,0:T(1,128)S(1)}, u32[]{:S(2)}, u32[]{:S(2)}) collective-permute-start(f32[1,1024]{1,0:T(1,128)S(1)} %get-tuple-element.19.end0), channel_id=1, source_target_pairs={{0,32},{1,33},{2,34},{3,35},{4,36},{5,37},{6,38},{7,39},{8,40},{9,... | collective-permute-start | bytes 12296 | tf_op jit(solution)/shard_map/ppermute | solution.py:223
  47.9 1.6 %copy-start.1 = (bf16[1024,1024]{1,0:T(8,128)(2,1)S(1)}, bf16[1024,1024]{1,0:T(8,128)(2,1)}, u32[]{:S(2)}) copy-start(bf16[1024,1024]{1,0:T(8,128)(2,1)} %copy-done) | copy-start | bytes 6291460
  50.0 0.8 %collective-permute-start.11 = (f32[1,1024]{1,0:T(1,128)S(1)}, f32[1,1024]{1,0:T(1,128)S(1)}, u32[]{:S(2)}, u32[]{:S(2)}) collective-permute-start(f32[1,1024]{1,0:T(1,128)S(1)} %get-tuple-element.22.end0), channel_id=1, source_target_pairs={{32,64},{33,65},{34,66},{35,67},{36,68},{37,69},{38,70},{39,71},{4... | collective-permute-start | bytes 12296 | tf_op jit(solution)/shard_map/ppermute | solution.py:223
  50.8 1.6 %copy-start.2 = (bf16[1024,1024]{1,0:T(8,128)(2,1)S(1)}, bf16[1024,1024]{1,0:T(8,128)(2,1)}, u32[]{:S(2)}) copy-start(bf16[1024,1024]{1,0:T(8,128)(2,1)} %copy-done) | copy-start | bytes 6291460
  52.4 14.2 %copy-start.3 = (bf16[1024,1024]{1,0:T(8,128)(2,1)S(1)}, bf16[1024,1024]{1,0:T(8,128)(2,1)}, u32[]{:S(2)}) copy-start(bf16[1024,1024]{1,0:T(8,128)(2,1)} %copy-done) | copy-start | bytes 6291460
  52.9 13.6 %collective-permute-start.12 = (f32[1,1024]{1,0:T(1,128)S(1)}, f32[1,1024]{1,0:T(1,128)S(1)}, u32[]{:S(2)}, u32[]{:S(2)}) collective-permute-start(f32[1,1024]{1,0:T(1,128)S(1)} %get-tuple-element.25.end0), channel_id=1, source_target_pairs={{64,96},{65,97},{66,98},{67,99},{68,100},{69,101},{70,102},{71,103... | collective-permute-start | bytes 12296 | tf_op jit(solution)/shard_map/ppermute | solution.py:223

commit v2 on v1

v2 whole, which is shorter than its diff:
```python
import functools

import jax
import jax.numpy as jnp
from jax import lax
from jax.experimental import pallas as pl
from jax.experimental.pallas import tpu as pltpu
from jax.sharding import PartitionSpec as P

F32 = jnp.float32
BF16 = jnp.bfloat16
RING = 4
BLOCKS = 4
MATMUL = (((1,), (0,)), ((), ()))
BY_ROWS = (((1,), (1,)), ((), ()))
BY_COLUMNS = (((0,), (0,)), ((), ()))


def dot(left, right, dims):
    return lax.dot_general(left, right, dims, preferred_element_type=F32)


def split(x):
    high = x.astype(BF16)
    rest = x - high.astype(F32)
    mid = rest.astype(BF16)
    low = (rest - mid.astype(F32)).astype(BF16)
    return high, mid, low


def stacked(x, rows):
    pieces = jnp.concatenate([piece.astype(F32) for piece in split(x)], axis=0)
    pad = jnp.zeros((rows - pieces.shape[0], x.shape[1]), F32)
    return jnp.concatenate([pieces, pad], axis=0).astype(BF16)


def step(model, x, source):
    parts = dot(stacked(x, 16), model, BY_ROWS)
    return parts[0:1] + parts[1:2] + parts[2:3] + source


def pack_kernel(trans_ref, gain_ref, obs_ref, start_ref, out_ref, held, sems):
    rows, width = trans_ref.shape[1], trans_ref.shape[2]
    g = 2 * width
    copies = [
        pltpu.make_async_copy(start_ref, held, sems.at[0]),
        pltpu.make_async_copy(trans_ref.at[0], out_ref.at[:, 0:width], sems.at[1]),
        pltpu.make_async_copy(trans_ref.at[1], out_ref.at[:, width:g], sems.at[2]),
        pltpu.make_async_copy(obs_ref, out_ref.at[:, g : g + 128], sems.at[3]),
        pltpu.make_async_copy(gain_ref, out_ref.at[:, g + 128 : g + 256], sems.at[4]),
    ]
    for copy in copies:
        copy.start()
    eye = (
        lax.broadcasted_iota(jnp.int32, (rows, rows), 0)
        == lax.broadcasted_iota(jnp.int32, (rows, rows), 1)
    ).astype(F32).astype(BF16)
    copies[0].wait()
    out_ref[:, g + 256 :] = dot(eye, stacked(held[...], 128), BY_ROWS).astype(BF16)
    for copy in copies[1:]:
        copy.wait()


def pack(transitions, gain, obs_op, start):
    rows, width = transitions.shape[1], transitions.shape[2]
    return pl.pallas_call(
        pack_kernel,
        in_specs=[pl.BlockSpec(memory_space=pltpu.HBM)] * 4,
        out_shape=jax.ShapeDtypeStruct((rows, 2 * width + 384), BF16),
        scratch_shapes=[pltpu.VMEM((1, rows), F32), pltpu.SemaphoreType.DMA((5,))],
        compiler_params=pltpu.CompilerParams(vmem_limit_bytes=4 << 20),
        name="pack",
    )(*(pltpu.with_memory_space_constraint(x, pltpu.HBM) for x in (transitions, gain, obs_op.T, start[None, :])))


def own_lanes(x, shift, rows):
    return pltpu.roll(x, shift, 1)[:, 0:rows]


def emit(shift, rows, u, v, end_ref, means_ref, last_ref):
    end_ref[...] = v
    mine = own_lanes(jnp.concatenate([u, v] + [u] * 6, axis=0), shift, rows)
    means_ref[...] = mine[0:2]
    last_ref[...] = mine[1:2]


def place(index):
    return index // (2 * RING), (index // 2) % RING, index % 2


def index_of(z, y, core):
    return ((z % RING) * RING + y % RING) * 2 + core


EARLY, LATE = (0, 1, RING - 1), (2,)


def row_offsets(rows, fars):
    z, y, core = place(lax.axis_index("state"))
    z, y = z + RING, y + RING
    offsets = []
    for side in (core, 1 - core):
        for far in fars:
            for near in range(RING):
                dz = far + side * (near - far)
                dy = near + side * (far - near)
                offsets.append(rows * index_of(z - dz, y - dy, side))
    return offsets


def put_rows(parts, fars, out_ref):
    rows = parts[0].shape[0] // RING
    where = row_offsets(rows, fars)
    for index, part in enumerate(parts):
        for j in range(RING):
            at = pl.multiple_of(where[index * RING + j], rows)
            out_ref[pl.ds(at, rows), :] = part[j * rows : (j + 1) * rows, :]


def lanes_shift(rows, width):
    return lax.rem(width - rows * lax.axis_index("state"), width)


def early_kernel(*refs):
    put_rows(refs[:-1], EARLY, refs[-1])


def early(parts, width):
    vmem = pl.BlockSpec(memory_space=pltpu.VMEM)
    return pl.pallas_call(
        early_kernel,
        in_specs=[vmem] * len(parts),
        out_shape=jax.ShapeDtypeStruct((width, parts[0].shape[1]), BF16),
        compiler_params=pltpu.CompilerParams(vmem_limit_bytes=4 << 20),
        name="early",
    )(*parts)


def total(parts):
    return parts[0:1] + parts[1:2] + parts[2:3]


def late_kernel(obs_ref, part0, part1, held_ref, all_ref, src_ref, end_ref, means_ref, last_ref, seen):
    del held_ref
    width = all_ref.shape[0]
    rows = means_ref.shape[1]
    g = 2 * width
    put_rows((part0, part1), LATE, all_ref)
    is_first = lax.axis_index("tm") == 0

    @pl.when(is_first)
    def _():
        pick = (
            lax.broadcasted_iota(jnp.int32, (16, 128), 0)
            == lax.broadcasted_iota(jnp.int32, (16, 128), 1)
        ).astype(F32).astype(BF16)
        x = total(dot(pick, all_ref[:, g + 256 : g + 384], BY_ROWS))
        states = []
        for k in range(2):
            y = total(dot(stacked(x, 16), all_ref[:, k * width : (k + 1) * width], BY_ROWS))
            seen_y = total(dot(stacked(y, 16), all_ref[:, g : g + 128], MATMUL))
            missed = stacked(obs_ref[k : k + 1, :] - seen_y, 16)
            x = y + total(dot(missed, all_ref[:, g + 128 : g + 256], BY_ROWS))
            states.append(x)
        src_ref[...] = jnp.zeros_like(src_ref)
        emit(lanes_shift(rows, width), rows, *states, end_ref, means_ref, last_ref)

    @pl.when(jnp.logical_not(is_first))
    def _():
        for k in range(2):
            source = dot(stacked(obs_ref[k : k + 1, :], 16), all_ref[:, g + 128 : g + 256], BY_ROWS)
            src_ref[k : k + 1, :] = total(source)
        seen[...] = dot(all_ref[:, g : g + 128], all_ref[:, 0:g], BY_COLUMNS).astype(BF16)
        for at in range(0, width, 128):
            fix = dot(all_ref[at : at + 128, g + 128 : g + 256], seen[...], MATMUL)
            model = all_ref[at : at + 128, 0:g].astype(F32) - fix
            all_ref[at : at + 128, 0:g] = model.astype(BF16)
        end_ref[...] = jnp.zeros_like(end_ref)
        means_ref[...] = jnp.zeros_like(means_ref)
        last_ref[...] = jnp.zeros_like(last_ref)


def chain_shapes(rows, width):
    return (
        jax.ShapeDtypeStruct((1, width), F32),
        jax.ShapeDtypeStruct((2, rows), F32),
        jax.ShapeDtypeStruct((1, rows), F32),
    )


def late(observations, parts, held, rows):
    vmem = pl.BlockSpec(memory_space=pltpu.VMEM)
    width, lanes = held.shape
    return pl.pallas_call(
        late_kernel,
        in_specs=[vmem] * 4,
        out_shape=(
            jax.ShapeDtypeStruct((width, lanes), BF16),
            jax.ShapeDtypeStruct((2, width), F32),
        )
        + chain_shapes(rows, width),
        scratch_shapes=[pltpu.VMEM((128, 2 * width), BF16)],
        input_output_aliases={3: 0},
        compiler_params=pltpu.CompilerParams(vmem_limit_bytes=16 << 20),
        name="late",
    )(observations, *parts, held)


def advance_kernel(
    block, all_ref, src_ref, x_ref, end0, means0, last0, end_ref, means_ref, last_ref
):
    rows, width = means_ref.shape[1], all_ref.shape[0]
    mine = lax.axis_index("tm") == block

    @pl.when(mine)
    def _():
        u = step(all_ref[:, 0:width], x_ref[...], src_ref[0:1, :])
        v = step(all_ref[:, width : 2 * width], u, src_ref[1:2, :])
        emit(lanes_shift(rows, width), rows, u, v, end_ref, means_ref, last_ref)

    @pl.when(jnp.logical_not(mine))
    def _():
        end_ref[...] = end0[...]
        means_ref[...] = means0[...]
        last_ref[...] = last0[...]


def advance(block, held, sources, x, before):
    vmem = pl.BlockSpec(memory_space=pltpu.VMEM)
    return pl.pallas_call(
        functools.partial(advance_kernel, block),
        in_specs=[vmem] * 6,
        out_shape=chain_shapes(before[1].shape[1], held.shape[0]),
        compiler_params=pltpu.CompilerParams(vmem_limit_bytes=8 << 20),
        name="advance",
    )(held, sources, x, *before)


def along(first, distance):
    route = []
    for index in range(2 * RING * RING):
        z, y, core = place(index)
        if (core == 0) == first:
            route.append((index, index_of(z, y + distance, core)))
        else:
            route.append((index, index_of(z + distance, y, core)))
    return route


SWAP = [(index, index ^ 1) for index in range(2 * RING * RING)]


def shards(transitions, gain, obs_op, observations, start):
    rows, width = transitions.shape[1], transitions.shape[2]
    mine = pack(transitions, gain, obs_op, start)
    near = [mine] + [lax.ppermute(mine, "state", along(True, d)) for d in range(1, RING)]
    line = jnp.concatenate(near, axis=0)
    ahead = lax.ppermute(line, "state", along(False, 1))
    behind = lax.ppermute(line, "state", along(False, RING - 1))
    half = line.shape[0] // 2
    across = [
        lax.ppermute(ahead[:half], "state", along(False, 1)),
        lax.ppermute(behind[half:], "state", along(False, RING - 1)),
    ]
    across = jnp.concatenate(across, axis=0)
    near_parts = [line, ahead, behind]
    near_parts += [lax.ppermute(part, "state", SWAP) for part in near_parts]
    held = early(near_parts, width)
    held, sources, *state = late(
        observations, (across, lax.ppermute(across, "state", SWAP)), held, rows
    )
    for block in range(1, BLOCKS):
        x = lax.ppermute(state[0], "tm", [(block - 1, block)])
        state = advance(block, held, sources, x, state)
    return state[1], state[2]


def solution(mesh):
    in_specs = (
        P("tm", "state", None),
        P("state", None),
        P(None, "state"),
        P("tm", None),
        P("state"),
    )
    out_specs = (P("tm", "state"), P("tm", "state"))
    return jax.shard_map(shards, mesh=mesh, in_specs=in_specs, out_specs=out_specs, check_vma=False)
```

time: 69.4 us -> 55.2 us (0.80)
  local copies, waits for them, and re-layouts: 11.8 us -> 0.11 us
  Pallas kernels: 9.06 us -> 5.49 us
  waiting for transfers between devices: 30.5 us -> 33.1 us
  between operations: 1.69 us -> 0.81 us
    unnamed x29 -> x3, local copies, waits for them, and re-layouts: 11.7 us -> 0.03 us
    pallas_call x5 -> x6, Pallas kernels: 9.06 us -> 5.49 us  [the longest x1 2.16 us: late(): pl.pallas_call(late_kernel, in_specs=[vmem] * 4, out_shape=(jax.ShapeDtyp...]
    ppermute x3, waiting for transfers between devices: 3.88 us -> 6.8 us  [shards(): lax.ppermute(mine, 'state', along(True, d))]
    ppermute x3, starting transfers between devices: 5.84 us -> 4.68 us  [shards(): lax.ppermute(mine, 'state', along(True, d))]
    ppermute x7 -> x8, starting transfers between devices: 7.08 us -> 8.13 us  [the longest x1 3.19 us: shards(): lax.ppermute(behind[half:], 'state', along(False, RING - 1))]
    ppermute x7 -> x8, waiting for transfers between devices: 14.5 us -> 13.9 us  [the longest x1 8.13 us: shards(): ahead = lax.ppermute(line, 'state', along(False, 1))]
  transfers between devices with their start and end apart: 13 -> 14, of which waited for: 7 -> 7; matrix products, arithmetic and copies ran while one was open for 1% -> 0% of each run, Pallas kernels for 0% -> 1%
where the time goes in v2:
time: 55.2 us; the launch traced here: 55 us
  waiting for transfers between devices  33.1 us (60%)
  starting transfers between devices  15.4 us (28%)
  Pallas kernels  5.49 us (10%)
  between operations  0.81 us (1%)
    ppermute x3, waiting for transfers between devices, shards(): x = lax.ppermute(state[0], 'tm', [(block - 1, block)])  12.4 us
    ppermute x1, waiting for transfers between devices, shards(): ahead = lax.ppermute(line, 'state', along(False, 1))  8.13 us
    ppermute x3, waiting for transfers between devices, shards(): lax.ppermute(mine, 'state', along(True, d))  6.8 us
    ppermute x3, starting transfers between devices, shards(): lax.ppermute(mine, 'state', along(True, d))  4.68 us
    ppermute x1, waiting for transfers between devices, shards(): lax.ppermute(ahead[:half], 'state', along(False, 1))  4.26 us
    ppermute x1, starting transfers between devices, shards(): lax.ppermute(behind[half:], 'state', along(False, RING - 1))  3.19 us
    ppermute x3, starting transfers between devices, shards(): x = lax.ppermute(state[0], 'tm', [(block - 1, block)])  2.62 us
    ppermute x1, starting transfers between devices, shards(): behind = lax.ppermute(line, 'state', along(False, RING - 1))  2.2 us
  transfers between devices with their start and end apart: 14, of which 7 were waited for; matrix products, arithmetic and copies ran while one was open for 0% of the time, Pallas kernels for 1%

profile of v2, /device:TPU:6, one launch (start us, length us, event | category | flops | bytes accessed | tf_op | source)
XLA Modules:
  0.0 55.0 jit_solution(16289662366737666425)
XLA Ops:
  0.6 0.9 %pack.1 = bf16[32,2432]{1,0:T(8,128)(2,1)S(1)} custom-call(bf16[2,32,1024]{2,1,0:T(8,128)(2,1)} %trans_ref.1, bf16[32,128]{1,0:T(8,128)(2,1)} %gain_ref.1, bf16[32,128]{1,0:T(8,128)(2,1)} %bitcast.2, f32[1,32]{1,0:T(1,128)} %bitcast.3), custom_call_target="tpu_custom_call" | custom-call | tf_op jit(solution)/shard_map/pack/pallas_call | solution.py:66
  1.6 3.1 %collective-permute-start.2 = (bf16[32,2432]{1,0:T(8,128)(2,1)S(1)}, bf16[32,2432]{1,0:T(8,128)(2,1)S(1)}, u32[]{:S(2)}, u32[]{:S(2)}) collective-permute-start(bf16[32,2432]{1,0:T(8,128)(2,1)S(1)} %pack.1), channel_id=1, source_target_pairs={{0,6},{1,25},{2,0},{3,27},{4,2},{5,29},{6,4},{7,31},{8,14},{9,1},{... | collective-permute-start | bytes 466952 | tf_op jit(solution)/shard_map/ppermute | solution.py:256
  4.7 0.6 %collective-permute-start.1 = (bf16[32,2432]{1,0:T(8,128)(2,1)S(1)}, bf16[32,2432]{1,0:T(8,128)(2,1)S(1)}, u32[]{:S(2)}, u32[]{:S(2)}) collective-permute-start(bf16[32,2432]{1,0:T(8,128)(2,1)S(1)} %pack.1), channel_id=1, source_target_pairs={{0,4},{1,17},{2,6},{3,19},{4,0},{5,21},{6,2},{7,23},{8,12},{9,25},... | collective-permute-start | bytes 466952 | tf_op jit(solution)/shard_map/ppermute | solution.py:256
  5.3 1.0 %collective-permute-start = (bf16[32,2432]{1,0:T(8,128)(2,1)S(1)}, bf16[32,2432]{1,0:T(8,128)(2,1)S(1)}, u32[]{:S(2)}, u32[]{:S(2)}) collective-permute-start(bf16[32,2432]{1,0:T(8,128)(2,1)S(1)} %pack.1), channel_id=1, source_target_pairs={{0,2},{1,9},{2,4},{3,11},{4,6},{5,13},{6,0},{7,15},{8,10},{9,17},{... | collective-permute-start | bytes 466952 | tf_op jit(solution)/shard_map/ppermute | solution.py:256
  6.3 2.8 %collective-permute-done.2 = bf16[32,2432]{1,0:T(8,128)(2,1)S(1)} collective-permute-done((bf16[32,2432]{1,0:T(8,128)(2,1)S(1)}, bf16[32,2432]{1,0:T(8,128)(2,1)S(1)}, u32[]{:S(2)}, u32[]{:S(2)}) %collective-permute-start.2) | collective-permute-done | bytes 155680 | tf_op jit(solution)/shard_map/ppermute | solution.py:256
  9.1 2.4 %collective-permute-done.1 = bf16[32,2432]{1,0:T(8,128)(2,1)S(1)} collective-permute-done((bf16[32,2432]{1,0:T(8,128)(2,1)S(1)}, bf16[32,2432]{1,0:T(8,128)(2,1)S(1)}, u32[]{:S(2)}, u32[]{:S(2)}) %collective-permute-start.1) | collective-permute-done | bytes 155680 | tf_op jit(solution)/shard_map/ppermute | solution.py:256
  11.5 1.6 %collective-permute-done = bf16[32,2432]{1,0:T(8,128)(2,1)S(1)} collective-permute-done((bf16[32,2432]{1,0:T(8,128)(2,1)S(1)}, bf16[32,2432]{1,0:T(8,128)(2,1)S(1)}, u32[]{:S(2)}, u32[]{:S(2)}) %collective-permute-start) | collective-permute-done | bytes 155680 | tf_op jit(solution)/shard_map/ppermute | solution.py:256
  13.1 2.0 %collective-permute-start.3 = (bf16[128,2432]{1,0:T(8,128)(2,1)S(1)}, bf16[128,2432]{1,0:T(8,128)(2,1)S(1)}, u32[]{:S(2)}, u32[]{:S(2)}) collective-permute-start(bf16[128,2432]{1,0:T(8,128)(2,1)S(1)} %pad_maximum_fusion.refs_0_), channel_id=1, source_target_pairs={{0,8},{1,3},{2,10},{3,5},{4,12},{5,7},{6,14},{7,1},{8,16},{9,11},{... | collective-permute-start | bytes 1867784 | tf_op jit(solution)/shard_map/ppermute | solution.py:258
  15.1 2.2 %collective-permute-start.5 = (bf16[128,2432]{1,0:T(8,128)(2,1)S(1)}, bf16[128,2432]{1,0:T(8,128)(2,1)S(1)}, u32[]{:S(2)}, u32[]{:S(2)}) collective-permute-start(bf16[128,2432]{1,0:T(8,128)(2,1)S(1)} %pad_maximum_fusion.refs_0_), channel_id=1, source_target_pairs={{0,24},{1,7},{2,26},{3,1},{4,28},{5,3},{6,30},{7,5},{8,0},{9,15},{... | collective-permute-start | bytes 1867784 | tf_op jit(solution)/shard_map/ppermute | solution.py:259
  17.3 8.1 %collective-permute-done.3.refs_1_ = bf16[128,2432]{1,0:T(8,128)(2,1)S(1)} collective-permute-done((bf16[128,2432]{1,0:T(8,128)(2,1)S(1)}, bf16[128,2432]{1,0:T(8,128)(2,1)S(1)}, u32[]{:S(2)}, u32[]{:S(2)}) %collective-permute-start.3) | collective-permute-done | bytes 622624 | tf_op jit(solution)/shard_map/ppermute | solution.py:258
  25.5 0.1 collective-permute-start.4
  25.5 0.1 collective-permute-start.8
  25.6 0.0 collective-permute-done.5.refs_2_
  25.7 3.2 %collective-permute-start.6 = (bf16[64,2432]{1,0:T(8,128)(2,1)S(1)}, bf16[64,2432]{1,0:T(8,128)(2,1)S(1)}, u32[]{:S(2)}, u32[]{:S(2)}) collective-permute-start(bf16[64,2432]{1,0:T(8,128)(2,1)S(1)} %slice.9), channel_id=1, source_target_pairs={{0,24},{1,7},{2,26},{3,1},{4,28},{5,3},{6,30},{7,5},{8,0},{9,15},{... | collective-permute-start | bytes 933896 | tf_op jit(solution)/shard_map/ppermute | solution.py:263
  28.9 0.0 collective-permute-start.10
  28.9 0.5 collective-permute-start.9
  29.4 4.3 %collective-permute-done.4 = bf16[64,2432]{1,0:T(8,128)(2,1)S(1)} collective-permute-done((bf16[64,2432]{1,0:T(8,128)(2,1)S(1)}, bf16[64,2432]{1,0:T(8,128)(2,1)S(1)}, u32[]{:S(2)}, u32[]{:S(2)}) %collective-permute-start.4) | collective-permute-done | bytes 311328 | tf_op jit(solution)/shard_map/ppermute | solution.py:262
  33.7 0.0 collective-permute-done.6
  33.7 0.0 copy-start
  33.7 0.1 collective-permute-start.7
  33.8 0.0 collective-permute-done.8.refs_3_
  33.8 0.0 collective-permute-done.10.refs_5_
  33.8 0.0 collective-permute-done.9.refs_4_
  33.8 0.5 early.1.held_ref
  34.3 1.5 %collective-permute-done.7.part1 = bf16[128,2432]{1,0:T(8,128)(2,1)S(1)} collective-permute-done((bf16[128,2432]{1,0:T(8,128)(2,1)S(1)}, bf16[128,2432]{1,0:T(8,128)(2,1)S(1)}, u32[]{:S(2)}, u32[]{:S(2)}) %collective-permute-start.7) | collective-permute-done | bytes 622624 | tf_op jit(solution)/shard_map/ppermute | solution.py:270
  35.9 0.0 copy-done
  35.9 2.2 %late.1 = (bf16[1024,2432]{1,0:T(8,128)(2,1)S(1)}, f32[2,1024]{1,0:T(2,128)S(1)}, f32[1,1024]{1,0:T(1,128)S(1)}, f32[2,32]{1,0:T(2,128)S(1)}, f32[1,32]{1,0:T(1,128)S(1)}) custom-call(f32[2,128]{1,0:T(2,128)S(1)} %copy-done, bf16[128,2432]{1,0:T(8,128)(2,1)S(1)} %constant_dynamic-update-slice_fusion.part0, ...), custom_call_target="tpu_custom_call", output_to_operand_aliasing={{0}: (3, {})} | custom-call | tf_op jit(solution)/shard_map/late/pallas_call | solution.py:194
  38.0 0.7 %collective-permute-start.11 = (f32[1,1024]{1,0:T(1,128)S(1)}, f32[1,1024]{1,0:T(1,128)S(1)}, u32[]{:S(2)}, u32[]{:S(2)}) collective-permute-start(f32[1,1024]{1,0:T(1,128)S(1)} %get-tuple-element.17.end0), channel_id=1, source_target_pairs={{0,32},{1,33},{2,34},{3,35},{4,36},{5,37},{6,38},{7,39},{8,40},{9,... | collective-permute-start | bytes 12296 | tf_op jit(solution)/shard_map/ppermute | solution.py:273
  38.7 0.0 collective-permute-done.11.x_ref
  38.7 0.7 %collective-permute-start.12 = (f32[1,1024]{1,0:T(1,128)S(1)}, f32[1,1024]{1,0:T(1,128)S(1)}, u32[]{:S(2)}, u32[]{:S(2)}) collective-permute-start(f32[1,1024]{1,0:T(1,128)S(1)} %get-tuple-element.20.end0), channel_id=1, source_target_pairs={{32,64},{33,65},{34,66},{35,67},{36,68},{37,69},{38,70},{39,71},{4... | collective-permute-start | bytes 12296 | tf_op jit(solution)/shard_map/ppermute | solution.py:273
  39.4 0.0 collective-permute-done.12.x_ref
  39.4 1.3 %collective-permute-start.13 = (f32[1,1024]{1,0:T(1,128)S(1)}, f32[1,1024]{1,0:T(1,128)S(1)}, u32[]{:S(2)}, u32[]{:S(2)}) collective-permute-start(f32[1,1024]{1,0:T(1,128)S(1)} %get-tuple-element.23.end0), channel_id=1, source_target_pairs={{64,96},{65,97},{66,98},{67,99},{68,100},{69,101},{70,102},{71,103... | collective-permute-start | bytes 12296 | tf_op jit(solution)/shard_map/ppermute | solution.py:273
  40.7 12.4 %collective-permute-done.13.x_ref = f32[1,1024]{1,0:T(1,128)S(1)} collective-permute-done((f32[1,1024]{1,0:T(1,128)S(1)}, f32[1,1024]{1,0:T(1,128)S(1)}, u32[]{:S(2)}, u32[]{:S(2)}) %collective-permute-start.13) | collective-permute-done | bytes 4128 | tf_op jit(solution)/shard_map/ppermute | solution.py:273
  53.2 1.9 %advance.5 = (f32[1,1024]{1,0:T(1,128)}, f32[2,32]{1,0:T(2,128)}, f32[1,32]{1,0:T(1,128)}) custom-call(bf16[1024,2432]{1,0:T(8,128)(2,1)S(1)} %get-tuple-element.15.all_ref, f32[2,1024]{1,0:T(2,128)S(1)} %get-tuple-element.16.src_ref, f32[1,1024]{1,0:T(1,128)S(1)} %collective-permute-done.13.x_ref, f32[1,1024]{1,0:T(1,128)S(1)} %get-tuple-element.23.end0, ...), custom_call_target="tpu_custom_call" | custom-call | tf_op jit(solution)/shard_map/advance/pallas_call | solution.py:230
  (7 shorter events, 0.2 us)
Async XLA Ops:
  1.6 7.5 %collective-permute-start.2 = (bf16[32,2432]{1,0:T(8,128)(2,1)S(1)}, bf16[32,2432]{1,0:T(8,128)(2,1)S(1)}, u32[]{:S(2)}, u32[]{:S(2)}) collective-permute-start(bf16[32,2432]{1,0:T(8,128)(2,1)S(1)} %pack.1), channel_id=1, source_target_pairs={{0,6},{1,25},{2,0},{3,27},{4,2},{5,29},{6,4},{7,31},{8,14},{9,1},{... | collective-permute-start | bytes 466952 | tf_op jit(solution)/shard_map/ppermute | solution.py:256
  4.7 6.8 %collective-permute-start.1 = (bf16[32,2432]{1,0:T(8,128)(2,1)S(1)}, bf16[32,2432]{1,0:T(8,128)(2,1)S(1)}, u32[]{:S(2)}, u32[]{:S(2)}) collective-permute-start(bf16[32,2432]{1,0:T(8,128)(2,1)S(1)} %pack.1), channel_id=1, source_target_pairs={{0,4},{1,17},{2,6},{3,19},{4,0},{5,21},{6,2},{7,23},{8,12},{9,25},... | collective-permute-start | bytes 466952 | tf_op jit(solution)/shard_map/ppermute | solution.py:256
  5.3 7.8 %collective-permute-start = (bf16[32,2432]{1,0:T(8,128)(2,1)S(1)}, bf16[32,2432]{1,0:T(8,128)(2,1)S(1)}, u32[]{:S(2)}, u32[]{:S(2)}) collective-permute-start(bf16[32,2432]{1,0:T(8,128)(2,1)S(1)} %pack.1), channel_id=1, source_target_pairs={{0,2},{1,9},{2,4},{3,11},{4,6},{5,13},{6,0},{7,15},{8,10},{9,17},{... | collective-permute-start | bytes 466952 | tf_op jit(solution)/shard_map/ppermute | solution.py:256
  13.1 12.3 %collective-permute-start.3 = (bf16[128,2432]{1,0:T(8,128)(2,1)S(1)}, bf16[128,2432]{1,0:T(8,128)(2,1)S(1)}, u32[]{:S(2)}, u32[]{:S(2)}) collective-permute-start(bf16[128,2432]{1,0:T(8,128)(2,1)S(1)} %pad_maximum_fusion.refs_0_), channel_id=1, source_target_pairs={{0,8},{1,3},{2,10},{3,5},{4,12},{5,7},{6,14},{7,1},{8,16},{9,11},{... | collective-permute-start | bytes 1867784 | tf_op jit(solution)/shard_map/ppermute | solution.py:258
  15.1 10.5 %collective-permute-start.5 = (bf16[128,2432]{1,0:T(8,128)(2,1)S(1)}, bf16[128,2432]{1,0:T(8,128)(2,1)S(1)}, u32[]{:S(2)}, u32[]{:S(2)}) collective-permute-start(bf16[128,2432]{1,0:T(8,128)(2,1)S(1)} %pad_maximum_fusion.refs_0_), channel_id=1, source_target_pairs={{0,24},{1,7},{2,26},{3,1},{4,28},{5,3},{6,30},{7,5},{8,0},{9,15},{... | collective-permute-start | bytes 1867784 | tf_op jit(solution)/shard_map/ppermute | solution.py:259
  25.5 8.2 %collective-permute-start.4 = (bf16[64,2432]{1,0:T(8,128)(2,1)S(1)}, bf16[64,2432]{1,0:T(8,128)(2,1)S(1)}, u32[]{:S(2)}, u32[]{:S(2)}) collective-permute-start(bf16[64,2432]{1,0:T(8,128)(2,1)S(1)} %slice.8), channel_id=1, source_target_pairs={{0,8},{1,3},{2,10},{3,5},{4,12},{5,7},{6,14},{7,1},{8,16},{9,11},{... | collective-permute-start | bytes 933896 | tf_op jit(solution)/shard_map/ppermute | solution.py:262
  25.5 8.3 %collective-permute-start.8 = (bf16[128,2432]{1,0:T(8,128)(2,1)S(1)}, bf16[128,2432]{1,0:T(8,128)(2,1)S(1)}, u32[]{:S(2)}, u32[]{:S(2)}) collective-permute-start(bf16[128,2432]{1,0:T(8,128)(2,1)S(1)} %pad_maximum_fusion.refs_0_), channel_id=1, source_target_pairs={{0,1},{1,0},{2,3},{3,2},{4,5},{5,4},{6,7},{7,6},{8,9},{9,8},{10,11... | collective-permute-start | bytes 1867784 | tf_op jit(solution)/shard_map/ppermute | solution.py:267
  25.7 8.0 %collective-permute-start.6 = (bf16[64,2432]{1,0:T(8,128)(2,1)S(1)}, bf16[64,2432]{1,0:T(8,128)(2,1)S(1)}, u32[]{:S(2)}, u32[]{:S(2)}) collective-permute-start(bf16[64,2432]{1,0:T(8,128)(2,1)S(1)} %slice.9), channel_id=1, source_target_pairs={{0,24},{1,7},{2,26},{3,1},{4,28},{5,3},{6,30},{7,5},{8,0},{9,15},{... | collective-permute-start | bytes 933896 | tf_op jit(solution)/shard_map/ppermute | solution.py:263
  28.9 5.0 %collective-permute-start.10 = (bf16[128,2432]{1,0:T(8,128)(2,1)S(1)}, bf16[128,2432]{1,0:T(8,128)(2,1)S(1)}, u32[]{:S(2)}, u32[]{:S(2)}) collective-permute-start(bf16[128,2432]{1,0:T(8,128)(2,1)S(1)} %collective-permute-done.5.refs_2_), channel_id=1, source_target_pairs={{0,1},{1,0},{2,3},{3,2},{4,5},{5,4},{6,7},{7,6},{8,9},{9,8},{10,11... | collective-permute-start | bytes 1867784 | tf_op jit(solution)/shard_map/ppermute | solution.py:267
  28.9 5.0 %collective-permute-start.9 = (bf16[128,2432]{1,0:T(8,128)(2,1)S(1)}, bf16[128,2432]{1,0:T(8,128)(2,1)S(1)}, u32[]{:S(2)}, u32[]{:S(2)}) collective-permute-start(bf16[128,2432]{1,0:T(8,128)(2,1)S(1)} %collective-permute-done.3.refs_1_), channel_id=1, source_target_pairs={{0,1},{1,0},{2,3},{3,2},{4,5},{5,4},{6,7},{7,6},{8,9},{9,8},{10,11... | collective-permute-start | bytes 1867784 | tf_op jit(solution)/shard_map/ppermute | solution.py:267
  33.7 2.1 %copy-start = (f32[2,128]{1,0:T(2,128)S(1)}, f32[2,128]{1,0:T(2,128)}, u32[]{:S(2)}) copy-start(f32[2,128]{1,0:T(2,128)} %obs_ref.1) | copy-start | bytes 3076
  33.7 2.1 %collective-permute-start.7 = (bf16[128,2432]{1,0:T(8,128)(2,1)S(1)}, bf16[128,2432]{1,0:T(8,128)(2,1)S(1)}, u32[]{:S(2)}, u32[]{:S(2)}) collective-permute-start(bf16[128,2432]{1,0:T(8,128)(2,1)S(1)} %constant_dynamic-update-slice_fusion.part0), channel_id=1, source_target_pairs={{0,1},{1,0},{2,3},{3,2},{4,5},{5,4},{6,7},{7,6},{8,9},{9,8},{10,11... | collective-permute-start | bytes 1867784 | tf_op jit(solution)/shard_map/ppermute | solution.py:270
  38.0 0.7 %collective-permute-start.11 = (f32[1,1024]{1,0:T(1,128)S(1)}, f32[1,1024]{1,0:T(1,128)S(1)}, u32[]{:S(2)}, u32[]{:S(2)}) collective-permute-start(f32[1,1024]{1,0:T(1,128)S(1)} %get-tuple-element.17.end0), channel_id=1, source_target_pairs={{0,32},{1,33},{2,34},{3,35},{4,36},{5,37},{6,38},{7,39},{8,40},{9,... | collective-permute-start | bytes 12296 | tf_op jit(solution)/shard_map/ppermute | solution.py:273
  38.7 0.7 %collective-permute-start.12 = (f32[1,1024]{1,0:T(1,128)S(1)}, f32[1,1024]{1,0:T(1,128)S(1)}, u32[]{:S(2)}, u32[]{:S(2)}) collective-permute-start(f32[1,1024]{1,0:T(1,128)S(1)} %get-tuple-element.20.end0), channel_id=1, source_target_pairs={{32,64},{33,65},{34,66},{35,67},{36,68},{37,69},{38,70},{39,71},{4... | collective-permute-start | bytes 12296 | tf_op jit(solution)/shard_map/ppermute | solution.py:273
  39.4 13.7 %collective-permute-start.13 = (f32[1,1024]{1,0:T(1,128)S(1)}, f32[1,1024]{1,0:T(1,128)S(1)}, u32[]{:S(2)}, u32[]{:S(2)}) collective-permute-start(f32[1,1024]{1,0:T(1,128)S(1)} %get-tuple-element.23.end0), channel_id=1, source_target_pairs={{64,96},{65,97},{66,98},{67,99},{68,100},{69,101},{70,102},{71,103... | collective-permute-start | bytes 12296 | tf_op jit(solution)/shard_map/ppermute | solution.py:273

commit v3 on v2

--- a/solution.py
+++ b/solution.py
@@ -73,17 +73,6 @@
     )(*(pltpu.with_memory_space_constraint(x, pltpu.HBM) for x in (transitions, gain, obs_op.T, start[None, :])))
 
 
-def own_lanes(x, shift, rows):
-    return pltpu.roll(x, shift, 1)[:, 0:rows]
-
-
-def emit(shift, rows, u, v, end_ref, means_ref, last_ref):
-    end_ref[...] = v
-    mine = own_lanes(jnp.concatenate([u, v] + [u] * 6, axis=0), shift, rows)
-    means_ref[...] = mine[0:2]
-    last_ref[...] = mine[1:2]
-
-
 def place(index):
     return index // (2 * RING), (index // 2) % RING, index % 2
 
@@ -140,10 +129,11 @@
     return parts[0:1] + parts[1:2] + parts[2:3]
 
 
-def late_kernel(obs_ref, part0, part1, held_ref, all_ref, src_ref, end_ref, means_ref, last_ref, seen):
+def late_kernel(
+    obs_ref, part0, part1, held_ref, all_ref, end_ref, kept_ref
+):
     del held_ref
     width = all_ref.shape[0]
-    rows = means_ref.shape[1]
     g = 2 * width
     put_rows((part0, part1), LATE, all_ref)
     is_first = lax.axis_index("tm") == 0
@@ -162,78 +152,131 @@
             missed = stacked(obs_ref[k : k + 1, :] - seen_y, 16)
             x = y + total(dot(missed, all_ref[:, g + 128 : g + 256], BY_ROWS))
             states.append(x)
-        src_ref[...] = jnp.zeros_like(src_ref)
-        emit(lanes_shift(rows, width), rows, *states, end_ref, means_ref, last_ref)
+        kept_ref[...] = states[0]
+        end_ref[...] = states[1]
 
     @pl.when(jnp.logical_not(is_first))
     def _():
-        for k in range(2):
-            source = dot(stacked(obs_ref[k : k + 1, :], 16), all_ref[:, g + 128 : g + 256], BY_ROWS)
-            src_ref[k : k + 1, :] = total(source)
+        kept_ref[...] = jnp.zeros_like(kept_ref)
+        end_ref[...] = jnp.zeros_like(end_ref)
+
+
+def late(observations, parts, held):
+    vmem = pl.BlockSpec(memory_space=pltpu.VMEM)
+    width, lanes = held.shape
+    row = jax.ShapeDtypeStruct((1, width), F32)
+    return pl.pallas_call(
+        late_kernel,
+        in_specs=[vmem] * 4,
+        out_shape=(jax.ShapeDtypeStruct((width, lanes), BF16), row, row),
+        input_output_aliases={3: 0},
+        compiler_params=pltpu.CompilerParams(vmem_limit_bytes=4 << 20),
+        name="late",
+    )(observations, *parts, held)
+
+
+def models_kernel(obs_ref, held_ref, all_ref, both_ref, src_ref, seen):
+    del held_ref
+    width = all_ref.shape[0]
+    g = 2 * width
+
+    @pl.when(lax.axis_index("tm") > 0)
+    def _():
         seen[...] = dot(all_ref[:, g : g + 128], all_ref[:, 0:g], BY_COLUMNS).astype(BF16)
         for at in range(0, width, 128):
             fix = dot(all_ref[at : at + 128, g + 128 : g + 256], seen[...], MATMUL)
             model = all_ref[at : at + 128, 0:g].astype(F32) - fix
             all_ref[at : at + 128, 0:g] = model.astype(BF16)
-        end_ref[...] = jnp.zeros_like(end_ref)
-        means_ref[...] = jnp.zeros_like(means_ref)
-        last_ref[...] = jnp.zeros_like(last_ref)
-
-
-def chain_shapes(rows, width):
-    return (
-        jax.ShapeDtypeStruct((1, width), F32),
-        jax.ShapeDtypeStruct((2, rows), F32),
-        jax.ShapeDtypeStruct((1, rows), F32),
-    )
-
-
-def late(observations, parts, held, rows):
+        sources = [
+            total(dot(stacked(obs_ref[k : k + 1, :], 16), all_ref[:, g + 128 : g + 256], BY_ROWS))
+            for k in range(2)
+        ]
+        src_ref[0:1, :] = sources[0]
+        src_ref[1:2, :] = step(all_ref[:, width:g], sources[0], sources[1])
+        for at in range(0, width, 256):
+            rows = all_ref[at : at + 256, width:g]
+            both_ref[at : at + 256, :] = dot(rows, all_ref[:, 0:width], MATMUL).astype(BF16)
+
+
+def models(observations, held):
     vmem = pl.BlockSpec(memory_space=pltpu.VMEM)
     width, lanes = held.shape
     return pl.pallas_call(
-        late_kernel,
-        in_specs=[vmem] * 4,
+        models_kernel,
+        in_specs=[vmem] * 2,
         out_shape=(
             jax.ShapeDtypeStruct((width, lanes), BF16),
+            jax.ShapeDtypeStruct((width, width), BF16),
             jax.ShapeDtypeStruct((2, width), F32),
-        )
-        + chain_shapes(rows, width),
+        ),
         scratch_shapes=[pltpu.VMEM((128, 2 * width), BF16)],
-        input_output_aliases={3: 0},
+        input_output_aliases={1: 0},
         compiler_params=pltpu.CompilerParams(vmem_limit_bytes=16 << 20),
-        name="late",
-    )(observations, *parts, held)
-
-
-def advance_kernel(
-    block, all_ref, src_ref, x_ref, end0, means0, last0, end_ref, means_ref, last_ref
-):
+        cost_estimate=pl.CostEstimate(
+            flops=2 * width**3, bytes_accessed=8 * width * width, transcendentals=0
+        ),
+        name="models",
+    )(observations, held)
+
+
+def advance_kernel(block, both_ref, src_ref, x_ref, end0, kept0, end_ref, kept_ref):
+    mine = lax.axis_index("tm") == block
+
+    @pl.when(mine)
+    def _():
+        x = x_ref[...]
+        end_ref[...] = step(both_ref[...], x, src_ref[1:2, :])
+        kept_ref[...] = x
+
+    @pl.when(jnp.logical_not(mine))
+    def _():
+        end_ref[...] = end0[...]
+        kept_ref[...] = kept0[...]
+
+
+def advance(block, both, sources, x, end, kept):
+    row = jax.ShapeDtypeStruct(x.shape, F32)
+    return pl.pallas_call(
+        functools.partial(advance_kernel, block),
+        in_specs=[pl.BlockSpec(memory_space=pltpu.VMEM)] * 5,
+        out_shape=(row, row),
+        compiler_params=pltpu.CompilerParams(vmem_limit_bytes=4 << 20),
+        name="advance",
+    )(both, sources, x, end, kept)
+
+
+def finish_kernel(all_ref, both_ref, src_ref, x_ref, end_ref, kept_ref, means_ref, last_ref, held):
     rows, width = means_ref.shape[1], all_ref.shape[0]
-    mine = lax.axis_index("tm") == block
-
-    @pl.when(mine)
-    def _():
-        u = step(all_ref[:, 0:width], x_ref[...], src_ref[0:1, :])
-        v = step(all_ref[:, width : 2 * width], u, src_ref[1:2, :])
-        emit(lanes_shift(rows, width), rows, u, v, end_ref, means_ref, last_ref)
-
-    @pl.when(jnp.logical_not(mine))
-    def _():
-        end_ref[...] = end0[...]
-        means_ref[...] = means0[...]
-        last_ref[...] = last0[...]
-
-
-def advance(block, held, sources, x, before):
-    vmem = pl.BlockSpec(memory_space=pltpu.VMEM)
-    return pl.pallas_call(
-        functools.partial(advance_kernel, block),
-        in_specs=[vmem] * 6,
-        out_shape=chain_shapes(before[1].shape[1], held.shape[0]),
-        compiler_params=pltpu.CompilerParams(vmem_limit_bytes=8 << 20),
-        name="advance",
-    )(held, sources, x, *before)
+    here = lax.axis_index("tm")
+    held[0:1, :] = kept_ref[...]
+    held[1:2, :] = end_ref[...]
+
+    @pl.when(here == BLOCKS - 1)
+    def _():
+        held[0:1, :] = step(all_ref[:, 0:width], x_ref[...], src_ref[0:1, :])
+        held[1:2, :] = step(both_ref[...], x_ref[...], src_ref[1:2, :])
+
+    @pl.when(jnp.logical_and(here > 0, here < BLOCKS - 1))
+    def _():
+        held[0:1, :] = step(all_ref[:, 0:width], kept_ref[...], src_ref[0:1, :])
+
+    mine = pltpu.roll(held[...], lanes_shift(rows, width), 1)
+    means_ref[...] = mine[0:2, 0:rows]
+    last_ref[...] = mine[1:2, 0:rows]
+
+
+def finish(held, both, sources, x, end, kept, rows):
+    return pl.pallas_call(
+        finish_kernel,
+        in_specs=[pl.BlockSpec(memory_space=pltpu.VMEM)] * 6,
+        out_shape=(
+            jax.ShapeDtypeStruct((2, rows), F32),
+            jax.ShapeDtypeStruct((1, rows), F32),
+        ),
+        scratch_shapes=[pltpu.VMEM((8, held.shape[0]), F32)],
+        compiler_params=pltpu.CompilerParams(vmem_limit_bytes=4 << 20),
+        name="finish",
+    )(held, both, sources, x, end, kept)
 
 
 def along(first, distance):
@@ -266,13 +309,16 @@
     near_parts = [line, ahead, behind]
     near_parts += [lax.ppermute(part, "state", SWAP) for part in near_parts]
     held = early(near_parts, width)
-    held, sources, *state = late(
-        observations, (across, lax.ppermute(across, "state", SWAP)), held, rows
-    )
-    for block in range(1, BLOCKS):
-        x = lax.ppermute(state[0], "tm", [(block - 1, block)])
-        state = advance(block, held, sources, x, state)
-    return state[1], state[2]
+    across = (across, lax.ppermute(across, "state", SWAP))
+    held, end, kept = late(observations, across, held)
+    x = lax.ppermute(end, "tm", [(0, 1)])
+    held, both, sources = models(observations, held)
+    end, kept = advance(1, both, sources, x, end, kept)
+    for block in range(2, BLOCKS - 1):
+        x = lax.ppermute(end, "tm", [(block - 1, block)])
+        end, kept = advance(block, both, sources, x, end, kept)
+    x = lax.ppermute(end, "tm", [(BLOCKS - 2, BLOCKS - 1)])
+    return finish(held, both, sources, x, end, kept, rows)
 
 
 def solution(mesh):

time: 55.2 us -> 51.7 us (0.937)
  waiting for transfers between devices: 33.1 us -> 25.7 us
  Pallas kernels: 5.49 us -> 8.28 us
  starting transfers between devices: 15.4 us -> 16.6 us
    pallas_call x3 -> x4, Pallas kernels: 1.92 us -> 6.68 us  [the longest x1 4.78 us: models(): pl.pallas_call(models_kernel, in_specs=[vmem] * 2, out_shape=(jax.ShapeDt...]
    ppermute x4, waiting for transfers between devices: 13.9 us -> 9.37 us  [the longest x1 7.83 us: shards(): x = lax.ppermute(end, 'tm', [(BLOCKS - 2, BLOCKS - 1)])]
    ppermute x3, waiting for transfers between devices: 6.8 us -> 3.88 us  [shards(): lax.ppermute(mine, 'state', along(True, d))]
    pallas_call x1, Pallas kernels: 2.16 us -> 0.19 us  [late(): pl.pallas_call(late_kernel, in_specs=[vmem] * 4, out_shape=(jax.ShapeDtyp...]
    ppermute x3, starting transfers between devices: 4.68 us -> 5.89 us  [shards(): lax.ppermute(mine, 'state', along(True, d))]
  transfers between devices with their start and end apart: 14 -> 14, of which waited for: 7 -> 7; matrix products, arithmetic and copies ran while one was open for 0% -> 0% of each run, Pallas kernels for 1% -> 10%
where the time goes in v3:
time: 51.7 us; the launch traced here: 51.5 us
  waiting for transfers between devices  25.7 us (50%)
  starting transfers between devices  16.6 us (32%)
  Pallas kernels  8.28 us (16%)
  between operations  0.82 us (2%)
    ppermute x1, waiting for transfers between devices, shards(): ahead = lax.ppermute(line, 'state', along(False, 1))  8.13 us
    ppermute x1, waiting for transfers between devices, shards(): x = lax.ppermute(end, 'tm', [(BLOCKS - 2, BLOCKS - 1)])  7.83 us
    ppermute x3, starting transfers between devices, shards(): lax.ppermute(mine, 'state', along(True, d))  5.89 us
    pallas_call x1, Pallas kernels, models(): pl.pallas_call(models_kernel, in_specs=[vmem] * 2, out_shape=(jax.ShapeDt...  4.78 us
    ppermute x1, waiting for transfers between devices, shards(): lax.ppermute(ahead[:half], 'state', along(False, 1))  4.26 us
    ppermute x3, waiting for transfers between devices, shards(): lax.ppermute(mine, 'state', along(True, d))  3.88 us
    ppermute x1, starting transfers between devices, shards(): lax.ppermute(behind[half:], 'state', along(False, RING - 1))  3.19 us
    ppermute x1, starting transfers between devices, shards(): behind = lax.ppermute(line, 'state', along(False, RING - 1))  2.2 us
  transfers between devices with their start and end apart: 14, of which 7 were waited for; matrix products, arithmetic and copies ran while one was open for 0% of the time, Pallas kernels for 10%

profile of v3, /device:TPU:6, one launch (start us, length us, event | category | flops | bytes accessed | tf_op | source)
XLA Modules:
  0.0 51.5 jit_solution(15335068541335819073)
XLA Ops:
  0.6 0.9 %pack.1 = bf16[32,2432]{1,0:T(8,128)(2,1)S(1)} custom-call(bf16[2,32,1024]{2,1,0:T(8,128)(2,1)} %trans_ref.1, bf16[32,128]{1,0:T(8,128)(2,1)} %gain_ref.1, bf16[32,128]{1,0:T(8,128)(2,1)} %bitcast.2, f32[1,32]{1,0:T(1,128)} %bitcast.3), custom_call_target="tpu_custom_call" | custom-call | tf_op jit(solution)/shard_map/pack/pallas_call | solution.py:66
  1.6 1.6 %collective-permute-start = (bf16[32,2432]{1,0:T(8,128)(2,1)S(1)}, bf16[32,2432]{1,0:T(8,128)(2,1)S(1)}, u32[]{:S(2)}, u32[]{:S(2)}) collective-permute-start(bf16[32,2432]{1,0:T(8,128)(2,1)S(1)} %pack.1), channel_id=1, source_target_pairs={{0,2},{1,9},{2,4},{3,11},{4,6},{5,13},{6,0},{7,15},{8,10},{9,17},{... | collective-permute-start | bytes 466952 | tf_op jit(solution)/shard_map/ppermute | solution.py:299
  3.2 2.9 %collective-permute-start.1 = (bf16[32,2432]{1,0:T(8,128)(2,1)S(1)}, bf16[32,2432]{1,0:T(8,128)(2,1)S(1)}, u32[]{:S(2)}, u32[]{:S(2)}) collective-permute-start(bf16[32,2432]{1,0:T(8,128)(2,1)S(1)} %pack.1), channel_id=1, source_target_pairs={{0,4},{1,17},{2,6},{3,19},{4,0},{5,21},{6,2},{7,23},{8,12},{9,25},... | collective-permute-start | bytes 466952 | tf_op jit(solution)/shard_map/ppermute | solution.py:299
  6.1 1.3 %collective-permute-start.2 = (bf16[32,2432]{1,0:T(8,128)(2,1)S(1)}, bf16[32,2432]{1,0:T(8,128)(2,1)S(1)}, u32[]{:S(2)}, u32[]{:S(2)}) collective-permute-start(bf16[32,2432]{1,0:T(8,128)(2,1)S(1)} %pack.1), channel_id=1, source_target_pairs={{0,6},{1,25},{2,0},{3,27},{4,2},{5,29},{6,4},{7,31},{8,14},{9,1},{... | collective-permute-start | bytes 466952 | tf_op jit(solution)/shard_map/ppermute | solution.py:299
  7.5 0.6 %collective-permute-done = bf16[32,2432]{1,0:T(8,128)(2,1)S(1)} collective-permute-done((bf16[32,2432]{1,0:T(8,128)(2,1)S(1)}, bf16[32,2432]{1,0:T(8,128)(2,1)S(1)}, u32[]{:S(2)}, u32[]{:S(2)}) %collective-permute-start) | collective-permute-done | bytes 155680 | tf_op jit(solution)/shard_map/ppermute | solution.py:299
  8.1 2.9 %collective-permute-done.1 = bf16[32,2432]{1,0:T(8,128)(2,1)S(1)} collective-permute-done((bf16[32,2432]{1,0:T(8,128)(2,1)S(1)}, bf16[32,2432]{1,0:T(8,128)(2,1)S(1)}, u32[]{:S(2)}, u32[]{:S(2)}) %collective-permute-start.1) | collective-permute-done | bytes 155680 | tf_op jit(solution)/shard_map/ppermute | solution.py:299
  11.0 0.4 collective-permute-done.2
  11.4 2.0 %collective-permute-start.3 = (bf16[128,2432]{1,0:T(8,128)(2,1)S(1)}, bf16[128,2432]{1,0:T(8,128)(2,1)S(1)}, u32[]{:S(2)}, u32[]{:S(2)}) collective-permute-start(bf16[128,2432]{1,0:T(8,128)(2,1)S(1)} %pad_maximum_fusion.refs_0_), channel_id=1, source_target_pairs={{0,8},{1,3},{2,10},{3,5},{4,12},{5,7},{6,14},{7,1},{8,16},{9,11},{... | collective-permute-start | bytes 1867784 | tf_op jit(solution)/shard_map/ppermute | solution.py:301
  13.4 2.2 %collective-permute-start.5 = (bf16[128,2432]{1,0:T(8,128)(2,1)S(1)}, bf16[128,2432]{1,0:T(8,128)(2,1)S(1)}, u32[]{:S(2)}, u32[]{:S(2)}) collective-permute-start(bf16[128,2432]{1,0:T(8,128)(2,1)S(1)} %pad_maximum_fusion.refs_0_), channel_id=1, source_target_pairs={{0,24},{1,7},{2,26},{3,1},{4,28},{5,3},{6,30},{7,5},{8,0},{9,15},{... | collective-permute-start | bytes 1867784 | tf_op jit(solution)/shard_map/ppermute | solution.py:302
  15.6 8.1 %collective-permute-done.3.refs_1_ = bf16[128,2432]{1,0:T(8,128)(2,1)S(1)} collective-permute-done((bf16[128,2432]{1,0:T(8,128)(2,1)S(1)}, bf16[128,2432]{1,0:T(8,128)(2,1)S(1)}, u32[]{:S(2)}, u32[]{:S(2)}) %collective-permute-start.3) | collective-permute-done | bytes 622624 | tf_op jit(solution)/shard_map/ppermute | solution.py:301
  23.7 0.1 collective-permute-start.4
  23.8 0.1 collective-permute-start.8
  23.9 0.0 collective-permute-done.5.refs_2_
  24.0 3.2 %collective-permute-start.6 = (bf16[64,2432]{1,0:T(8,128)(2,1)S(1)}, bf16[64,2432]{1,0:T(8,128)(2,1)S(1)}, u32[]{:S(2)}, u32[]{:S(2)}) collective-permute-start(bf16[64,2432]{1,0:T(8,128)(2,1)S(1)} %slice.9), channel_id=1, source_target_pairs={{0,24},{1,7},{2,26},{3,1},{4,28},{5,3},{6,30},{7,5},{8,0},{9,15},{... | collective-permute-start | bytes 933896 | tf_op jit(solution)/shard_map/ppermute | solution.py:306
  27.2 0.0 collective-permute-start.10
  27.2 0.5 collective-permute-start.9
  27.7 4.3 %collective-permute-done.4 = bf16[64,2432]{1,0:T(8,128)(2,1)S(1)} collective-permute-done((bf16[64,2432]{1,0:T(8,128)(2,1)S(1)}, bf16[64,2432]{1,0:T(8,128)(2,1)S(1)}, u32[]{:S(2)}, u32[]{:S(2)}) %collective-permute-start.4) | collective-permute-done | bytes 311328 | tf_op jit(solution)/shard_map/ppermute | solution.py:305
  32.0 0.0 collective-permute-done.6
  32.0 0.0 copy-start
  32.0 0.1 collective-permute-start.7
  32.1 0.0 collective-permute-done.8.refs_3_
  32.1 0.0 collective-permute-done.10.refs_5_
  32.1 0.0 collective-permute-done.9.refs_4_
  32.1 0.5 early.1.held_ref
  32.6 1.5 %collective-permute-done.7.part1 = bf16[128,2432]{1,0:T(8,128)(2,1)S(1)} collective-permute-done((bf16[128,2432]{1,0:T(8,128)(2,1)S(1)}, bf16[128,2432]{1,0:T(8,128)(2,1)S(1)}, u32[]{:S(2)}, u32[]{:S(2)}) %collective-permute-start.7) | collective-permute-done | bytes 622624 | tf_op jit(solution)/shard_map/ppermute | solution.py:312
  34.1 0.0 copy-done
  34.1 0.2 late.1
  34.3 0.7 %collective-permute-start.11 = (f32[1,1024]{1,0:T(1,128)S(1)}, f32[1,1024]{1,0:T(1,128)S(1)}, u32[]{:S(2)}, u32[]{:S(2)}) collective-permute-start(f32[1,1024]{1,0:T(1,128)S(1)} %get-tuple-element.16.end0), channel_id=1, source_target_pairs={{0,32},{1,33},{2,34},{3,35},{4,36},{5,37},{6,38},{7,39},{8,40},{9,... | collective-permute-start | bytes 12296 | tf_op jit(solution)/shard_map/ppermute | solution.py:314
  35.0 4.8 %models.1 = (bf16[1024,2432]{1,0:T(8,128)(2,1)S(1)}, bf16[1024,1024]{1,0:T(8,128)(2,1)S(1)}, f32[2,1024]{1,0:T(2,128)S(1)}) custom-call(f32[2,128]{1,0:T(2,128)S(1)} %copy-done, bf16[1024,2432]{1,0:T(8,128)(2,1)S(1)} %get-tuple-element.12.held_ref), custom_call_target="tpu_custom_call", output_to_operand_aliasing={{0}: (1, {})} | custom-call | flops 2147483648 | bytes 8388608 | tf_op jit(solution)/shard_map/models/pallas_call | solution.py:204
  39.8 0.0 collective-permute-done.11.x_ref
  39.8 0.7 %collective-permute-start.12 = (f32[1,1024]{1,0:T(1,128)S(1)}, f32[1,1024]{1,0:T(1,128)S(1)}, u32[]{:S(2)}, u32[]{:S(2)}) collective-permute-start(f32[1,1024]{1,0:T(1,128)S(1)} %get-tuple-element.18.end0), channel_id=1, source_target_pairs={{32,64},{33,65},{34,66},{35,67},{36,68},{37,69},{38,70},{39,71},{4... | collective-permute-start | bytes 12296 | tf_op jit(solution)/shard_map/ppermute | solution.py:318
  40.5 0.0 collective-permute-done.12.x_ref
  40.6 1.3 %collective-permute-start.13 = (f32[1,1024]{1,0:T(1,128)S(1)}, f32[1,1024]{1,0:T(1,128)S(1)}, u32[]{:S(2)}, u32[]{:S(2)}) collective-permute-start(f32[1,1024]{1,0:T(1,128)S(1)} %get-tuple-element.20.end_ref), channel_id=1, source_target_pairs={{64,96},{65,97},{66,98},{67,99},{68,100},{69,101},{70,102},{71,103... | collective-permute-start | bytes 12296 | tf_op jit(solution)/shard_map/ppermute | solution.py:320
  41.9 7.8 %collective-permute-done.13.x_ref = f32[1,1024]{1,0:T(1,128)S(1)} collective-permute-done((f32[1,1024]{1,0:T(1,128)S(1)}, f32[1,1024]{1,0:T(1,128)S(1)}, u32[]{:S(2)}, u32[]{:S(2)}) %collective-permute-start.13) | collective-permute-done | bytes 4128 | tf_op jit(solution)/shard_map/ppermute | solution.py:320
  49.7 1.9 %finish.1 = (f32[2,32]{1,0:T(2,128)}, f32[1,32]{1,0:T(1,128)}) custom-call(bf16[1024,2432]{1,0:T(8,128)(2,1)S(1)} %get-tuple-element.13.all_ref, bf16[1024,1024]{1,0:T(8,128)(2,1)S(1)} %get-tuple-element.14.both_ref, f32[2,1024]{1,0:T(2,128)S(1)} %get-tuple-element.15.src_ref, f32[1,1024]{1,0:T(1,128)S(1)} %collective-permute-done.13.x_ref, ...), custom_call_target="tpu_custom_call" | custom-call | tf_op jit(solution)/shard_map/finish/pallas_call | solution.py:269
  (7 shorter events, 0.2 us)
Async XLA Ops:
  1.6 6.5 %collective-permute-start = (bf16[32,2432]{1,0:T(8,128)(2,1)S(1)}, bf16[32,2432]{1,0:T(8,128)(2,1)S(1)}, u32[]{:S(2)}, u32[]{:S(2)}) collective-permute-start(bf16[32,2432]{1,0:T(8,128)(2,1)S(1)} %pack.1), channel_id=1, source_target_pairs={{0,2},{1,9},{2,4},{3,11},{4,6},{5,13},{6,0},{7,15},{8,10},{9,17},{... | collective-permute-start | bytes 466952 | tf_op jit(solution)/shard_map/ppermute | solution.py:299
  3.2 7.8 %collective-permute-start.1 = (bf16[32,2432]{1,0:T(8,128)(2,1)S(1)}, bf16[32,2432]{1,0:T(8,128)(2,1)S(1)}, u32[]{:S(2)}, u32[]{:S(2)}) collective-permute-start(bf16[32,2432]{1,0:T(8,128)(2,1)S(1)} %pack.1), channel_id=1, source_target_pairs={{0,4},{1,17},{2,6},{3,19},{4,0},{5,21},{6,2},{7,23},{8,12},{9,25},... | collective-permute-start | bytes 466952 | tf_op jit(solution)/shard_map/ppermute | solution.py:299
  6.1 5.2 %collective-permute-start.2 = (bf16[32,2432]{1,0:T(8,128)(2,1)S(1)}, bf16[32,2432]{1,0:T(8,128)(2,1)S(1)}, u32[]{:S(2)}, u32[]{:S(2)}) collective-permute-start(bf16[32,2432]{1,0:T(8,128)(2,1)S(1)} %pack.1), channel_id=1, source_target_pairs={{0,6},{1,25},{2,0},{3,27},{4,2},{5,29},{6,4},{7,31},{8,14},{9,1},{... | collective-permute-start | bytes 466952 | tf_op jit(solution)/shard_map/ppermute | solution.py:299
  11.4 12.3 %collective-permute-start.3 = (bf16[128,2432]{1,0:T(8,128)(2,1)S(1)}, bf16[128,2432]{1,0:T(8,128)(2,1)S(1)}, u32[]{:S(2)}, u32[]{:S(2)}) collective-permute-start(bf16[128,2432]{1,0:T(8,128)(2,1)S(1)} %pad_maximum_fusion.refs_0_), channel_id=1, source_target_pairs={{0,8},{1,3},{2,10},{3,5},{4,12},{5,7},{6,14},{7,1},{8,16},{9,11},{... | collective-permute-start | bytes 1867784 | tf_op jit(solution)/shard_map/ppermute | solution.py:301
  13.4 10.5 %collective-permute-start.5 = (bf16[128,2432]{1,0:T(8,128)(2,1)S(1)}, bf16[128,2432]{1,0:T(8,128)(2,1)S(1)}, u32[]{:S(2)}, u32[]{:S(2)}) collective-permute-start(bf16[128,2432]{1,0:T(8,128)(2,1)S(1)} %pad_maximum_fusion.refs_0_), channel_id=1, source_target_pairs={{0,24},{1,7},{2,26},{3,1},{4,28},{5,3},{6,30},{7,5},{8,0},{9,15},{... | collective-permute-start | bytes 1867784 | tf_op jit(solution)/shard_map/ppermute | solution.py:302
  23.7 8.2 %collective-permute-start.4 = (bf16[64,2432]{1,0:T(8,128)(2,1)S(1)}, bf16[64,2432]{1,0:T(8,128)(2,1)S(1)}, u32[]{:S(2)}, u32[]{:S(2)}) collective-permute-start(bf16[64,2432]{1,0:T(8,128)(2,1)S(1)} %slice.8), channel_id=1, source_target_pairs={{0,8},{1,3},{2,10},{3,5},{4,12},{5,7},{6,14},{7,1},{8,16},{9,11},{... | collective-permute-start | bytes 933896 | tf_op jit(solution)/shard_map/ppermute | solution.py:305
  23.8 8.3 %collective-permute-start.8 = (bf16[128,2432]{1,0:T(8,128)(2,1)S(1)}, bf16[128,2432]{1,0:T(8,128)(2,1)S(1)}, u32[]{:S(2)}, u32[]{:S(2)}) collective-permute-start(bf16[128,2432]{1,0:T(8,128)(2,1)S(1)} %pad_maximum_fusion.refs_0_), channel_id=1, source_target_pairs={{0,1},{1,0},{2,3},{3,2},{4,5},{5,4},{6,7},{7,6},{8,9},{9,8},{10,11... | collective-permute-start | bytes 1867784 | tf_op jit(solution)/shard_map/ppermute | solution.py:310
  24.0 8.0 %collective-permute-start.6 = (bf16[64,2432]{1,0:T(8,128)(2,1)S(1)}, bf16[64,2432]{1,0:T(8,128)(2,1)S(1)}, u32[]{:S(2)}, u32[]{:S(2)}) collective-permute-start(bf16[64,2432]{1,0:T(8,128)(2,1)S(1)} %slice.9), channel_id=1, source_target_pairs={{0,24},{1,7},{2,26},{3,1},{4,28},{5,3},{6,30},{7,5},{8,0},{9,15},{... | collective-permute-start | bytes 933896 | tf_op jit(solution)/shard_map/ppermute | solution.py:306
  27.2 5.0 %collective-permute-start.10 = (bf16[128,2432]{1,0:T(8,128)(2,1)S(1)}, bf16[128,2432]{1,0:T(8,128)(2,1)S(1)}, u32[]{:S(2)}, u32[]{:S(2)}) collective-permute-start(bf16[128,2432]{1,0:T(8,128)(2,1)S(1)} %collective-permute-done.5.refs_2_), channel_id=1, source_target_pairs={{0,1},{1,0},{2,3},{3,2},{4,5},{5,4},{6,7},{7,6},{8,9},{9,8},{10,11... | collective-permute-start | bytes 1867784 | tf_op jit(solution)/shard_map/ppermute | solution.py:310
  27.2 5.0 %collective-permute-start.9 = (bf16[128,2432]{1,0:T(8,128)(2,1)S(1)}, bf16[128,2432]{1,0:T(8,128)(2,1)S(1)}, u32[]{:S(2)}, u32[]{:S(2)}) collective-permute-start(bf16[128,2432]{1,0:T(8,128)(2,1)S(1)} %collective-permute-done.3.refs_1_), channel_id=1, source_target_pairs={{0,1},{1,0},{2,3},{3,2},{4,5},{5,4},{6,7},{7,6},{8,9},{9,8},{10,11... | collective-permute-start | bytes 1867784 | tf_op jit(solution)/shard_map/ppermute | solution.py:310
  32.0 2.1 %copy-start = (f32[2,128]{1,0:T(2,128)S(1)}, f32[2,128]{1,0:T(2,128)}, u32[]{:S(2)}) copy-start(f32[2,128]{1,0:T(2,128)} %obs_ref.3) | copy-start | bytes 3076
  32.0 2.1 %collective-permute-start.7 = (bf16[128,2432]{1,0:T(8,128)(2,1)S(1)}, bf16[128,2432]{1,0:T(8,128)(2,1)S(1)}, u32[]{:S(2)}, u32[]{:S(2)}) collective-permute-start(bf16[128,2432]{1,0:T(8,128)(2,1)S(1)} %constant_dynamic-update-slice_fusion.part0), channel_id=1, source_target_pairs={{0,1},{1,0},{2,3},{3,2},{4,5},{5,4},{6,7},{7,6},{8,9},{9,8},{10,11... | collective-permute-start | bytes 1867784 | tf_op jit(solution)/shard_map/ppermute | solution.py:312
  34.3 5.5 %collective-permute-start.11 = (f32[1,1024]{1,0:T(1,128)S(1)}, f32[1,1024]{1,0:T(1,128)S(1)}, u32[]{:S(2)}, u32[]{:S(2)}) collective-permute-start(f32[1,1024]{1,0:T(1,128)S(1)} %get-tuple-element.16.end0), channel_id=1, source_target_pairs={{0,32},{1,33},{2,34},{3,35},{4,36},{5,37},{6,38},{7,39},{8,40},{9,... | collective-permute-start | bytes 12296 | tf_op jit(solution)/shard_map/ppermute | solution.py:314
  39.8 0.7 %collective-permute-start.12 = (f32[1,1024]{1,0:T(1,128)S(1)}, f32[1,1024]{1,0:T(1,128)S(1)}, u32[]{:S(2)}, u32[]{:S(2)}) collective-permute-start(f32[1,1024]{1,0:T(1,128)S(1)} %get-tuple-element.18.end0), channel_id=1, source_target_pairs={{32,64},{33,65},{34,66},{35,67},{36,68},{37,69},{38,70},{39,71},{4... | collective-permute-start | bytes 12296 | tf_op jit(solution)/shard_map/ppermute | solution.py:318
  40.6 9.1 %collective-permute-start.13 = (f32[1,1024]{1,0:T(1,128)S(1)}, f32[1,1024]{1,0:T(1,128)S(1)}, u32[]{:S(2)}, u32[]{:S(2)}) collective-permute-start(f32[1,1024]{1,0:T(1,128)S(1)} %get-tuple-element.20.end_ref), channel_id=1, source_target_pairs={{64,96},{65,97},{66,98},{67,99},{68,100},{69,101},{70,102},{71,103... | collective-permute-start | bytes 12296 | tf_op jit(solution)/shard_map/ppermute | solution.py:320

commit v4 on v3

--- a/solution.py
+++ b/solution.py
@@ -81,6 +81,7 @@
     return ((z % RING) * RING + y % RING) * 2 + core
 
 
+NEAR = (0, 3, 2, 1)
 EARLY, LATE = (0, 1, RING - 1), (2,)
 
 
@@ -90,7 +91,7 @@
     offsets = []
     for side in (core, 1 - core):
         for far in fars:
-            for near in range(RING):
+            for near in NEAR:
                 dz = far + side * (near - far)
                 dy = near + side * (far - near)
                 offsets.append(rows * index_of(z - dz, y - dy, side))
@@ -175,7 +176,7 @@
     )(observations, *parts, held)
 
 
-def models_kernel(obs_ref, held_ref, all_ref, both_ref, src_ref, seen):
+def models_kernel(obs_ref, held_ref, all_ref, src_ref, seen):
     del held_ref
     width = all_ref.shape[0]
     g = 2 * width
@@ -192,10 +193,7 @@
             for k in range(2)
         ]
         src_ref[0:1, :] = sources[0]
-        src_ref[1:2, :] = step(all_ref[:, width:g], sources[0], sources[1])
-        for at in range(0, width, 256):
-            rows = all_ref[at : at + 256, width:g]
-            both_ref[at : at + 256, :] = dot(rows, all_ref[:, 0:width], MATMUL).astype(BF16)
+        src_ref[1:2, :] = sources[1]
 
 
 def models(observations, held):
@@ -206,27 +204,57 @@
         in_specs=[vmem] * 2,
         out_shape=(
             jax.ShapeDtypeStruct((width, lanes), BF16),
-            jax.ShapeDtypeStruct((width, width), BF16),
             jax.ShapeDtypeStruct((2, width), F32),
         ),
         scratch_shapes=[pltpu.VMEM((128, 2 * width), BF16)],
         input_output_aliases={1: 0},
         compiler_params=pltpu.CompilerParams(vmem_limit_bytes=16 << 20),
         cost_estimate=pl.CostEstimate(
-            flops=2 * width**3, bytes_accessed=8 * width * width, transcendentals=0
+            flops=512 * width**2, bytes_accessed=8 * width * width, transcendentals=0
         ),
         name="models",
     )(observations, held)
 
 
-def advance_kernel(block, both_ref, src_ref, x_ref, end0, kept0, end_ref, kept_ref):
-    mine = lax.axis_index("tm") == block
+def product_kernel(all_ref, src_ref, after_ref, both_ref, sum_ref):
+    del after_ref
+    width = all_ref.shape[0]
+    g = 2 * width
+
+    @pl.when(lax.axis_index("tm") > 1)
+    def _():
+        sum_ref[...] = step(all_ref[:, width:g], src_ref[0:1, :], src_ref[1:2, :])
+        for at in range(0, width, 256):
+            rows = all_ref[at : at + 256, width:g]
+            both_ref[at : at + 256, :] = dot(rows, all_ref[:, 0:width], MATMUL).astype(BF16)
+
+
+def product(held, sources, after):
+    width = held.shape[0]
+    return pl.pallas_call(
+        product_kernel,
+        in_specs=[pl.BlockSpec(memory_space=pltpu.VMEM)] * 3,
+        out_shape=(
+            jax.ShapeDtypeStruct((width, width), BF16),
+            jax.ShapeDtypeStruct((1, width), F32),
+        ),
+        compiler_params=pltpu.CompilerParams(vmem_limit_bytes=8 << 20),
+        cost_estimate=pl.CostEstimate(
+            flops=2 * width**3, bytes_accessed=6 * width * width, transcendentals=0
+        ),
+        name="product",
+    )(held, sources, after)
+
+
+def second_kernel(all_ref, src_ref, x_ref, end0, kept0, end_ref, kept_ref):
+    mine = lax.axis_index("tm") == 1
 
     @pl.when(mine)
     def _():
-        x = x_ref[...]
-        end_ref[...] = step(both_ref[...], x, src_ref[1:2, :])
-        kept_ref[...] = x
+        width = all_ref.shape[0]
+        u = step(all_ref[:, 0:width], x_ref[...], src_ref[0:1, :])
+        end_ref[...] = step(all_ref[:, width : 2 * width], u, src_ref[1:2, :])
+        kept_ref[...] = u
 
     @pl.when(jnp.logical_not(mine))
     def _():
@@ -234,7 +262,33 @@
         kept_ref[...] = kept0[...]
 
 
-def advance(block, both, sources, x, end, kept):
+def second(held, sources, x, end, kept):
+    row = jax.ShapeDtypeStruct(x.shape, F32)
+    return pl.pallas_call(
+        second_kernel,
+        in_specs=[pl.BlockSpec(memory_space=pltpu.VMEM)] * 5,
+        out_shape=(row, row),
+        compiler_params=pltpu.CompilerParams(vmem_limit_bytes=4 << 20),
+        name="second",
+    )(held, sources, x, end, kept)
+
+
+def advance_kernel(block, both_ref, sum_ref, x_ref, end0, kept0, end_ref, kept_ref):
+    mine = lax.axis_index("tm") == block
+
+    @pl.when(mine)
+    def _():
+        x = x_ref[...]
+        end_ref[...] = step(both_ref[...], x, sum_ref[...])
+        kept_ref[...] = x
+
+    @pl.when(jnp.logical_not(mine))
+    def _():
+        end_ref[...] = end0[...]
+        kept_ref[...] = kept0[...]
+
+
+def advance(block, both, sums, x, end, kept):
     row = jax.ShapeDtypeStruct(x.shape, F32)
     return pl.pallas_call(
         functools.partial(advance_kernel, block),
@@ -242,10 +296,10 @@
         out_shape=(row, row),
         compiler_params=pltpu.CompilerParams(vmem_limit_bytes=4 << 20),
         name="advance",
-    )(both, sources, x, end, kept)
-
-
-def finish_kernel(all_ref, both_ref, src_ref, x_ref, end_ref, kept_ref, means_ref, last_ref, held):
+    )(both, sums, x, end, kept)
+
+
+def finish_kernel(all_ref, both_ref, src_ref, sum_ref, x_ref, end_ref, kept_ref, means_ref, last_ref, held):
     rows, width = means_ref.shape[1], all_ref.shape[0]
     here = lax.axis_index("tm")
     held[0:1, :] = kept_ref[...]
@@ -254,9 +308,9 @@
     @pl.when(here == BLOCKS - 1)
     def _():
         held[0:1, :] = step(all_ref[:, 0:width], x_ref[...], src_ref[0:1, :])
-        held[1:2, :] = step(both_ref[...], x_ref[...], src_ref[1:2, :])
-
-    @pl.when(jnp.logical_and(here > 0, here < BLOCKS - 1))
+        held[1:2, :] = step(both_ref[...], x_ref[...], sum_ref[...])
+
+    @pl.when(jnp.logical_and(here > 1, here < BLOCKS - 1))
     def _():
         held[0:1, :] = step(all_ref[:, 0:width], kept_ref[...], src_ref[0:1, :])
 
@@ -265,10 +319,10 @@
     last_ref[...] = mine[1:2, 0:rows]
 
 
-def finish(held, both, sources, x, end, kept, rows):
+def finish(held, both, sources, sums, x, end, kept, rows):
     return pl.pallas_call(
         finish_kernel,
-        in_specs=[pl.BlockSpec(memory_space=pltpu.VMEM)] * 6,
+        in_specs=[pl.BlockSpec(memory_space=pltpu.VMEM)] * 7,
         out_shape=(
             jax.ShapeDtypeStruct((2, rows), F32),
             jax.ShapeDtypeStruct((1, rows), F32),
@@ -276,7 +330,7 @@
         scratch_shapes=[pltpu.VMEM((8, held.shape[0]), F32)],
         compiler_params=pltpu.CompilerParams(vmem_limit_bytes=4 << 20),
         name="finish",
-    )(held, both, sources, x, end, kept)
+    )(held, both, sources, sums, x, end, kept)
 
 
 def along(first, distance):
@@ -296,7 +350,7 @@
 def shards(transitions, gain, obs_op, observations, start):
     rows, width = transitions.shape[1], transitions.shape[2]
     mine = pack(transitions, gain, obs_op, start)
-    near = [mine] + [lax.ppermute(mine, "state", along(True, d)) for d in range(1, RING)]
+    near = [mine] + [lax.ppermute(mine, "state", along(True, d)) for d in NEAR[1:]]
     line = jnp.concatenate(near, axis=0)
     ahead = lax.ppermute(line, "state", along(False, 1))
     behind = lax.ppermute(line, "state", along(False, RING - 1))
@@ -312,13 +366,14 @@
     across = (across, lax.ppermute(across, "state", SWAP))
     held, end, kept = late(observations, across, held)
     x = lax.ppermute(end, "tm", [(0, 1)])
-    held, both, sources = models(observations, held)
-    end, kept = advance(1, both, sources, x, end, kept)
+    held, sources = models(observations, held)
+    end, kept = second(held, sources, x, end, kept)
+    both, sums = product(held, sources, end)
     for block in range(2, BLOCKS - 1):
         x = lax.ppermute(end, "tm", [(block - 1, block)])
-        end, kept = advance(block, both, sources, x, end, kept)
+        end, kept = advance(block, both, sums, x, end, kept)
     x = lax.ppermute(end, "tm", [(BLOCKS - 2, BLOCKS - 1)])
-    return finish(held, both, sources, x, end, kept, rows)
+    return finish(held, both, sources, sums, x, end, kept, rows)
 
 
 def solution(mesh):

time: 51.7 us -> 50.8 us (0.983)
  waiting for transfers between devices: 25.7 us -> 24.7 us
    pallas_call x0 -> x2, Pallas kernels: none -> 2.91 us  [the longest x1 2.89 us: product(): pl.pallas_call(product_kernel, in_specs=[pl.BlockSpec(memory_space=pltpu....]
    pallas_call x1, Pallas kernels: 4.78 us -> 2.03 us  [models(): pl.pallas_call(models_kernel, in_specs=[vmem] * 2, out_shape=(jax.ShapeDt...]
    ppermute x1, waiting for transfers between devices: 7.83 us -> 6.81 us  [shards(): x = lax.ppermute(end, 'tm', [(BLOCKS - 2, BLOCKS - 1)])]
  transfers between devices with their start and end apart: 14 -> 14, of which waited for: 7 -> 7; matrix products, arithmetic and copies ran while one was open for 0% -> 0% of each run, Pallas kernels for 10% -> 11%
where the time goes in v4:
time: 50.8 us; the launch traced here: 50.6 us
  waiting for transfers between devices  24.7 us (49%)
  starting transfers between devices  16.6 us (33%)
  Pallas kernels  8.37 us (16%)
  between operations  0.82 us (2%)
    ppermute x1, waiting for transfers between devices, shards(): ahead = lax.ppermute(line, 'state', along(False, 1))  8.13 us
    ppermute x1, waiting for transfers between devices, shards(): x = lax.ppermute(end, 'tm', [(BLOCKS - 2, BLOCKS - 1)])  6.81 us
    ppermute x3, starting transfers between devices, shards(): lax.ppermute(mine, 'state', along(True, d))  5.89 us
    ppermute x1, waiting for transfers between devices, shards(): lax.ppermute(ahead[:half], 'state', along(False, 1))  4.26 us
    ppermute x3, waiting for transfers between devices, shards(): lax.ppermute(mine, 'state', along(True, d))  3.88 us
    ppermute x1, starting transfers between devices, shards(): lax.ppermute(behind[half:], 'state', along(False, RING - 1))  3.19 us
    pallas_call x1, Pallas kernels, product(): pl.pallas_call(product_kernel, in_specs=[pl.BlockSpec(memory_space=pltpu....  2.89 us
    ppermute x1, starting transfers between devices, shards(): behind = lax.ppermute(line, 'state', along(False, RING - 1))  2.2 us
  transfers between devices with their start and end apart: 14, of which 7 were waited for; matrix products, arithmetic and copies ran while one was open for 0% of the time, Pallas kernels for 11%

profile of v4, /device:TPU:6, one launch (start us, length us, event | category | flops | bytes accessed | tf_op | source)
XLA Modules:
  0.0 50.6 jit_solution(9997233246581087255)
XLA Ops:
  0.6 0.9 %pack.1 = bf16[32,2432]{1,0:T(8,128)(2,1)S(1)} custom-call(bf16[2,32,1024]{2,1,0:T(8,128)(2,1)} %trans_ref.1, bf16[32,128]{1,0:T(8,128)(2,1)} %gain_ref.1, bf16[32,128]{1,0:T(8,128)(2,1)} %bitcast.2, f32[1,32]{1,0:T(1,128)} %bitcast.3), custom_call_target="tpu_custom_call" | custom-call | tf_op jit(solution)/shard_map/pack/pallas_call | solution.py:66
  1.6 1.6 %collective-permute-start.2 = (bf16[32,2432]{1,0:T(8,128)(2,1)S(1)}, bf16[32,2432]{1,0:T(8,128)(2,1)S(1)}, u32[]{:S(2)}, u32[]{:S(2)}) collective-permute-start(bf16[32,2432]{1,0:T(8,128)(2,1)S(1)} %pack.1), channel_id=1, source_target_pairs={{0,2},{1,9},{2,4},{3,11},{4,6},{5,13},{6,0},{7,15},{8,10},{9,17},{... | collective-permute-start | bytes 466952 | tf_op jit(solution)/shard_map/ppermute | solution.py:353
  3.2 2.9 %collective-permute-start.1 = (bf16[32,2432]{1,0:T(8,128)(2,1)S(1)}, bf16[32,2432]{1,0:T(8,128)(2,1)S(1)}, u32[]{:S(2)}, u32[]{:S(2)}) collective-permute-start(bf16[32,2432]{1,0:T(8,128)(2,1)S(1)} %pack.1), channel_id=1, source_target_pairs={{0,4},{1,17},{2,6},{3,19},{4,0},{5,21},{6,2},{7,23},{8,12},{9,25},... | collective-permute-start | bytes 466952 | tf_op jit(solution)/shard_map/ppermute | solution.py:353
  6.1 1.3 %collective-permute-start = (bf16[32,2432]{1,0:T(8,128)(2,1)S(1)}, bf16[32,2432]{1,0:T(8,128)(2,1)S(1)}, u32[]{:S(2)}, u32[]{:S(2)}) collective-permute-start(bf16[32,2432]{1,0:T(8,128)(2,1)S(1)} %pack.1), channel_id=1, source_target_pairs={{0,6},{1,25},{2,0},{3,27},{4,2},{5,29},{6,4},{7,31},{8,14},{9,1},{... | collective-permute-start | bytes 466952 | tf_op jit(solution)/shard_map/ppermute | solution.py:353
  7.5 0.6 %collective-permute-done.2 = bf16[32,2432]{1,0:T(8,128)(2,1)S(1)} collective-permute-done((bf16[32,2432]{1,0:T(8,128)(2,1)S(1)}, bf16[32,2432]{1,0:T(8,128)(2,1)S(1)}, u32[]{:S(2)}, u32[]{:S(2)}) %collective-permute-start.2) | collective-permute-done | bytes 155680 | tf_op jit(solution)/shard_map/ppermute | solution.py:353
  8.1 2.9 %collective-permute-done.1 = bf16[32,2432]{1,0:T(8,128)(2,1)S(1)} collective-permute-done((bf16[32,2432]{1,0:T(8,128)(2,1)S(1)}, bf16[32,2432]{1,0:T(8,128)(2,1)S(1)}, u32[]{:S(2)}, u32[]{:S(2)}) %collective-permute-start.1) | collective-permute-done | bytes 155680 | tf_op jit(solution)/shard_map/ppermute | solution.py:353
  11.0 0.4 collective-permute-done
  11.4 2.0 %collective-permute-start.3 = (bf16[128,2432]{1,0:T(8,128)(2,1)S(1)}, bf16[128,2432]{1,0:T(8,128)(2,1)S(1)}, u32[]{:S(2)}, u32[]{:S(2)}) collective-permute-start(bf16[128,2432]{1,0:T(8,128)(2,1)S(1)} %pad_maximum_fusion.refs_0_), channel_id=1, source_target_pairs={{0,8},{1,3},{2,10},{3,5},{4,12},{5,7},{6,14},{7,1},{8,16},{9,11},{... | collective-permute-start | bytes 1867784 | tf_op jit(solution)/shard_map/ppermute | solution.py:355
  13.4 2.2 %collective-permute-start.5 = (bf16[128,2432]{1,0:T(8,128)(2,1)S(1)}, bf16[128,2432]{1,0:T(8,128)(2,1)S(1)}, u32[]{:S(2)}, u32[]{:S(2)}) collective-permute-start(bf16[128,2432]{1,0:T(8,128)(2,1)S(1)} %pad_maximum_fusion.refs_0_), channel_id=1, source_target_pairs={{0,24},{1,7},{2,26},{3,1},{4,28},{5,3},{6,30},{7,5},{8,0},{9,15},{... | collective-permute-start | bytes 1867784 | tf_op jit(solution)/shard_map/ppermute | solution.py:356
  15.6 8.1 %collective-permute-done.3.refs_1_ = bf16[128,2432]{1,0:T(8,128)(2,1)S(1)} collective-permute-done((bf16[128,2432]{1,0:T(8,128)(2,1)S(1)}, bf16[128,2432]{1,0:T(8,128)(2,1)S(1)}, u32[]{:S(2)}, u32[]{:S(2)}) %collective-permute-start.3) | collective-permute-done | bytes 622624 | tf_op jit(solution)/shard_map/ppermute | solution.py:355
  23.7 0.1 collective-permute-start.4
  23.8 0.1 collective-permute-start.8
  23.9 0.0 collective-permute-done.5.refs_2_
  24.0 3.2 %collective-permute-start.6 = (bf16[64,2432]{1,0:T(8,128)(2,1)S(1)}, bf16[64,2432]{1,0:T(8,128)(2,1)S(1)}, u32[]{:S(2)}, u32[]{:S(2)}) collective-permute-start(bf16[64,2432]{1,0:T(8,128)(2,1)S(1)} %slice.9), channel_id=1, source_target_pairs={{0,24},{1,7},{2,26},{3,1},{4,28},{5,3},{6,30},{7,5},{8,0},{9,15},{... | collective-permute-start | bytes 933896 | tf_op jit(solution)/shard_map/ppermute | solution.py:360
  27.2 0.0 collective-permute-start.10
  27.2 0.5 %collective-permute-start.9 = (bf16[128,2432]{1,0:T(8,128)(2,1)S(1)}, bf16[128,2432]{1,0:T(8,128)(2,1)S(1)}, u32[]{:S(2)}, u32[]{:S(2)}) collective-permute-start(bf16[128,2432]{1,0:T(8,128)(2,1)S(1)} %collective-permute-done.3.refs_1_), channel_id=1, source_target_pairs={{0,1},{1,0},{2,3},{3,2},{4,5},{5,4},{6,7},{7,6},{8,9},{9,8},{10,11... | collective-permute-start | bytes 1867784 | tf_op jit(solution)/shard_map/ppermute | solution.py:364
  27.7 4.3 %collective-permute-done.4 = bf16[64,2432]{1,0:T(8,128)(2,1)S(1)} collective-permute-done((bf16[64,2432]{1,0:T(8,128)(2,1)S(1)}, bf16[64,2432]{1,0:T(8,128)(2,1)S(1)}, u32[]{:S(2)}, u32[]{:S(2)}) %collective-permute-start.4) | collective-permute-done | bytes 311328 | tf_op jit(solution)/shard_map/ppermute | solution.py:359
  32.0 0.0 collective-permute-done.6
  32.0 0.0 copy-start
  32.0 0.1 collective-permute-start.7
  32.1 0.0 collective-permute-done.8.refs_3_
  32.1 0.0 collective-permute-done.10.refs_5_
  32.1 0.0 collective-permute-done.9.refs_4_
  32.1 0.4 early.1.held_ref
  32.6 1.6 %collective-permute-done.7.part1 = bf16[128,2432]{1,0:T(8,128)(2,1)S(1)} collective-permute-done((bf16[128,2432]{1,0:T(8,128)(2,1)S(1)}, bf16[128,2432]{1,0:T(8,128)(2,1)S(1)}, u32[]{:S(2)}, u32[]{:S(2)}) %collective-permute-start.7) | collective-permute-done | bytes 622624 | tf_op jit(solution)/shard_map/ppermute | solution.py:366
  34.1 0.0 copy-done
  34.1 0.2 late.1
  34.3 0.7 %collective-permute-start.11 = (f32[1,1024]{1,0:T(1,128)S(1)}, f32[1,1024]{1,0:T(1,128)S(1)}, u32[]{:S(2)}, u32[]{:S(2)}) collective-permute-start(f32[1,1024]{1,0:T(1,128)S(1)} %get-tuple-element.16.end0), channel_id=1, source_target_pairs={{0,32},{1,33},{2,34},{3,35},{4,36},{5,37},{6,38},{7,39},{8,40},{9,... | collective-permute-start | bytes 12296 | tf_op jit(solution)/shard_map/ppermute | solution.py:368
  35.0 2.0 %models.1 = (bf16[1024,2432]{1,0:T(8,128)(2,1)S(1)}, f32[2,1024]{1,0:T(2,128)S(1)}) custom-call(f32[2,128]{1,0:T(2,128)S(1)} %copy-done, bf16[1024,2432]{1,0:T(8,128)(2,1)S(1)} %get-tuple-element.13.held_ref), custom_call_target="tpu_custom_call", output_to_operand_aliasing={{0}: (1, {})} | custom-call | flops 536870912 | bytes 8388608 | tf_op jit(solution)/shard_map/models/pallas_call | solution.py:202
  37.0 0.0 collective-permute-done.11.x_ref
  37.1 0.7 %collective-permute-start.12 = (f32[1,1024]{1,0:T(1,128)S(1)}, f32[1,1024]{1,0:T(1,128)S(1)}, u32[]{:S(2)}, u32[]{:S(2)}) collective-permute-start(f32[1,1024]{1,0:T(1,128)S(1)} %get-tuple-element.18.after_ref.end0), channel_id=1, source_target_pairs={{32,64},{33,65},{34,66},{35,67},{36,68},{37,69},{38,70},{39,71},{4... | collective-permute-start | bytes 12296 | tf_op jit(solution)/shard_map/ppermute | solution.py:373
  37.7 2.9 %product.1 = (bf16[1024,1024]{1,0:T(8,128)(2,1)S(1)}, f32[1,1024]{1,0:T(1,128)S(1)}) custom-call(bf16[1024,2432]{1,0:T(8,128)(2,1)S(1)} %get-tuple-element.14.all_ref, f32[2,1024]{1,0:T(2,128)S(1)} %get-tuple-element.15.src_ref, f32[1,1024]{1,0:T(1,128)S(1)} %get-tuple-element.18.after_ref.end0), custom_call_target="tpu_custom_call" | custom-call | flops 2147483648 | bytes 6291456 | tf_op jit(solution)/shard_map/product/pallas_call | solution.py:234
  40.6 0.0 collective-permute-done.12.x_ref
  40.7 1.3 %collective-permute-start.13 = (f32[1,1024]{1,0:T(1,128)S(1)}, f32[1,1024]{1,0:T(1,128)S(1)}, u32[]{:S(2)}, u32[]{:S(2)}) collective-permute-start(f32[1,1024]{1,0:T(1,128)S(1)} %get-tuple-element.22.end_ref), channel_id=1, source_target_pairs={{64,96},{65,97},{66,98},{67,99},{68,100},{69,101},{70,102},{71,103... | collective-permute-start | bytes 12296 | tf_op jit(solution)/shard_map/ppermute | solution.py:375
  42.0 6.8 %collective-permute-done.13.x_ref = f32[1,1024]{1,0:T(1,128)S(1)} collective-permute-done((f32[1,1024]{1,0:T(1,128)S(1)}, f32[1,1024]{1,0:T(1,128)S(1)}, u32[]{:S(2)}, u32[]{:S(2)}) %collective-permute-start.13) | collective-permute-done | bytes 4128 | tf_op jit(solution)/shard_map/ppermute | solution.py:375
  48.8 1.9 %finish.1 = (f32[2,32]{1,0:T(2,128)}, f32[1,32]{1,0:T(1,128)}) custom-call(bf16[1024,2432]{1,0:T(8,128)(2,1)S(1)} %get-tuple-element.14.all_ref, bf16[1024,1024]{1,0:T(8,128)(2,1)S(1)} %get-tuple-element.19.both_ref, f32[2,1024]{1,0:T(2,128)S(1)} %get-tuple-element.15.src_ref, f32[1,1024]{1,0:T(1,128)S(1)} %get-tuple-element.20.sum_ref, ...), custom_call_target="tpu_custom_call" | custom-call | tf_op jit(solution)/shard_map/finish/pallas_call | solution.py:323
  (7 shorter events, 0.2 us)
Async XLA Ops:
  1.6 6.5 %collective-permute-start.2 = (bf16[32,2432]{1,0:T(8,128)(2,1)S(1)}, bf16[32,2432]{1,0:T(8,128)(2,1)S(1)}, u32[]{:S(2)}, u32[]{:S(2)}) collective-permute-start(bf16[32,2432]{1,0:T(8,128)(2,1)S(1)} %pack.1), channel_id=1, source_target_pairs={{0,2},{1,9},{2,4},{3,11},{4,6},{5,13},{6,0},{7,15},{8,10},{9,17},{... | collective-permute-start | bytes 466952 | tf_op jit(solution)/shard_map/ppermute | solution.py:353
  3.2 7.8 %collective-permute-start.1 = (bf16[32,2432]{1,0:T(8,128)(2,1)S(1)}, bf16[32,2432]{1,0:T(8,128)(2,1)S(1)}, u32[]{:S(2)}, u32[]{:S(2)}) collective-permute-start(bf16[32,2432]{1,0:T(8,128)(2,1)S(1)} %pack.1), channel_id=1, source_target_pairs={{0,4},{1,17},{2,6},{3,19},{4,0},{5,21},{6,2},{7,23},{8,12},{9,25},... | collective-permute-start | bytes 466952 | tf_op jit(solution)/shard_map/ppermute | solution.py:353
  6.1 5.2 %collective-permute-start = (bf16[32,2432]{1,0:T(8,128)(2,1)S(1)}, bf16[32,2432]{1,0:T(8,128)(2,1)S(1)}, u32[]{:S(2)}, u32[]{:S(2)}) collective-permute-start(bf16[32,2432]{1,0:T(8,128)(2,1)S(1)} %pack.1), channel_id=1, source_target_pairs={{0,6},{1,25},{2,0},{3,27},{4,2},{5,29},{6,4},{7,31},{8,14},{9,1},{... | collective-permute-start | bytes 466952 | tf_op jit(solution)/shard_map/ppermute | solution.py:353
  11.4 12.3 %collective-permute-start.3 = (bf16[128,2432]{1,0:T(8,128)(2,1)S(1)}, bf16[128,2432]{1,0:T(8,128)(2,1)S(1)}, u32[]{:S(2)}, u32[]{:S(2)}) collective-permute-start(bf16[128,2432]{1,0:T(8,128)(2,1)S(1)} %pad_maximum_fusion.refs_0_), channel_id=1, source_target_pairs={{0,8},{1,3},{2,10},{3,5},{4,12},{5,7},{6,14},{7,1},{8,16},{9,11},{... | collective-permute-start | bytes 1867784 | tf_op jit(solution)/shard_map/ppermute | solution.py:355
  13.4 10.5 %collective-permute-start.5 = (bf16[128,2432]{1,0:T(8,128)(2,1)S(1)}, bf16[128,2432]{1,0:T(8,128)(2,1)S(1)}, u32[]{:S(2)}, u32[]{:S(2)}) collective-permute-start(bf16[128,2432]{1,0:T(8,128)(2,1)S(1)} %pad_maximum_fusion.refs_0_), channel_id=1, source_target_pairs={{0,24},{1,7},{2,26},{3,1},{4,28},{5,3},{6,30},{7,5},{8,0},{9,15},{... | collective-permute-start | bytes 1867784 | tf_op jit(solution)/shard_map/ppermute | solution.py:356
  23.7 8.2 %collective-permute-start.4 = (bf16[64,2432]{1,0:T(8,128)(2,1)S(1)}, bf16[64,2432]{1,0:T(8,128)(2,1)S(1)}, u32[]{:S(2)}, u32[]{:S(2)}) collective-permute-start(bf16[64,2432]{1,0:T(8,128)(2,1)S(1)} %slice.8), channel_id=1, source_target_pairs={{0,8},{1,3},{2,10},{3,5},{4,12},{5,7},{6,14},{7,1},{8,16},{9,11},{... | collective-permute-start | bytes 933896 | tf_op jit(solution)/shard_map/ppermute | solution.py:359
  23.8 8.3 %collective-permute-start.8 = (bf16[128,2432]{1,0:T(8,128)(2,1)S(1)}, bf16[128,2432]{1,0:T(8,128)(2,1)S(1)}, u32[]{:S(2)}, u32[]{:S(2)}) collective-permute-start(bf16[128,2432]{1,0:T(8,128)(2,1)S(1)} %pad_maximum_fusion.refs_0_), channel_id=1, source_target_pairs={{0,1},{1,0},{2,3},{3,2},{4,5},{5,4},{6,7},{7,6},{8,9},{9,8},{10,11... | collective-permute-start | bytes 1867784 | tf_op jit(solution)/shard_map/ppermute | solution.py:364
  24.0 8.0 %collective-permute-start.6 = (bf16[64,2432]{1,0:T(8,128)(2,1)S(1)}, bf16[64,2432]{1,0:T(8,128)(2,1)S(1)}, u32[]{:S(2)}, u32[]{:S(2)}) collective-permute-start(bf16[64,2432]{1,0:T(8,128)(2,1)S(1)} %slice.9), channel_id=1, source_target_pairs={{0,24},{1,7},{2,26},{3,1},{4,28},{5,3},{6,30},{7,5},{8,0},{9,15},{... | collective-permute-start | bytes 933896 | tf_op jit(solution)/shard_map/ppermute | solution.py:360
  27.2 5.0 %collective-permute-start.10 = (bf16[128,2432]{1,0:T(8,128)(2,1)S(1)}, bf16[128,2432]{1,0:T(8,128)(2,1)S(1)}, u32[]{:S(2)}, u32[]{:S(2)}) collective-permute-start(bf16[128,2432]{1,0:T(8,128)(2,1)S(1)} %collective-permute-done.5.refs_2_), channel_id=1, source_target_pairs={{0,1},{1,0},{2,3},{3,2},{4,5},{5,4},{6,7},{7,6},{8,9},{9,8},{10,11... | collective-permute-start | bytes 1867784 | tf_op jit(solution)/shard_map/ppermute | solution.py:364
  27.2 5.0 %collective-permute-start.9 = (bf16[128,2432]{1,0:T(8,128)(2,1)S(1)}, bf16[128,2432]{1,0:T(8,128)(2,1)S(1)}, u32[]{:S(2)}, u32[]{:S(2)}) collective-permute-start(bf16[128,2432]{1,0:T(8,128)(2,1)S(1)} %collective-permute-done.3.refs_1_), channel_id=1, source_target_pairs={{0,1},{1,0},{2,3},{3,2},{4,5},{5,4},{6,7},{7,6},{8,9},{9,8},{10,11... | collective-permute-start | bytes 1867784 | tf_op jit(solution)/shard_map/ppermute | solution.py:364
  32.0 2.1 %copy-start = (f32[2,128]{1,0:T(2,128)S(1)}, f32[2,128]{1,0:T(2,128)}, u32[]{:S(2)}) copy-start(f32[2,128]{1,0:T(2,128)} %obs_ref.3) | copy-start | bytes 3076
  32.0 2.1 %collective-permute-start.7 = (bf16[128,2432]{1,0:T(8,128)(2,1)S(1)}, bf16[128,2432]{1,0:T(8,128)(2,1)S(1)}, u32[]{:S(2)}, u32[]{:S(2)}) collective-permute-start(bf16[128,2432]{1,0:T(8,128)(2,1)S(1)} %constant_dynamic-update-slice_fusion.part0), channel_id=1, source_target_pairs={{0,1},{1,0},{2,3},{3,2},{4,5},{5,4},{6,7},{7,6},{8,9},{9,8},{10,11... | collective-permute-start | bytes 1867784 | tf_op jit(solution)/shard_map/ppermute | solution.py:366
  34.3 2.7 %collective-permute-start.11 = (f32[1,1024]{1,0:T(1,128)S(1)}, f32[1,1024]{1,0:T(1,128)S(1)}, u32[]{:S(2)}, u32[]{:S(2)}) collective-permute-start(f32[1,1024]{1,0:T(1,128)S(1)} %get-tuple-element.16.end0), channel_id=1, source_target_pairs={{0,32},{1,33},{2,34},{3,35},{4,36},{5,37},{6,38},{7,39},{8,40},{9,... | collective-permute-start | bytes 12296 | tf_op jit(solution)/shard_map/ppermute | solution.py:368
  37.1 3.6 %collective-permute-start.12 = (f32[1,1024]{1,0:T(1,128)S(1)}, f32[1,1024]{1,0:T(1,128)S(1)}, u32[]{:S(2)}, u32[]{:S(2)}) collective-permute-start(f32[1,1024]{1,0:T(1,128)S(1)} %get-tuple-element.18.after_ref.end0), channel_id=1, source_target_pairs={{32,64},{33,65},{34,66},{35,67},{36,68},{37,69},{38,70},{39,71},{4... | collective-permute-start | bytes 12296 | tf_op jit(solution)/shard_map/ppermute | solution.py:373
  40.7 8.1 %collective-permute-start.13 = (f32[1,1024]{1,0:T(1,128)S(1)}, f32[1,1024]{1,0:T(1,128)S(1)}, u32[]{:S(2)}, u32[]{:S(2)}) collective-permute-start(f32[1,1024]{1,0:T(1,128)S(1)} %get-tuple-element.22.end_ref), channel_id=1, source_target_pairs={{64,96},{65,97},{66,98},{67,99},{68,100},{69,101},{70,102},{71,103... | collective-permute-start | bytes 12296 | tf_op jit(solution)/shard_map/ppermute | solution.py:375

commit v5 on v4

--- a/solution.py
+++ b/solution.py
@@ -107,10 +107,6 @@
             out_ref[pl.ds(at, rows), :] = part[j * rows : (j + 1) * rows, :]
 
 
-def lanes_shift(rows, width):
-    return lax.rem(width - rows * lax.axis_index("state"), width)
-
-
 def early_kernel(*refs):
     put_rows(refs[:-1], EARLY, refs[-1])
 
@@ -314,7 +310,10 @@
     def _():
         held[0:1, :] = step(all_ref[:, 0:width], kept_ref[...], src_ref[0:1, :])
 
-    mine = pltpu.roll(held[...], lanes_shift(rows, width), 1)
+    offset = rows * lax.axis_index("state")
+    inside = lax.rem(offset, 128)
+    lanes = held[:, pl.ds(pl.multiple_of(offset - inside, 128), 128)]
+    mine = pltpu.roll(lanes, lax.rem(128 - inside, 128), 1)
     means_ref[...] = mine[0:2, 0:rows]
     last_ref[...] = mine[1:2, 0:rows]
 

time: 50.8 us -> 50.8 us (level)
  no operation moved by 1% of the time
where the time goes in v5:
time: 50.8 us; the launch traced here: 50.6 us
  waiting for transfers between devices  24.7 us (49%)
  starting transfers between devices  16.6 us (33%)
  Pallas kernels  8.36 us (16%)
  between operations  0.82 us (2%)
    ppermute x1, waiting for transfers between devices, shards(): ahead = lax.ppermute(line, 'state', along(False, 1))  8.13 us
    ppermute x1, waiting for transfers between devices, shards(): x = lax.ppermute(end, 'tm', [(BLOCKS - 2, BLOCKS - 1)])  6.81 us
    ppermute x3, starting transfers between devices, shards(): lax.ppermute(mine, 'state', along(True, d))  5.89 us
    ppermute x1, waiting for transfers between devices, shards(): lax.ppermute(ahead[:half], 'state', along(False, 1))  4.26 us
    ppermute x3, waiting for transfers between devices, shards(): lax.ppermute(mine, 'state', along(True, d))  3.88 us
    ppermute x1, starting transfers between devices, shards(): lax.ppermute(behind[half:], 'state', along(False, RING - 1))  3.19 us
    pallas_call x1, Pallas kernels, product(): pl.pallas_call(product_kernel, in_specs=[pl.BlockSpec(memory_space=pltpu....  2.89 us
    ppermute x1, starting transfers between devices, shards(): behind = lax.ppermute(line, 'state', along(False, RING - 1))  2.2 us
  transfers between devices with their start and end apart: 14, of which 7 were waited for; matrix products, arithmetic and copies ran while one was open for 0% of the time, Pallas kernels for 11%

profile of v5, /device:TPU:6, one launch (start us, length us, event | category | flops | bytes accessed | tf_op | source)
XLA Modules:
  0.0 50.6 jit_solution(15891902706068497423)
XLA Ops:
  0.6 0.9 %pack.1 = bf16[32,2432]{1,0:T(8,128)(2,1)S(1)} custom-call(bf16[2,32,1024]{2,1,0:T(8,128)(2,1)} %trans_ref.1, bf16[32,128]{1,0:T(8,128)(2,1)} %gain_ref.1, bf16[32,128]{1,0:T(8,128)(2,1)} %bitcast.2, f32[1,32]{1,0:T(1,128)} %bitcast.3), custom_call_target="tpu_custom_call" | custom-call | tf_op jit(solution)/shard_map/pack/pallas_call | solution.py:66
  1.6 1.6 %collective-permute-start.2 = (bf16[32,2432]{1,0:T(8,128)(2,1)S(1)}, bf16[32,2432]{1,0:T(8,128)(2,1)S(1)}, u32[]{:S(2)}, u32[]{:S(2)}) collective-permute-start(bf16[32,2432]{1,0:T(8,128)(2,1)S(1)} %pack.1), channel_id=1, source_target_pairs={{0,2},{1,9},{2,4},{3,11},{4,6},{5,13},{6,0},{7,15},{8,10},{9,17},{... | collective-permute-start | bytes 466952 | tf_op jit(solution)/shard_map/ppermute | solution.py:352
  3.2 2.9 %collective-permute-start.1 = (bf16[32,2432]{1,0:T(8,128)(2,1)S(1)}, bf16[32,2432]{1,0:T(8,128)(2,1)S(1)}, u32[]{:S(2)}, u32[]{:S(2)}) collective-permute-start(bf16[32,2432]{1,0:T(8,128)(2,1)S(1)} %pack.1), channel_id=1, source_target_pairs={{0,4},{1,17},{2,6},{3,19},{4,0},{5,21},{6,2},{7,23},{8,12},{9,25},... | collective-permute-start | bytes 466952 | tf_op jit(solution)/shard_map/ppermute | solution.py:352
  6.1 1.3 %collective-permute-start = (bf16[32,2432]{1,0:T(8,128)(2,1)S(1)}, bf16[32,2432]{1,0:T(8,128)(2,1)S(1)}, u32[]{:S(2)}, u32[]{:S(2)}) collective-permute-start(bf16[32,2432]{1,0:T(8,128)(2,1)S(1)} %pack.1), channel_id=1, source_target_pairs={{0,6},{1,25},{2,0},{3,27},{4,2},{5,29},{6,4},{7,31},{8,14},{9,1},{... | collective-permute-start | bytes 466952 | tf_op jit(solution)/shard_map/ppermute | solution.py:352
  7.5 0.6 %collective-permute-done.2 = bf16[32,2432]{1,0:T(8,128)(2,1)S(1)} collective-permute-done((bf16[32,2432]{1,0:T(8,128)(2,1)S(1)}, bf16[32,2432]{1,0:T(8,128)(2,1)S(1)}, u32[]{:S(2)}, u32[]{:S(2)}) %collective-permute-start.2) | collective-permute-done | bytes 155680 | tf_op jit(solution)/shard_map/ppermute | solution.py:352
  8.1 2.9 %collective-permute-done.1 = bf16[32,2432]{1,0:T(8,128)(2,1)S(1)} collective-permute-done((bf16[32,2432]{1,0:T(8,128)(2,1)S(1)}, bf16[32,2432]{1,0:T(8,128)(2,1)S(1)}, u32[]{:S(2)}, u32[]{:S(2)}) %collective-permute-start.1) | collective-permute-done | bytes 155680 | tf_op jit(solution)/shard_map/ppermute | solution.py:352
  11.0 0.4 collective-permute-done
  11.4 2.0 %collective-permute-start.3 = (bf16[128,2432]{1,0:T(8,128)(2,1)S(1)}, bf16[128,2432]{1,0:T(8,128)(2,1)S(1)}, u32[]{:S(2)}, u32[]{:S(2)}) collective-permute-start(bf16[128,2432]{1,0:T(8,128)(2,1)S(1)} %pad_maximum_fusion.refs_0_), channel_id=1, source_target_pairs={{0,8},{1,3},{2,10},{3,5},{4,12},{5,7},{6,14},{7,1},{8,16},{9,11},{... | collective-permute-start | bytes 1867784 | tf_op jit(solution)/shard_map/ppermute | solution.py:354
  13.4 2.2 %collective-permute-start.5 = (bf16[128,2432]{1,0:T(8,128)(2,1)S(1)}, bf16[128,2432]{1,0:T(8,128)(2,1)S(1)}, u32[]{:S(2)}, u32[]{:S(2)}) collective-permute-start(bf16[128,2432]{1,0:T(8,128)(2,1)S(1)} %pad_maximum_fusion.refs_0_), channel_id=1, source_target_pairs={{0,24},{1,7},{2,26},{3,1},{4,28},{5,3},{6,30},{7,5},{8,0},{9,15},{... | collective-permute-start | bytes 1867784 | tf_op jit(solution)/shard_map/ppermute | solution.py:355
  15.6 8.1 %collective-permute-done.3.refs_1_ = bf16[128,2432]{1,0:T(8,128)(2,1)S(1)} collective-permute-done((bf16[128,2432]{1,0:T(8,128)(2,1)S(1)}, bf16[128,2432]{1,0:T(8,128)(2,1)S(1)}, u32[]{:S(2)}, u32[]{:S(2)}) %collective-permute-start.3) | collective-permute-done | bytes 622624 | tf_op jit(solution)/shard_map/ppermute | solution.py:354
  23.7 0.1 collective-permute-start.4
  23.8 0.1 collective-permute-start.8
  23.9 0.0 collective-permute-done.5.refs_2_
  24.0 3.2 %collective-permute-start.6 = (bf16[64,2432]{1,0:T(8,128)(2,1)S(1)}, bf16[64,2432]{1,0:T(8,128)(2,1)S(1)}, u32[]{:S(2)}, u32[]{:S(2)}) collective-permute-start(bf16[64,2432]{1,0:T(8,128)(2,1)S(1)} %slice.9), channel_id=1, source_target_pairs={{0,24},{1,7},{2,26},{3,1},{4,28},{5,3},{6,30},{7,5},{8,0},{9,15},{... | collective-permute-start | bytes 933896 | tf_op jit(solution)/shard_map/ppermute | solution.py:359
  27.2 0.0 collective-permute-start.10
  27.2 0.5 %collective-permute-start.9 = (bf16[128,2432]{1,0:T(8,128)(2,1)S(1)}, bf16[128,2432]{1,0:T(8,128)(2,1)S(1)}, u32[]{:S(2)}, u32[]{:S(2)}) collective-permute-start(bf16[128,2432]{1,0:T(8,128)(2,1)S(1)} %collective-permute-done.3.refs_1_), channel_id=1, source_target_pairs={{0,1},{1,0},{2,3},{3,2},{4,5},{5,4},{6,7},{7,6},{8,9},{9,8},{10,11... | collective-permute-start | bytes 1867784 | tf_op jit(solution)/shard_map/ppermute | solution.py:363
  27.7 4.3 %collective-permute-done.4 = bf16[64,2432]{1,0:T(8,128)(2,1)S(1)} collective-permute-done((bf16[64,2432]{1,0:T(8,128)(2,1)S(1)}, bf16[64,2432]{1,0:T(8,128)(2,1)S(1)}, u32[]{:S(2)}, u32[]{:S(2)}) %collective-permute-start.4) | collective-permute-done | bytes 311328 | tf_op jit(solution)/shard_map/ppermute | solution.py:358
  32.0 0.0 collective-permute-done.6
  32.0 0.0 copy-start
  32.0 0.1 collective-permute-start.7
  32.1 0.0 collective-permute-done.8.refs_3_
  32.1 0.0 collective-permute-done.10.refs_5_
  32.1 0.0 collective-permute-done.9.refs_4_
  32.1 0.4 early.1.held_ref
  32.6 1.6 %collective-permute-done.7.part1 = bf16[128,2432]{1,0:T(8,128)(2,1)S(1)} collective-permute-done((bf16[128,2432]{1,0:T(8,128)(2,1)S(1)}, bf16[128,2432]{1,0:T(8,128)(2,1)S(1)}, u32[]{:S(2)}, u32[]{:S(2)}) %collective-permute-start.7) | collective-permute-done | bytes 622624 | tf_op jit(solution)/shard_map/ppermute | solution.py:365
  34.1 0.0 copy-done
  34.1 0.2 late.1
  34.3 0.7 %collective-permute-start.11 = (f32[1,1024]{1,0:T(1,128)S(1)}, f32[1,1024]{1,0:T(1,128)S(1)}, u32[]{:S(2)}, u32[]{:S(2)}) collective-permute-start(f32[1,1024]{1,0:T(1,128)S(1)} %get-tuple-element.16.end0), channel_id=1, source_target_pairs={{0,32},{1,33},{2,34},{3,35},{4,36},{5,37},{6,38},{7,39},{8,40},{9,... | collective-permute-start | bytes 12296 | tf_op jit(solution)/shard_map/ppermute | solution.py:367
  35.0 2.0 %models.1 = (bf16[1024,2432]{1,0:T(8,128)(2,1)S(1)}, f32[2,1024]{1,0:T(2,128)S(1)}) custom-call(f32[2,128]{1,0:T(2,128)S(1)} %copy-done, bf16[1024,2432]{1,0:T(8,128)(2,1)S(1)} %get-tuple-element.13.held_ref), custom_call_target="tpu_custom_call", output_to_operand_aliasing={{0}: (1, {})} | custom-call | flops 536870912 | bytes 8388608 | tf_op jit(solution)/shard_map/models/pallas_call | solution.py:198
  37.0 0.0 collective-permute-done.11.x_ref
  37.1 0.7 %collective-permute-start.12 = (f32[1,1024]{1,0:T(1,128)S(1)}, f32[1,1024]{1,0:T(1,128)S(1)}, u32[]{:S(2)}, u32[]{:S(2)}) collective-permute-start(f32[1,1024]{1,0:T(1,128)S(1)} %get-tuple-element.18.after_ref.end0), channel_id=1, source_target_pairs={{32,64},{33,65},{34,66},{35,67},{36,68},{37,69},{38,70},{39,71},{4... | collective-permute-start | bytes 12296 | tf_op jit(solution)/shard_map/ppermute | solution.py:372
  37.7 2.9 %product.1 = (bf16[1024,1024]{1,0:T(8,128)(2,1)S(1)}, f32[1,1024]{1,0:T(1,128)S(1)}) custom-call(bf16[1024,2432]{1,0:T(8,128)(2,1)S(1)} %get-tuple-element.14.all_ref, f32[2,1024]{1,0:T(2,128)S(1)} %get-tuple-element.15.src_ref, f32[1,1024]{1,0:T(1,128)S(1)} %get-tuple-element.18.after_ref.end0), custom_call_target="tpu_custom_call" | custom-call | flops 2147483648 | bytes 6291456 | tf_op jit(solution)/shard_map/product/pallas_call | solution.py:230
  40.6 0.0 collective-permute-done.12.x_ref
  40.7 1.3 %collective-permute-start.13 = (f32[1,1024]{1,0:T(1,128)S(1)}, f32[1,1024]{1,0:T(1,128)S(1)}, u32[]{:S(2)}, u32[]{:S(2)}) collective-permute-start(f32[1,1024]{1,0:T(1,128)S(1)} %get-tuple-element.22.end_ref), channel_id=1, source_target_pairs={{64,96},{65,97},{66,98},{67,99},{68,100},{69,101},{70,102},{71,103... | collective-permute-start | bytes 12296 | tf_op jit(solution)/shard_map/ppermute | solution.py:374
  42.0 6.8 %collective-permute-done.13.x_ref = f32[1,1024]{1,0:T(1,128)S(1)} collective-permute-done((f32[1,1024]{1,0:T(1,128)S(1)}, f32[1,1024]{1,0:T(1,128)S(1)}, u32[]{:S(2)}, u32[]{:S(2)}) %collective-permute-start.13) | collective-permute-done | bytes 4128 | tf_op jit(solution)/shard_map/ppermute | solution.py:374
  48.8 1.8 %finish.1 = (f32[2,32]{1,0:T(2,128)}, f32[1,32]{1,0:T(1,128)}) custom-call(bf16[1024,2432]{1,0:T(8,128)(2,1)S(1)} %get-tuple-element.14.all_ref, bf16[1024,1024]{1,0:T(8,128)(2,1)S(1)} %get-tuple-element.19.both_ref, f32[2,1024]{1,0:T(2,128)S(1)} %get-tuple-element.15.src_ref, f32[1,1024]{1,0:T(1,128)S(1)} %get-tuple-element.20.sum_ref, ...), custom_call_target="tpu_custom_call" | custom-call | tf_op jit(solution)/shard_map/finish/pallas_call | solution.py:322
  (7 shorter events, 0.2 us)
Async XLA Ops:
  1.6 6.5 %collective-permute-start.2 = (bf16[32,2432]{1,0:T(8,128)(2,1)S(1)}, bf16[32,2432]{1,0:T(8,128)(2,1)S(1)}, u32[]{:S(2)}, u32[]{:S(2)}) collective-permute-start(bf16[32,2432]{1,0:T(8,128)(2,1)S(1)} %pack.1), channel_id=1, source_target_pairs={{0,2},{1,9},{2,4},{3,11},{4,6},{5,13},{6,0},{7,15},{8,10},{9,17},{... | collective-permute-start | bytes 466952 | tf_op jit(solution)/shard_map/ppermute | solution.py:352
  3.2 7.8 %collective-permute-start.1 = (bf16[32,2432]{1,0:T(8,128)(2,1)S(1)}, bf16[32,2432]{1,0:T(8,128)(2,1)S(1)}, u32[]{:S(2)}, u32[]{:S(2)}) collective-permute-start(bf16[32,2432]{1,0:T(8,128)(2,1)S(1)} %pack.1), channel_id=1, source_target_pairs={{0,4},{1,17},{2,6},{3,19},{4,0},{5,21},{6,2},{7,23},{8,12},{9,25},... | collective-permute-start | bytes 466952 | tf_op jit(solution)/shard_map/ppermute | solution.py:352
  6.1 5.2 %collective-permute-start = (bf16[32,2432]{1,0:T(8,128)(2,1)S(1)}, bf16[32,2432]{1,0:T(8,128)(2,1)S(1)}, u32[]{:S(2)}, u32[]{:S(2)}) collective-permute-start(bf16[32,2432]{1,0:T(8,128)(2,1)S(1)} %pack.1), channel_id=1, source_target_pairs={{0,6},{1,25},{2,0},{3,27},{4,2},{5,29},{6,4},{7,31},{8,14},{9,1},{... | collective-permute-start | bytes 466952 | tf_op jit(solution)/shard_map/ppermute | solution.py:352
  11.4 12.3 %collective-permute-start.3 = (bf16[128,2432]{1,0:T(8,128)(2,1)S(1)}, bf16[128,2432]{1,0:T(8,128)(2,1)S(1)}, u32[]{:S(2)}, u32[]{:S(2)}) collective-permute-start(bf16[128,2432]{1,0:T(8,128)(2,1)S(1)} %pad_maximum_fusion.refs_0_), channel_id=1, source_target_pairs={{0,8},{1,3},{2,10},{3,5},{4,12},{5,7},{6,14},{7,1},{8,16},{9,11},{... | collective-permute-start | bytes 1867784 | tf_op jit(solution)/shard_map/ppermute | solution.py:354
  13.4 10.5 %collective-permute-start.5 = (bf16[128,2432]{1,0:T(8,128)(2,1)S(1)}, bf16[128,2432]{1,0:T(8,128)(2,1)S(1)}, u32[]{:S(2)}, u32[]{:S(2)}) collective-permute-start(bf16[128,2432]{1,0:T(8,128)(2,1)S(1)} %pad_maximum_fusion.refs_0_), channel_id=1, source_target_pairs={{0,24},{1,7},{2,26},{3,1},{4,28},{5,3},{6,30},{7,5},{8,0},{9,15},{... | collective-permute-start | bytes 1867784 | tf_op jit(solution)/shard_map/ppermute | solution.py:355
  23.7 8.2 %collective-permute-start.4 = (bf16[64,2432]{1,0:T(8,128)(2,1)S(1)}, bf16[64,2432]{1,0:T(8,128)(2,1)S(1)}, u32[]{:S(2)}, u32[]{:S(2)}) collective-permute-start(bf16[64,2432]{1,0:T(8,128)(2,1)S(1)} %slice.8), channel_id=1, source_target_pairs={{0,8},{1,3},{2,10},{3,5},{4,12},{5,7},{6,14},{7,1},{8,16},{9,11},{... | collective-permute-start | bytes 933896 | tf_op jit(solution)/shard_map/ppermute | solution.py:358
  23.8 8.3 %collective-permute-start.8 = (bf16[128,2432]{1,0:T(8,128)(2,1)S(1)}, bf16[128,2432]{1,0:T(8,128)(2,1)S(1)}, u32[]{:S(2)}, u32[]{:S(2)}) collective-permute-start(bf16[128,2432]{1,0:T(8,128)(2,1)S(1)} %pad_maximum_fusion.refs_0_), channel_id=1, source_target_pairs={{0,1},{1,0},{2,3},{3,2},{4,5},{5,4},{6,7},{7,6},{8,9},{9,8},{10,11... | collective-permute-start | bytes 1867784 | tf_op jit(solution)/shard_map/ppermute | solution.py:363
  24.0 8.0 %collective-permute-start.6 = (bf16[64,2432]{1,0:T(8,128)(2,1)S(1)}, bf16[64,2432]{1,0:T(8,128)(2,1)S(1)}, u32[]{:S(2)}, u32[]{:S(2)}) collective-permute-start(bf16[64,2432]{1,0:T(8,128)(2,1)S(1)} %slice.9), channel_id=1, source_target_pairs={{0,24},{1,7},{2,26},{3,1},{4,28},{5,3},{6,30},{7,5},{8,0},{9,15},{... | collective-permute-start | bytes 933896 | tf_op jit(solution)/shard_map/ppermute | solution.py:359
  27.2 5.0 %collective-permute-start.10 = (bf16[128,2432]{1,0:T(8,128)(2,1)S(1)}, bf16[128,2432]{1,0:T(8,128)(2,1)S(1)}, u32[]{:S(2)}, u32[]{:S(2)}) collective-permute-start(bf16[128,2432]{1,0:T(8,128)(2,1)S(1)} %collective-permute-done.5.refs_2_), channel_id=1, source_target_pairs={{0,1},{1,0},{2,3},{3,2},{4,5},{5,4},{6,7},{7,6},{8,9},{9,8},{10,11... | collective-permute-start | bytes 1867784 | tf_op jit(solution)/shard_map/ppermute | solution.py:363
  27.2 5.0 %collective-permute-start.9 = (bf16[128,2432]{1,0:T(8,128)(2,1)S(1)}, bf16[128,2432]{1,0:T(8,128)(2,1)S(1)}, u32[]{:S(2)}, u32[]{:S(2)}) collective-permute-start(bf16[128,2432]{1,0:T(8,128)(2,1)S(1)} %collective-permute-done.3.refs_1_), channel_id=1, source_target_pairs={{0,1},{1,0},{2,3},{3,2},{4,5},{5,4},{6,7},{7,6},{8,9},{9,8},{10,11... | collective-permute-start | bytes 1867784 | tf_op jit(solution)/shard_map/ppermute | solution.py:363
  32.0 2.1 %copy-start = (f32[2,128]{1,0:T(2,128)S(1)}, f32[2,128]{1,0:T(2,128)}, u32[]{:S(2)}) copy-start(f32[2,128]{1,0:T(2,128)} %obs_ref.3) | copy-start | bytes 3076
  32.0 2.1 %collective-permute-start.7 = (bf16[128,2432]{1,0:T(8,128)(2,1)S(1)}, bf16[128,2432]{1,0:T(8,128)(2,1)S(1)}, u32[]{:S(2)}, u32[]{:S(2)}) collective-permute-start(bf16[128,2432]{1,0:T(8,128)(2,1)S(1)} %constant_dynamic-update-slice_fusion.part0), channel_id=1, source_target_pairs={{0,1},{1,0},{2,3},{3,2},{4,5},{5,4},{6,7},{7,6},{8,9},{9,8},{10,11... | collective-permute-start | bytes 1867784 | tf_op jit(solution)/shard_map/ppermute | solution.py:365
  34.3 2.7 %collective-permute-start.11 = (f32[1,1024]{1,0:T(1,128)S(1)}, f32[1,1024]{1,0:T(1,128)S(1)}, u32[]{:S(2)}, u32[]{:S(2)}) collective-permute-start(f32[1,1024]{1,0:T(1,128)S(1)} %get-tuple-element.16.end0), channel_id=1, source_target_pairs={{0,32},{1,33},{2,34},{3,35},{4,36},{5,37},{6,38},{7,39},{8,40},{9,... | collective-permute-start | bytes 12296 | tf_op jit(solution)/shard_map/ppermute | solution.py:367
  37.1 3.6 %collective-permute-start.12 = (f32[1,1024]{1,0:T(1,128)S(1)}, f32[1,1024]{1,0:T(1,128)S(1)}, u32[]{:S(2)}, u32[]{:S(2)}) collective-permute-start(f32[1,1024]{1,0:T(1,128)S(1)} %get-tuple-element.18.after_ref.end0), channel_id=1, source_target_pairs={{32,64},{33,65},{34,66},{35,67},{36,68},{37,69},{38,70},{39,71},{4... | collective-permute-start | bytes 12296 | tf_op jit(solution)/shard_map/ppermute | solution.py:372
  40.7 8.1 %collective-permute-start.13 = (f32[1,1024]{1,0:T(1,128)S(1)}, f32[1,1024]{1,0:T(1,128)S(1)}, u32[]{:S(2)}, u32[]{:S(2)}) collective-permute-start(f32[1,1024]{1,0:T(1,128)S(1)} %get-tuple-element.22.end_ref), channel_id=1, source_target_pairs={{64,96},{65,97},{66,98},{67,99},{68,100},{69,101},{70,102},{71,103... | collective-permute-start | bytes 12296 | tf_op jit(solution)/shard_map/ppermute | solution.py:374

commit v6 on v4

--- a/solution.py
+++ b/solution.py
@@ -81,7 +81,7 @@
     return ((z % RING) * RING + y % RING) * 2 + core
 
 
-NEAR = (0, 3, 2, 1)
+NEAR = (3, 0, 2, 1)
 EARLY, LATE = (0, 1, RING - 1), (2,)
 
 
@@ -350,7 +350,7 @@
 def shards(transitions, gain, obs_op, observations, start):
     rows, width = transitions.shape[1], transitions.shape[2]
     mine = pack(transitions, gain, obs_op, start)
-    near = [mine] + [lax.ppermute(mine, "state", along(True, d)) for d in NEAR[1:]]
+    near = [mine if d == 0 else lax.ppermute(mine, "state", along(True, d)) for d in NEAR]
     line = jnp.concatenate(near, axis=0)
     ahead = lax.ppermute(line, "state", along(False, 1))
     behind = lax.ppermute(line, "state", along(False, RING - 1))

time: 50.8 us -> 50.8 us (level)
  no operation moved by 1% of the time
where the time goes in v6:
time: 50.8 us; the launch traced here: 50.6 us
  waiting for transfers between devices  24.7 us (49%)
  starting transfers between devices  16.6 us (33%)
  Pallas kernels  8.38 us (16%)
  between operations  0.82 us (2%)
    ppermute x1, waiting for transfers between devices, shards(): ahead = lax.ppermute(line, 'state', along(False, 1))  8.13 us
    ppermute x1, waiting for transfers between devices, shards(): x = lax.ppermute(end, 'tm', [(BLOCKS - 2, BLOCKS - 1)])  6.81 us
    ppermute x3, starting transfers between devices, shards(): lax.ppermute(mine, 'state', along(True, d))  5.89 us
    ppermute x1, waiting for transfers between devices, shards(): lax.ppermute(ahead[:half], 'state', along(False, 1))  4.26 us
    ppermute x3, waiting for transfers between devices, shards(): lax.ppermute(mine, 'state', along(True, d))  3.88 us
    ppermute x1, starting transfers between devices, shards(): lax.ppermute(behind[half:], 'state', along(False, RING - 1))  3.19 us
    pallas_call x1, Pallas kernels, product(): pl.pallas_call(product_kernel, in_specs=[pl.BlockSpec(memory_space=pltpu....  2.89 us
    ppermute x1, starting transfers between devices, shards(): behind = lax.ppermute(line, 'state', along(False, RING - 1))  2.2 us
  transfers between devices with their start and end apart: 14, of which 7 were waited for; matrix products, arithmetic and copies ran while one was open for 0% of the time, Pallas kernels for 11%

profile of v6, /device:TPU:6, one launch (start us, length us, event | category | flops | bytes accessed | tf_op | source)
XLA Modules:
  0.0 50.6 jit_solution(15422540463374000340)
XLA Ops:
  0.6 0.9 %pack.1 = bf16[32,2432]{1,0:T(8,128)(2,1)S(1)} custom-call(bf16[2,32,1024]{2,1,0:T(8,128)(2,1)} %trans_ref.1, bf16[32,128]{1,0:T(8,128)(2,1)} %gain_ref.1, bf16[32,128]{1,0:T(8,128)(2,1)} %bitcast.2, f32[1,32]{1,0:T(1,128)} %bitcast.3), custom_call_target="tpu_custom_call" | custom-call | tf_op jit(solution)/shard_map/pack/pallas_call | solution.py:66
  1.6 1.6 %collective-permute-start.2 = (bf16[32,2432]{1,0:T(8,128)(2,1)S(1)}, bf16[32,2432]{1,0:T(8,128)(2,1)S(1)}, u32[]{:S(2)}, u32[]{:S(2)}) collective-permute-start(bf16[32,2432]{1,0:T(8,128)(2,1)S(1)} %pack.1), channel_id=1, source_target_pairs={{0,2},{1,9},{2,4},{3,11},{4,6},{5,13},{6,0},{7,15},{8,10},{9,17},{... | collective-permute-start | bytes 466952 | tf_op jit(solution)/shard_map/ppermute | solution.py:353
  3.2 2.9 %collective-permute-start.1 = (bf16[32,2432]{1,0:T(8,128)(2,1)S(1)}, bf16[32,2432]{1,0:T(8,128)(2,1)S(1)}, u32[]{:S(2)}, u32[]{:S(2)}) collective-permute-start(bf16[32,2432]{1,0:T(8,128)(2,1)S(1)} %pack.1), channel_id=1, source_target_pairs={{0,4},{1,17},{2,6},{3,19},{4,0},{5,21},{6,2},{7,23},{8,12},{9,25},... | collective-permute-start | bytes 466952 | tf_op jit(solution)/shard_map/ppermute | solution.py:353
  6.1 1.3 %collective-permute-start = (bf16[32,2432]{1,0:T(8,128)(2,1)S(1)}, bf16[32,2432]{1,0:T(8,128)(2,1)S(1)}, u32[]{:S(2)}, u32[]{:S(2)}) collective-permute-start(bf16[32,2432]{1,0:T(8,128)(2,1)S(1)} %pack.1), channel_id=1, source_target_pairs={{0,6},{1,25},{2,0},{3,27},{4,2},{5,29},{6,4},{7,31},{8,14},{9,1},{... | collective-permute-start | bytes 466952 | tf_op jit(solution)/shard_map/ppermute | solution.py:353
  7.5 0.6 %collective-permute-done.2 = bf16[32,2432]{1,0:T(8,128)(2,1)S(1)} collective-permute-done((bf16[32,2432]{1,0:T(8,128)(2,1)S(1)}, bf16[32,2432]{1,0:T(8,128)(2,1)S(1)}, u32[]{:S(2)}, u32[]{:S(2)}) %collective-permute-start.2) | collective-permute-done | bytes 155680 | tf_op jit(solution)/shard_map/ppermute | solution.py:353
  8.1 2.9 %collective-permute-done.1 = bf16[32,2432]{1,0:T(8,128)(2,1)S(1)} collective-permute-done((bf16[32,2432]{1,0:T(8,128)(2,1)S(1)}, bf16[32,2432]{1,0:T(8,128)(2,1)S(1)}, u32[]{:S(2)}, u32[]{:S(2)}) %collective-permute-start.1) | collective-permute-done | bytes 155680 | tf_op jit(solution)/shard_map/ppermute | solution.py:353
  11.0 0.4 collective-permute-done
  11.4 2.0 %collective-permute-start.3 = (bf16[128,2432]{1,0:T(8,128)(2,1)S(1)}, bf16[128,2432]{1,0:T(8,128)(2,1)S(1)}, u32[]{:S(2)}, u32[]{:S(2)}) collective-permute-start(bf16[128,2432]{1,0:T(8,128)(2,1)S(1)} %pad_maximum_fusion.refs_0_), channel_id=1, source_target_pairs={{0,8},{1,3},{2,10},{3,5},{4,12},{5,7},{6,14},{7,1},{8,16},{9,11},{... | collective-permute-start | bytes 1867784 | tf_op jit(solution)/shard_map/ppermute | solution.py:355
  13.4 2.2 %collective-permute-start.5 = (bf16[128,2432]{1,0:T(8,128)(2,1)S(1)}, bf16[128,2432]{1,0:T(8,128)(2,1)S(1)}, u32[]{:S(2)}, u32[]{:S(2)}) collective-permute-start(bf16[128,2432]{1,0:T(8,128)(2,1)S(1)} %pad_maximum_fusion.refs_0_), channel_id=1, source_target_pairs={{0,24},{1,7},{2,26},{3,1},{4,28},{5,3},{6,30},{7,5},{8,0},{9,15},{... | collective-permute-start | bytes 1867784 | tf_op jit(solution)/shard_map/ppermute | solution.py:356
  15.6 8.1 %collective-permute-done.3.refs_1_ = bf16[128,2432]{1,0:T(8,128)(2,1)S(1)} collective-permute-done((bf16[128,2432]{1,0:T(8,128)(2,1)S(1)}, bf16[128,2432]{1,0:T(8,128)(2,1)S(1)}, u32[]{:S(2)}, u32[]{:S(2)}) %collective-permute-start.3) | collective-permute-done | bytes 622624 | tf_op jit(solution)/shard_map/ppermute | solution.py:355
  23.7 0.1 collective-permute-start.4
  23.8 0.1 collective-permute-start.8
  23.9 0.0 collective-permute-done.5.refs_2_
  24.0 3.2 %collective-permute-start.6 = (bf16[64,2432]{1,0:T(8,128)(2,1)S(1)}, bf16[64,2432]{1,0:T(8,128)(2,1)S(1)}, u32[]{:S(2)}, u32[]{:S(2)}) collective-permute-start(bf16[64,2432]{1,0:T(8,128)(2,1)S(1)} %slice.9), channel_id=1, source_target_pairs={{0,24},{1,7},{2,26},{3,1},{4,28},{5,3},{6,30},{7,5},{8,0},{9,15},{... | collective-permute-start | bytes 933896 | tf_op jit(solution)/shard_map/ppermute | solution.py:360
  27.2 0.0 collective-permute-start.10
  27.2 0.5 %collective-permute-start.9 = (bf16[128,2432]{1,0:T(8,128)(2,1)S(1)}, bf16[128,2432]{1,0:T(8,128)(2,1)S(1)}, u32[]{:S(2)}, u32[]{:S(2)}) collective-permute-start(bf16[128,2432]{1,0:T(8,128)(2,1)S(1)} %collective-permute-done.3.refs_1_), channel_id=1, source_target_pairs={{0,1},{1,0},{2,3},{3,2},{4,5},{5,4},{6,7},{7,6},{8,9},{9,8},{10,11... | collective-permute-start | bytes 1867784 | tf_op jit(solution)/shard_map/ppermute | solution.py:364
  27.7 4.3 %collective-permute-done.4 = bf16[64,2432]{1,0:T(8,128)(2,1)S(1)} collective-permute-done((bf16[64,2432]{1,0:T(8,128)(2,1)S(1)}, bf16[64,2432]{1,0:T(8,128)(2,1)S(1)}, u32[]{:S(2)}, u32[]{:S(2)}) %collective-permute-start.4) | collective-permute-done | bytes 311328 | tf_op jit(solution)/shard_map/ppermute | solution.py:359
  32.0 0.0 collective-permute-done.6
  32.0 0.0 copy-start
  32.0 0.1 collective-permute-start.7
  32.1 0.0 collective-permute-done.8.refs_3_
  32.1 0.0 collective-permute-done.10.refs_5_
  32.1 0.0 collective-permute-done.9.refs_4_
  32.1 0.4 early.1.held_ref
  32.6 1.6 %collective-permute-done.7.part1 = bf16[128,2432]{1,0:T(8,128)(2,1)S(1)} collective-permute-done((bf16[128,2432]{1,0:T(8,128)(2,1)S(1)}, bf16[128,2432]{1,0:T(8,128)(2,1)S(1)}, u32[]{:S(2)}, u32[]{:S(2)}) %collective-permute-start.7) | collective-permute-done | bytes 622624 | tf_op jit(solution)/shard_map/ppermute | solution.py:366
  34.1 0.0 copy-done
  34.1 0.2 late.1
  34.3 0.7 %collective-permute-start.11 = (f32[1,1024]{1,0:T(1,128)S(1)}, f32[1,1024]{1,0:T(1,128)S(1)}, u32[]{:S(2)}, u32[]{:S(2)}) collective-permute-start(f32[1,1024]{1,0:T(1,128)S(1)} %get-tuple-element.16.end0), channel_id=1, source_target_pairs={{0,32},{1,33},{2,34},{3,35},{4,36},{5,37},{6,38},{7,39},{8,40},{9,... | collective-permute-start | bytes 12296 | tf_op jit(solution)/shard_map/ppermute | solution.py:368
  35.0 2.0 %models.1 = (bf16[1024,2432]{1,0:T(8,128)(2,1)S(1)}, f32[2,1024]{1,0:T(2,128)S(1)}) custom-call(f32[2,128]{1,0:T(2,128)S(1)} %copy-done, bf16[1024,2432]{1,0:T(8,128)(2,1)S(1)} %get-tuple-element.13.held_ref), custom_call_target="tpu_custom_call", output_to_operand_aliasing={{0}: (1, {})} | custom-call | flops 536870912 | bytes 8388608 | tf_op jit(solution)/shard_map/models/pallas_call | solution.py:202
  37.0 0.0 collective-permute-done.11.x_ref
  37.1 0.7 %collective-permute-start.12 = (f32[1,1024]{1,0:T(1,128)S(1)}, f32[1,1024]{1,0:T(1,128)S(1)}, u32[]{:S(2)}, u32[]{:S(2)}) collective-permute-start(f32[1,1024]{1,0:T(1,128)S(1)} %get-tuple-element.18.after_ref.end0), channel_id=1, source_target_pairs={{32,64},{33,65},{34,66},{35,67},{36,68},{37,69},{38,70},{39,71},{4... | collective-permute-start | bytes 12296 | tf_op jit(solution)/shard_map/ppermute | solution.py:373
  37.7 2.9 %product.1 = (bf16[1024,1024]{1,0:T(8,128)(2,1)S(1)}, f32[1,1024]{1,0:T(1,128)S(1)}) custom-call(bf16[1024,2432]{1,0:T(8,128)(2,1)S(1)} %get-tuple-element.14.all_ref, f32[2,1024]{1,0:T(2,128)S(1)} %get-tuple-element.15.src_ref, f32[1,1024]{1,0:T(1,128)S(1)} %get-tuple-element.18.after_ref.end0), custom_call_target="tpu_custom_call" | custom-call | flops 2147483648 | bytes 6291456 | tf_op jit(solution)/shard_map/product/pallas_call | solution.py:234
  40.6 0.0 collective-permute-done.12.x_ref
  40.7 1.3 %collective-permute-start.13 = (f32[1,1024]{1,0:T(1,128)S(1)}, f32[1,1024]{1,0:T(1,128)S(1)}, u32[]{:S(2)}, u32[]{:S(2)}) collective-permute-start(f32[1,1024]{1,0:T(1,128)S(1)} %get-tuple-element.22.end_ref), channel_id=1, source_target_pairs={{64,96},{65,97},{66,98},{67,99},{68,100},{69,101},{70,102},{71,103... | collective-permute-start | bytes 12296 | tf_op jit(solution)/shard_map/ppermute | solution.py:375
  42.0 6.8 %collective-permute-done.13.x_ref = f32[1,1024]{1,0:T(1,128)S(1)} collective-permute-done((f32[1,1024]{1,0:T(1,128)S(1)}, f32[1,1024]{1,0:T(1,128)S(1)}, u32[]{:S(2)}, u32[]{:S(2)}) %collective-permute-start.13) | collective-permute-done | bytes 4128 | tf_op jit(solution)/shard_map/ppermute | solution.py:375
  48.8 1.9 %finish.1 = (f32[2,32]{1,0:T(2,128)}, f32[1,32]{1,0:T(1,128)}) custom-call(bf16[1024,2432]{1,0:T(8,128)(2,1)S(1)} %get-tuple-element.14.all_ref, bf16[1024,1024]{1,0:T(8,128)(2,1)S(1)} %get-tuple-element.19.both_ref, f32[2,1024]{1,0:T(2,128)S(1)} %get-tuple-element.15.src_ref, f32[1,1024]{1,0:T(1,128)S(1)} %get-tuple-element.20.sum_ref, ...), custom_call_target="tpu_custom_call" | custom-call | tf_op jit(solution)/shard_map/finish/pallas_call | solution.py:323
  (7 shorter events, 0.2 us)
Async XLA Ops:
  1.6 6.5 %collective-permute-start.2 = (bf16[32,2432]{1,0:T(8,128)(2,1)S(1)}, bf16[32,2432]{1,0:T(8,128)(2,1)S(1)}, u32[]{:S(2)}, u32[]{:S(2)}) collective-permute-start(bf16[32,2432]{1,0:T(8,128)(2,1)S(1)} %pack.1), channel_id=1, source_target_pairs={{0,2},{1,9},{2,4},{3,11},{4,6},{5,13},{6,0},{7,15},{8,10},{9,17},{... | collective-permute-start | bytes 466952 | tf_op jit(solution)/shard_map/ppermute | solution.py:353
  3.2 7.8 %collective-permute-start.1 = (bf16[32,2432]{1,0:T(8,128)(2,1)S(1)}, bf16[32,2432]{1,0:T(8,128)(2,1)S(1)}, u32[]{:S(2)}, u32[]{:S(2)}) collective-permute-start(bf16[32,2432]{1,0:T(8,128)(2,1)S(1)} %pack.1), channel_id=1, source_target_pairs={{0,4},{1,17},{2,6},{3,19},{4,0},{5,21},{6,2},{7,23},{8,12},{9,25},... | collective-permute-start | bytes 466952 | tf_op jit(solution)/shard_map/ppermute | solution.py:353
  6.1 5.2 %collective-permute-start = (bf16[32,2432]{1,0:T(8,128)(2,1)S(1)}, bf16[32,2432]{1,0:T(8,128)(2,1)S(1)}, u32[]{:S(2)}, u32[]{:S(2)}) collective-permute-start(bf16[32,2432]{1,0:T(8,128)(2,1)S(1)} %pack.1), channel_id=1, source_target_pairs={{0,6},{1,25},{2,0},{3,27},{4,2},{5,29},{6,4},{7,31},{8,14},{9,1},{... | collective-permute-start | bytes 466952 | tf_op jit(solution)/shard_map/ppermute | solution.py:353
  11.4 12.3 %collective-permute-start.3 = (bf16[128,2432]{1,0:T(8,128)(2,1)S(1)}, bf16[128,2432]{1,0:T(8,128)(2,1)S(1)}, u32[]{:S(2)}, u32[]{:S(2)}) collective-permute-start(bf16[128,2432]{1,0:T(8,128)(2,1)S(1)} %pad_maximum_fusion.refs_0_), channel_id=1, source_target_pairs={{0,8},{1,3},{2,10},{3,5},{4,12},{5,7},{6,14},{7,1},{8,16},{9,11},{... | collective-permute-start | bytes 1867784 | tf_op jit(solution)/shard_map/ppermute | solution.py:355
  13.4 10.5 %collective-permute-start.5 = (bf16[128,2432]{1,0:T(8,128)(2,1)S(1)}, bf16[128,2432]{1,0:T(8,128)(2,1)S(1)}, u32[]{:S(2)}, u32[]{:S(2)}) collective-permute-start(bf16[128,2432]{1,0:T(8,128)(2,1)S(1)} %pad_maximum_fusion.refs_0_), channel_id=1, source_target_pairs={{0,24},{1,7},{2,26},{3,1},{4,28},{5,3},{6,30},{7,5},{8,0},{9,15},{... | collective-permute-start | bytes 1867784 | tf_op jit(solution)/shard_map/ppermute | solution.py:356
  23.7 8.2 %collective-permute-start.4 = (bf16[64,2432]{1,0:T(8,128)(2,1)S(1)}, bf16[64,2432]{1,0:T(8,128)(2,1)S(1)}, u32[]{:S(2)}, u32[]{:S(2)}) collective-permute-start(bf16[64,2432]{1,0:T(8,128)(2,1)S(1)} %slice.8), channel_id=1, source_target_pairs={{0,8},{1,3},{2,10},{3,5},{4,12},{5,7},{6,14},{7,1},{8,16},{9,11},{... | collective-permute-start | bytes 933896 | tf_op jit(solution)/shard_map/ppermute | solution.py:359
  23.8 8.3 %collective-permute-start.8 = (bf16[128,2432]{1,0:T(8,128)(2,1)S(1)}, bf16[128,2432]{1,0:T(8,128)(2,1)S(1)}, u32[]{:S(2)}, u32[]{:S(2)}) collective-permute-start(bf16[128,2432]{1,0:T(8,128)(2,1)S(1)} %pad_maximum_fusion.refs_0_), channel_id=1, source_target_pairs={{0,1},{1,0},{2,3},{3,2},{4,5},{5,4},{6,7},{7,6},{8,9},{9,8},{10,11... | collective-permute-start | bytes 1867784 | tf_op jit(solution)/shard_map/ppermute | solution.py:364
  24.0 8.0 %collective-permute-start.6 = (bf16[64,2432]{1,0:T(8,128)(2,1)S(1)}, bf16[64,2432]{1,0:T(8,128)(2,1)S(1)}, u32[]{:S(2)}, u32[]{:S(2)}) collective-permute-start(bf16[64,2432]{1,0:T(8,128)(2,1)S(1)} %slice.9), channel_id=1, source_target_pairs={{0,24},{1,7},{2,26},{3,1},{4,28},{5,3},{6,30},{7,5},{8,0},{9,15},{... | collective-permute-start | bytes 933896 | tf_op jit(solution)/shard_map/ppermute | solution.py:360
  27.2 5.0 %collective-permute-start.10 = (bf16[128,2432]{1,0:T(8,128)(2,1)S(1)}, bf16[128,2432]{1,0:T(8,128)(2,1)S(1)}, u32[]{:S(2)}, u32[]{:S(2)}) collective-permute-start(bf16[128,2432]{1,0:T(8,128)(2,1)S(1)} %collective-permute-done.5.refs_2_), channel_id=1, source_target_pairs={{0,1},{1,0},{2,3},{3,2},{4,5},{5,4},{6,7},{7,6},{8,9},{9,8},{10,11... | collective-permute-start | bytes 1867784 | tf_op jit(solution)/shard_map/ppermute | solution.py:364
  27.2 5.0 %collective-permute-start.9 = (bf16[128,2432]{1,0:T(8,128)(2,1)S(1)}, bf16[128,2432]{1,0:T(8,128)(2,1)S(1)}, u32[]{:S(2)}, u32[]{:S(2)}) collective-permute-start(bf16[128,2432]{1,0:T(8,128)(2,1)S(1)} %collective-permute-done.3.refs_1_), channel_id=1, source_target_pairs={{0,1},{1,0},{2,3},{3,2},{4,5},{5,4},{6,7},{7,6},{8,9},{9,8},{10,11... | collective-permute-start | bytes 1867784 | tf_op jit(solution)/shard_map/ppermute | solution.py:364
  32.0 2.1 %copy-start = (f32[2,128]{1,0:T(2,128)S(1)}, f32[2,128]{1,0:T(2,128)}, u32[]{:S(2)}) copy-start(f32[2,128]{1,0:T(2,128)} %obs_ref.3) | copy-start | bytes 3076
  32.0 2.1 %collective-permute-start.7 = (bf16[128,2432]{1,0:T(8,128)(2,1)S(1)}, bf16[128,2432]{1,0:T(8,128)(2,1)S(1)}, u32[]{:S(2)}, u32[]{:S(2)}) collective-permute-start(bf16[128,2432]{1,0:T(8,128)(2,1)S(1)} %constant_dynamic-update-slice_fusion.part0), channel_id=1, source_target_pairs={{0,1},{1,0},{2,3},{3,2},{4,5},{5,4},{6,7},{7,6},{8,9},{9,8},{10,11... | collective-permute-start | bytes 1867784 | tf_op jit(solution)/shard_map/ppermute | solution.py:366
  34.3 2.7 %collective-permute-start.11 = (f32[1,1024]{1,0:T(1,128)S(1)}, f32[1,1024]{1,0:T(1,128)S(1)}, u32[]{:S(2)}, u32[]{:S(2)}) collective-permute-start(f32[1,1024]{1,0:T(1,128)S(1)} %get-tuple-element.16.end0), channel_id=1, source_target_pairs={{0,32},{1,33},{2,34},{3,35},{4,36},{5,37},{6,38},{7,39},{8,40},{9,... | collective-permute-start | bytes 12296 | tf_op jit(solution)/shard_map/ppermute | solution.py:368
  37.1 3.6 %collective-permute-start.12 = (f32[1,1024]{1,0:T(1,128)S(1)}, f32[1,1024]{1,0:T(1,128)S(1)}, u32[]{:S(2)}, u32[]{:S(2)}) collective-permute-start(f32[1,1024]{1,0:T(1,128)S(1)} %get-tuple-element.18.after_ref.end0), channel_id=1, source_target_pairs={{32,64},{33,65},{34,66},{35,67},{36,68},{37,69},{38,70},{39,71},{4... | collective-permute-start | bytes 12296 | tf_op jit(solution)/shard_map/ppermute | solution.py:373
  40.7 8.1 %collective-permute-start.13 = (f32[1,1024]{1,0:T(1,128)S(1)}, f32[1,1024]{1,0:T(1,128)S(1)}, u32[]{:S(2)}, u32[]{:S(2)}) collective-permute-start(f32[1,1024]{1,0:T(1,128)S(1)} %get-tuple-element.22.end_ref), channel_id=1, source_target_pairs={{64,96},{65,97},{66,98},{67,99},{68,100},{69,101},{70,102},{71,103... | collective-permute-start | bytes 12296 | tf_op jit(solution)/shard_map/ppermute | solution.py:375
